TPU v7x, 256 devices: a whole 4x4x8 slice. The times are simulated.
256 devices in a mesh: docs: 2 (over y_hi), ctx: 8 (over z), mp: 16 (over y_lo, x, core).
Axes of the slice: x: 4, y: 4 (y_hi: 2, y_lo: 2; y = y_hi * 2 + y_lo), z: 8, core: 2. Of those that a mesh axis runs over, the one named last changes fastest.
Arguments:
- residual_in: bfloat16 [8192, 5376], P(('docs', 'ctx', 'mp')), parts along dimension 0, may hold values from -15 to 15
- document_start: int32 [8192], P(('docs', 'ctx')), parts along dimension 0, may hold values from 0 to 3584, as said below
- input_gain: float32 [5376], replicated, may hold values from 0.25 to 1.75
- query_weight: bfloat16 [5376, 4096], P(None, 'mp'), may hold values from -0.078125 to 0.078125
- key_weight: bfloat16 [5376, 2048], P(None, 'mp'), may hold values from -0.078125 to 0.078125
- value_weight: bfloat16 [5376, 2048], P(None, 'mp'), may hold values from -0.078125 to 0.078125
- query_gain: float32 [128], replicated, may hold values from 0.6 to 20
- key_gain: float32 [128], replicated, may hold values from 0.6 to 20
- output_weight: bfloat16 [4096, 5376], P('mp'), may hold values from -0.09375 to 0.09375
- post_gain: float32 [5376], replicated, may hold values from 0.25 to 1.75
Outputs:
- residual_out: bfloat16 [8192, 5376], P(('docs', 'ctx', 'mp')), parts along dimension 0
There are 2 independent parts, one for each index of `docs`. A program takes and returns all parts, laid end to end along the dimension named above; an argument that names none is the same for every part. Nothing has to cross between parts.
Inputs may be any that keep to these rules, and one draw needn't show every extreme that they name: `document_start`: each entry is the index of the first token of that token's document; the documents lie end to end, there are 4 of them, one has exactly 3072 tokens, and the last has exactly 512 tokens.
All inputs are finite; a program needn't handle non-finite values.
Results may differ from a plain program's by a relative error of at most 0.014.
The roundings to bfloat16 on the way count: a program that leaves them out, or rounds other values in their place, can miss the bound.
Values may be sent and summed in bfloat16 or wider, within the bound.
No kernel may reach another device: no remote copies, remote signals or barrier semaphores. Data moves between devices by JAX's collectives and lax.ppermute only.
A program may use at most 64 MiB of HBM per device.

v0:
```python
import math

import jax
import jax.numpy as jnp
from jax import lax
from jax.sharding import PartitionSpec as P

query_scalar = 168.0
rope_base = 1000000.0
rope_factor = 8.0
epsilon = 1e-06


def make_angles(positions, head_size):
    frequency = rope_base ** (-(jnp.arange(head_size // 2, dtype=jnp.float32) * 2.0 / head_size))
    return (positions.astype(jnp.float32) / rope_factor)[:, None] * frequency[None, :]


def norm_rotate(values, head_gain, angles, head_count):
    tokens_here = values.shape[0]
    head_size = head_gain.shape[0]
    shaped = values.reshape(tokens_here, head_count, head_size)
    scaled = (
        shaped * lax.rsqrt(jnp.mean(shaped * shaped, axis=-1, keepdims=True) + epsilon) * head_gain
    )
    half_size = head_size // 2
    first_half = scaled[..., :half_size]
    second_half = scaled[..., half_size:]
    cosine = jnp.cos(angles)[:, None, :]
    sine_values = jnp.sin(angles)[:, None, :]
    rotated = jnp.concatenate(
        [
            first_half * cosine - second_half * sine_values,
            second_half * cosine + first_half * sine_values,
        ],
        axis=-1,
    )
    return rotated.astype(jnp.bfloat16)


def block_step(query_block, carried, key_piece, value_piece, key_index, first_row, piece_rows):
    queries, query_index, query_start = query_block

    def compute(running):
        running_max, running_total, accumulated = running
        scores = jnp.einsum(
            "tkgd,nkd->tkgn", queries, key_piece, preferred_element_type=jnp.float32
        ) / math.sqrt(query_scalar)
        allowed = (key_index[None, :] >= query_start[:, None]) & (
            key_index[None, :] <= query_index[:, None]
        )
        allowed = allowed[:, None, None, :]
        masked = jnp.where(allowed, scores, -1e30)
        new_max = jnp.maximum(running_max, jnp.max(masked, axis=-1))
        weights = jnp.where(allowed, jnp.exp(masked - new_max[..., None]), 0.0)
        new_total = jnp.sum(weights, axis=-1)
        product = jnp.einsum(
            "tkgn,nkd->tkgd",
            weights.astype(jnp.bfloat16),
            value_piece,
            preferred_element_type=jnp.float32,
        )
        return (new_max, new_total, product)

    def keep(running):
        return running

    is_live = (first_row <= jnp.max(query_index)) & (
        first_row + piece_rows - 1 >= jnp.min(query_start)
    )
    return lax.cond(is_live, compute, keep, carried)


def attend(query_blocks, key_rows, value_rows):
    initial = []
    for query_block in query_blocks:
        query_rows, kv_count, group_size, head_size = query_block[0].shape
        initial.append(
            (
                jnp.full((query_rows, kv_count, group_size), -1e30, jnp.float32),
                jnp.zeros((query_rows, kv_count, group_size), jnp.float32),
                jnp.zeros((query_rows, kv_count, group_size, head_size), jnp.float32),
            )
        )
    carried = tuple(initial)
    first_row = jnp.int32(0)
    key_piece = lax.all_gather(key_rows, "ctx", axis=0, tiled=True)
    value_piece = lax.all_gather(value_rows, "ctx", axis=0, tiled=True)
    piece_rows = key_piece.shape[0]
    key_index = jnp.arange(piece_rows, dtype=jnp.int32)
    outcome = []
    for query_block, carry_block in zip(query_blocks, carried):
        outcome.append(
            block_step(
                query_block, carry_block, key_piece, value_piece, key_index, first_row, piece_rows
            )
        )
    finals = tuple(outcome)
    results = []
    for final_block in finals:
        running_max, running_total, accumulated = final_block
        query_rows = accumulated.shape[0]
        results.append(
            (accumulated / running_total[..., None]).reshape(query_rows, -1).astype(jnp.bfloat16)
        )
    return results[0]


def body(
    residual_in,
    document_start,
    input_gain,
    query_weight,
    key_weight,
    value_weight,
    query_gain,
    key_gain,
    output_weight,
    post_gain,
):
    head_size = query_gain.shape[0]
    gathered = lax.all_gather(residual_in, "mp", axis=0, tiled=True)
    local_tokens = gathered.shape[0]
    widened = gathered.astype(jnp.float32)
    normed = (
        widened
        * lax.rsqrt(jnp.mean(widened * widened, axis=-1, keepdims=True) + epsilon)
        * input_gain
    ).astype(jnp.bfloat16)
    query_raw = jnp.dot(normed, query_weight, preferred_element_type=jnp.float32)
    key_raw = jnp.dot(normed, key_weight, preferred_element_type=jnp.float32)
    value_rows = jnp.dot(normed, value_weight, preferred_element_type=jnp.float32).astype(
        jnp.bfloat16
    )
    query_count = query_weight.shape[1] // head_size
    kv_count = key_weight.shape[1] // head_size
    group_size = query_count // kv_count
    block_index = lax.axis_index("ctx")
    positions = block_index * local_tokens + jnp.arange(local_tokens, dtype=jnp.int32)
    angles = make_angles(positions - document_start, head_size)
    query_rot = norm_rotate(query_raw, query_gain, angles, query_count).reshape(
        local_tokens, kv_count, group_size, head_size
    )
    key_rot = norm_rotate(key_raw, key_gain, angles, kv_count)
    value_heads = value_rows.reshape(local_tokens, kv_count, head_size)
    attended = attend([(query_rot, positions, document_start)], key_rot, value_heads)
    summed = lax.psum_scatter(
        jnp.dot(attended, output_weight, preferred_element_type=jnp.float32).astype(jnp.bfloat16),
        "mp",
        scatter_dimension=0,
        tiled=True,
    ).astype(jnp.float32)
    branch = (
        summed * lax.rsqrt(jnp.mean(summed * summed, axis=-1, keepdims=True) + epsilon) * post_gain
    )
    return (residual_in.astype(jnp.float32) + branch).astype(jnp.bfloat16)


def solution(mesh):
    return jax.shard_map(
        body,
        mesh=mesh,
        in_specs=(
            P(("docs", "ctx", "mp"), None),
            P(("docs", "ctx")),
            P(),
            P(None, "mp"),
            P(None, "mp"),
            P(None, "mp"),
            P(),
            P(),
            P("mp", None),
            P(),
        ),
        out_specs=P(("docs", "ctx", "mp"), None),
        check_vma=False,
    )
```

profile of v0, /device:TPU:160, one launch (start us, length us, event | category | flops | bytes accessed | tf_op | source)
XLA Modules:
  0.0 243.9 jit_solution(6276417553406046301)
XLA Ops:
  6.5 0.7 all-gather.5.cloned.1.call-update
  7.3 45.7 %all-gather.5.cloned.1.call-done = bf16[512,5376]{1,0:T(8,128)(2,1)} async-done(((bf16[32,5376]{1,0:T(8,128)(2,1)}), bf16[512,5376]{1,0:T(8,128)(2,1)}) %all-gather.5.cloned.1.call-update) | async-done | bytes 5505040 | tf_op jit(solution)/shard_map/all_gather | solution.py:122
  53.0 3.9 %fusion.17 = f32[512]{0:T(512)S(1)} fusion(bf16[512,5376]{1,0:T(8,128)(2,1)} %all-gather.5.cloned.1.call-done), kind=kLoop, calls=%fused_computation.20 | loop fusion | flops 8257024 | bytes 5507072 | tf_op jit(solution)/shard_map/reduce_sum | solution.py:127
  57.2 1.9 fusion.19
  59.1 2.4 copy-done.1
  61.5 2.3 convolution_convert_fusion.1
  63.9 4.9 %multiply_reduce_fusion.1 = (f32[512]{0:T(512)S(1)}, f32[512,128]{0,1:T(8,128)S(1)}) fusion(bf16[512,5376]{1,0:T(8,128)(2,1)} %copy-done.1, bf16[5376,128]{1,0:T(8,128)(2,1)} %param.16), kind=kOutput, calls=%fused_computation.42 | convolution fusion | flops 704773632 | bytes 7145472 | tf_op jit(solution)/shard_map/dot_general | solution.py:131
  69.5 0.7 pad_maximum_fusion.1
  70.9 0.7 reduce_min.9
  73.4 1.7 multiply_cosine_fusion
  75.1 5.9 %multiply_reduce_fusion = (f32[512,2]{0,1:T(2,128)S(1)}, f32[512,256]{0,1:T(8,128)}) fusion(bf16[512,5376]{1,0:T(8,128)(2,1)} %copy-done.1, bf16[5376,256]{1,0:T(8,128)(2,1)} %param.15), kind=kOutput, calls=%fused_computation.35 | convolution fusion | flops 1409547264 | bytes 8785920 | tf_op jit(solution)/shard_map/dot_general | solution.py:130
  81.0 1.2 copy.21
  82.5 1.2 fusion.24
  83.8 16.4 %all-gather.9.cloned.1.call-done = bf16[4096,128]{1,0:T(8,128)(2,1)} async-done(((bf16[512,128]{1,0:T(8,128)(2,1)}), bf16[4096,128]{1,0:T(8,128)(2,1)}) %all-gather.9.cloned.1.call-update) | async-done | bytes 1048592 | tf_op jit(solution)/shard_map/all_gather | solution.py:88
  100.2 39.0 %all-gather.7.cloned.1.call-done = bf16[4096,1,128]{0,2,1:T(8,128)(2,1)} async-done(((bf16[512,1,128]{0,2,1:T(8,128)(2,1)}), bf16[4096,1,128]{0,2,1:T(8,128)(2,1)}) %all-gather.7.cloned.1.call-update) | async-done | bytes 1048592 | tf_op jit(solution)/shard_map/all_gather | solution.py:87
  139.2 18.4 %conditional.1 = (f32[512,1,2]{0,2,1:T(2,128)S(1)}, f32[512,1,2,128]{0,3,2,1:T(8,128)S(1)}) conditional(s32[]{:T(128)} %convert_element_type.54, () %tuple.13, (s32[4096]{0:T(1024)S(1)}, s32[4096]{0:T(1024)S(1)}, s32[512]{0:T(512)}, s32[512]{0:T(512)}, bf16[4096,1,128]{0,2,1:T(8,128)(2,1)}, /*index=5*/bf16[512,1,2,128]{3,0,2,1:T(8,128)(2,1)S(1)}, ...), branch_computations={%region_5.0_spmd, %region_6.9_spmd} | conditional | flops 2208300032 | bytes 65859628 | solution.py:71
  139.2 3.8 %compare_and_fusion = pred[512,4096]{0,1:T(8,128)(4,1)S(1)} fusion(s32[512]{0:T(512)} %get-tuple-element.21, s32[512]{0:T(512)} %get-tuple-element.19, s32[4096]{0:T(1024)S(1)} %get-tuple-element.20, s32[4096]{0:T(1024)S(1)} %get-tuple-element.20), kind=kLoop, calls=%fused_computation.8 | loop fusion | flops 6291456 | bytes 2134016 | tf_op jit(solution)/shard_map/cond/branch_1_fun/and | solution.py:49
  143.0 5.1 %fusion = (f32[512,2]{0,1:T(2,128)S(1)}, f32[4096,512,2]{1,0,2:T(8,128)S(1)}) fusion(pred[512,4096]{0,1:T(8,128)(4,1)S(1)} %compare_and_fusion, bf16[512,1,2,128]{3,0,2,1:T(8,128)(2,1)S(1)} %get-tuple-element.23, bf16[4096,1,128]{0,2,1:T(8,128)(2,1)} %get-tuple-element.47), kind=kOutput, calls=%fused_computation.2 | convolution fusion | flops 1086323712 | bytes 20189184 | tf_op jit(solution)/shard_map/cond/branch_1_fun/tkgd,nkd->tkgn/dot_general | solution.py:46
  148.2 5.0 %fusion.7 = f32[512,1,2,128]{0,3,2,1:T(8,128)S(1)} fusion(f32[4096,512,2]{1,0,2:T(8,128)S(1)} %get-tuple-element.52, f32[512,2]{0,1:T(2,128)S(1)} %broadcast_maximum_fusion, pred[512,4096]{0,1:T(8,128)(4,1)S(1)} %compare_and_fusion, bf16[4096,1,128]{2,0,1:T(8,128)(2,1)S(1)} %copy-done.10), kind=kOutput, calls=%fused_computation.9 | convolution fusion | flops 1094713344 | bytes 20451328 | tf_op jit(solution)/shard_map/cond/branch_1_fun/tkgn,nkd->tkgd/dot_general | solution.py:57
  153.2 4.4 %fusion.2 = f32[512,2]{0,1:T(2,128)S(1)} fusion(f32[4096,512,2]{1,0,2:T(8,128)S(1)} %get-tuple-element.52, f32[512,2]{0,1:T(2,128)S(1)} %broadcast_maximum_fusion, pred[512,4096]{0,1:T(8,128)(4,1)S(1)} %compare_and_fusion), kind=kLoop, calls=%fused_computation.4 | loop fusion | flops 20970496 | bytes 18882560 | tf_op jit(solution)/shard_map/cond/branch_1_fun/reduce_sum | solution.py:56
  157.7 4.0 %convolution_convert_fusion = bf16[512,5376]{1,0:T(8,128)(2,1)} fusion(bf16[512,256]{0,1:T(8,128)(2,1)S(1)} %bitcast.65, bf16[256,5376]{1,0:T(8,128)(2,1)S(1)} %copy-done), kind=kOutput, calls=%fused_computation.23 | convolution fusion | flops 1412038656 | bytes 8519680 | tf_op jit(solution)/shard_map/dot_general | solution.py:148
  161.8 72.5 %reduce-scatter.2.cloned.1.call-done = bf16[32,5376]{1,0:T(8,128)(2,1)} async-done(((bf16[512,5376]{1,0:T(8,128)(2,1)}), bf16[32,5376]{1,0:T(8,128)(2,1)}) %reduce-scatter.2.cloned.1.call-update) | async-done | bytes 344080 | tf_op jit(solution)/shard_map/reduce_scatter | solution.py:147
  234.2 1.2 fusion.20
  235.4 1.9 fusion.23
  (43 shorter events, 2.9 us)
Async XLA Ops:
  6.5 151.1 %copy-start = (bf16[256,5376]{1,0:T(8,128)(2,1)S(1)}, bf16[256,5376]{1,0:T(8,128)(2,1)}, u32[]{:S(2)}) copy-start(bf16[256,5376]{1,0:T(8,128)(2,1)} %param.20) | copy-start | bytes 8257540
  6.5 50.3 %copy-start.5 = (f32[5376]{0:T(1024)S(1)}, f32[5376]{0:T(1024)}, u32[]{:S(2)}) copy-start(f32[5376]{0:T(1024)} %param.14) | copy-start | bytes 64516
  6.5 46.5 %all-gather.5.cloned.1.call-start = ((), (), s32[]{:S(2)}) async-start(), calls=%async_computation.1 | async-start | bytes 5849088 | tf_op jit(solution)/shard_map/all_gather | solution.py:122
  7.3 92.9 %all-gather.9.cloned.1.call-start = ((), (), s32[]{:S(2)}) async-start(), calls=%async_computation.4 | async-start | bytes 1179648 | tf_op jit(solution)/shard_map/all_gather | solution.py:88
  53.0 4.2 %copy-start.2 = (bf16[512,5376]{1,0:T(8,128)(2,1)S(1)}, bf16[512,5376]{1,0:T(8,128)(2,1)}, u32[]{:S(2)}) copy-start(bf16[512,5376]{1,0:T(8,128)(2,1)} %all-gather.5.cloned.1.call-done) | copy-start | bytes 16515076
  57.2 4.3 %copy-start.9 = (bf16[5376,128]{1,0:T(8,128)(2,1)S(1)}, bf16[5376,128]{1,0:T(8,128)(2,1)}, u32[]{:S(2)}) copy-start(bf16[5376,128]{1,0:T(8,128)(2,1)} %param.17) | copy-start | bytes 4128772
  59.1 2.4 copy-start.1
  61.5 2.4 copy-start.6
  63.7 5.1 %copy-start.7 = (f32[128]{0:T(128)S(1)}, f32[128]{0:T(128)}, u32[]{:S(2)}) copy-start(f32[128]{0:T(128)} %param.19) | copy-start | bytes 1540
  63.8 75.5 %all-gather.7.cloned.1.call-start = ((), (), s32[]{:S(2)}) async-start(), calls=%async_computation.2 | async-start | bytes 1179648 | tf_op jit(solution)/shard_map/all_gather | solution.py:87
  70.2 164.1 %reduce-scatter.2.cloned.1.call-start = ((), (), s32[]{:S(2)}) async-start(), calls=%async_computation.3 | async-start | bytes 5849088 | tf_op jit(solution)/shard_map/reduce_scatter | solution.py:147
  75.1 7.1 %copy-start.8 = (f32[128]{0:T(128)S(1)}, f32[128]{0:T(128)}, u32[]{:S(2)}) copy-start(f32[128]{0:T(128)} %param.18) | copy-start | bytes 1540
  143.0 5.2 %copy-start.10 = (bf16[4096,1,128]{2,0,1:T(8,128)(2,1)S(1)}, bf16[4096,1,128]{2,0,1:T(8,128)(2,1)}, u32[]{:S(2)}) copy-start(bf16[4096,1,128]{2,0,1:T(8,128)(2,1)} %get-tuple-element.24) | copy-start | bytes 3145732 | tf_op jit(solution)/shard_map/cond
  157.7 77.7 %copy-start.3 = (bf16[32,5376]{1,0:T(8,128)(2,1)S(1)}, bf16[32,5376]{1,0:T(8,128)(2,1)}, u32[]{:S(2)}) copy-start(bf16[32,5376]{1,0:T(8,128)(2,1)} %param.12) | copy-start | bytes 1032196
  157.7 77.7 %copy-start.4 = (f32[5376]{0:T(1024)S(1)}, f32[5376]{0:T(1024)}, u32[]{:S(2)}) copy-start(f32[5376]{0:T(1024)} %param.21) | copy-start | bytes 64516
Sparse Core Ops, SparseCore 0:
  9.2 43.7 all-gather.4
  63.9 36.2 all-gather.8
  102.0 37.1 all-gather.6
  161.9 72.3 reduce-scatter.1
where the time goes:
time: 246 us; the launch traced here: 244 us
  waiting for transfers between devices  174 us (71%)
  matrix products  27.2 us (11%)
  other arithmetic  23.6 us (10%)
  between operations  14.6 us (6%)
  local copies, waits for them, and re-layouts  3.98 us (2%)
    reduce_scatter x1, waiting for transfers between devices, body(): lax.psum_scatter(jnp.dot(attended, output_weight, preferred_element_type=...  72.5 us
    all_gather x1, waiting for transfers between devices, body(): gathered = lax.all_gather(residual_in, 'mp', axis=0, tiled=True)  45.7 us
    all_gather x1, waiting for transfers between devices, attend(): key_piece = lax.all_gather(key_rows, 'ctx', axis=0, tiled=True)  39 us
    all_gather x1, waiting for transfers between devices, attend(): value_piece = lax.all_gather(value_rows, 'ctx', axis=0, tiled=True)  16.4 us
    dot_general x1, matrix products, body(): jnp.dot(normed, query_weight, preferred_element_type=jnp.float32)  5.87 us
    dot_general x1, matrix products, compute(): jnp.einsum('tkgd,nkd->tkgn', queries, key_piece, preferred_element_type=j...  5.13 us
    dot_general x1, matrix products, compute(): jnp.einsum('tkgn,nkd->tkgd', weights.astype(jnp.bfloat16), value_piece, p...  4.97 us
    dot_general x1, matrix products, body(): key_raw = jnp.dot(normed, key_weight, preferred_element_type=jnp.float32)  4.92 us
  transfers between devices with their start and end apart: 4, of which 4 were waited for; matrix products, arithmetic and copies ran while one was open for 8% of the time, Pallas kernels for 0%

commit v1 on v0

v1 whole, which is shorter than its diff:
```python
import functools
import math

import jax
import jax.numpy as jnp
from jax import lax
from jax.experimental import pallas as pl
from jax.experimental.pallas import tpu as pltpu
from jax.sharding import PartitionSpec as P

query_scalar = 168.0
rope_base = 1000000.0
rope_factor = 8.0
epsilon = 1e-06

D = 5376
THIRD = D // 3
HD = 128
ROWS = 32
BLOCK = 512
VMEM_LIMIT = 56 * 1024 * 1024

XA, XB, YY, CC = 2, 6, 8, 1
ORDERS = ((XA, XB, YY), (XB, YY, XA), (YY, XA, XB))
BITS = {XA: 1, XB: 2, YY: 4}


def mp_mask(index):
    return (XA if index & 1 else 0) ^ (XB if index & 2 else 0) ^ (YY if index & 4 else 0)


def gathered_order(part):
    first, second, third = (BITS[link] for link in ORDERS[part])
    return [
        (first if k & 1 else 0) | (second if k & 2 else 0) | (third if k & 4 else 0)
        for k in range(8)
    ]


def swap(value, link):
    return lax.ppermute(value, "mp", [(m, m ^ link) for m in range(16)])


def whole(count):
    return [pl.BlockSpec(memory_space=pltpu.VMEM)] * count


def params():
    return pltpu.CompilerParams(vmem_limit_bytes=VMEM_LIMIT)


def shape(rows, columns, dtype=jnp.bfloat16):
    return jax.ShapeDtypeStruct((rows, columns), dtype)


def norm_kernel(x_ref, gain_ref, *outs):
    x = x_ref[...].astype(jnp.float32)
    inverse = lax.rsqrt(jnp.mean(x * x, axis=-1, keepdims=True) + epsilon)
    normed = (x * inverse * gain_ref[...]).astype(jnp.bfloat16)
    for part, out in enumerate(outs):
        out[...] = normed[:, part * THIRD : (part + 1) * THIRD]


def norm_rows(residual, gain):
    return pl.pallas_call(
        norm_kernel,
        out_shape=[shape(ROWS, THIRD)] * 3,
        in_specs=whole(2),
        out_specs=whole(3),
        compiler_params=params(),
        name="norm_rows",
    )(residual, gain.reshape(1, D))


def join_kernel(extra, *refs):
    held, came, outs = refs[0:3], refs[3:6], refs[6:]
    for part in range(3):
        rows = held[part].shape[0]
        outs[part][0:rows] = held[part][...]
        outs[part][rows : 2 * rows] = came[part][...]
        if extra:
            outs[3][part, 0:rows] = held[part][...]
            outs[3][part, rows : 2 * rows] = came[part][...]


def join(held, came, extra):
    rows = held[0].shape[0]
    outs = [shape(2 * rows, THIRD)] * 3
    if extra:
        outs = outs + [jax.ShapeDtypeStruct((3, 2 * rows, THIRD), jnp.bfloat16)]
    return pl.pallas_call(
        functools.partial(join_kernel, extra),
        out_shape=outs,
        in_specs=whole(6),
        out_specs=whole(len(outs)),
        compiler_params=params(),
        name="join_rows",
    )(*held, *came)


def gather_tokens(thirds):
    came = [swap(thirds[p], ORDERS[p][0]) for p in range(3)]
    two = join(thirds, came, False)
    came = [swap(two[p], ORDERS[p][1]) for p in range(3)]
    *four, packed = join(two, came, True)
    late = [swap(four[p], ORDERS[p][2]) for p in range(3)]
    other = swap(packed, CC)
    other_late = [swap(late[p], CC) for p in range(3)]
    return four, late, other, other_late


def rotate(raw, gain, cosine, sine):
    inverse = lax.rsqrt(jnp.mean(raw * raw, axis=-1, keepdims=True) + epsilon)
    scaled = raw * inverse * gain
    turned = pltpu.roll(scaled, HD // 2, 1)
    return (scaled * cosine + turned * sine).astype(jnp.bfloat16)


def project_kernel(weight_count, *refs):
    x_refs = refs[0:10]
    w_refs = refs[10 : 10 + weight_count]
    gain_ref, cos_ref, sin_ref, out_ref, xs, ws, acc, x_sem, w_sem = refs[10 + weight_count :]
    four, late, other, other_late = x_refs[0:3], x_refs[3:6], x_refs[6], x_refs[7:10]
    width = 2 * HD // weight_count
    copies = []
    for part in range(3):
        rows = pl.ds(part * THIRD, THIRD)
        group = []
        for k, w in enumerate(w_refs):
            group.append(
                pltpu.make_async_copy(
                    w.at[rows], ws.at[rows, pl.ds(k * width, width)], w_sem.at[part, k]
                )
            )
        for k, source in enumerate((four[part], late[part], other.at[part], other_late[part])):
            group.append(
                pltpu.make_async_copy(
                    source, xs.at[part, pl.ds(128 * k, 128)], x_sem.at[part, k]
                )
            )
        copies.append(group)
    for group in copies:
        for copy in group:
            copy.start()
    for part in range(3):
        for copy in copies[part]:
            copy.wait()
        product = jnp.dot(
            xs[part],
            ws[part * THIRD : (part + 1) * THIRD],
            preferred_element_type=jnp.float32,
        )
        if part == 0:
            acc[...] = product
        else:
            for k, place in enumerate(gathered_order(part)):
                for core in range(2):
                    to = (core * 8 + place) * ROWS
                    at = (core * 8 + k) * ROWS
                    acc[to : to + ROWS] += product[at : at + ROWS]
    gain = gain_ref[...]
    out_ref[:, 0:HD] = rotate(acc[:, 0:HD], gain, cos_ref[...], sin_ref[...])
    if weight_count == 1:
        out_ref[:, HD : 2 * HD] = rotate(acc[:, HD : 2 * HD], gain, cos_ref[...], sin_ref[...])
    else:
        out_ref[:, HD : 2 * HD] = acc[:, HD : 2 * HD].astype(jnp.bfloat16)


def project(pieces, weights, gain, cosine, sine, name):
    four, late, other, other_late = pieces
    return pl.pallas_call(
        functools.partial(project_kernel, len(weights)),
        out_shape=shape(BLOCK, 2 * HD),
        in_specs=[pl.BlockSpec(memory_space=pl.ANY)] * (10 + len(weights)) + whole(3),
        out_specs=whole(1)[0],
        scratch_shapes=[
            pltpu.VMEM((3, BLOCK, THIRD), jnp.bfloat16),
            pltpu.VMEM((D, 2 * HD), jnp.bfloat16),
            pltpu.VMEM((BLOCK, 2 * HD), jnp.float32),
            pltpu.SemaphoreType.DMA((3, 4)),
            pltpu.SemaphoreType.DMA((3, 2)),
        ],
        compiler_params=params(),
        cost_estimate=pl.CostEstimate(
            flops=2 * BLOCK * D * 2 * HD, bytes_accessed=9000000, transcendentals=0
        ),
        name=name,
    )(*four, *late, other, *other_late, *weights, gain.reshape(1, HD), cosine, sine)


def share_keys(rows):
    def move(value, pairs):
        return lax.ppermute(value, "ctx", pairs)

    forward, backward = rows, rows
    ahead, behind = [], []
    for k in range(3):
        forward = move(forward, [(c, c + 1) for c in range(k, 6)])
        backward = move(backward, [((c - k) % 8, (c - k - 1) % 8) for c in range(3)])
        ahead.append(forward)
        behind.append(backward)
    key_far = move(forward[:, :HD], [(3, 4), (4, 5), (5, 6)])
    value_far = move(backward[:, HD:], [(5, 4), (6, 5), (7, 6)])
    return [rows, *ahead, behind[2], behind[1]], key_far, value_far


NEG = -1e30
TILE = 256


def attend_kernel(
    where_ref,
    q_ref,
    position_ref,
    start_ref,
    offset_ref,
    *refs,
):
    blocks, key_far, value_far = refs[0:6], refs[6], refs[7]
    out_ref, kv, top, total, acc, sem = refs[8:]
    block = where_ref[0]
    live = where_ref[1]
    slots = (0, 1, 2, 3, 5, 6)
    copies = []
    for k, slot in enumerate(slots):
        copies.append((slot, pltpu.make_async_copy(blocks[k], kv.at[slot], sem.at[k])))
    copies.append((4, pltpu.make_async_copy(key_far, kv.at[4, :, pl.ds(0, HD)], sem.at[6])))
    copies.append((4, pltpu.make_async_copy(value_far, kv.at[4, :, pl.ds(HD, HD)], sem.at[7])))
    for slot, copy in copies:
        pl.when(slot < live)(copy.start)
    top[...] = jnp.full(top.shape, NEG, jnp.float32)
    total[...] = jnp.zeros(total.shape, jnp.float32)
    acc[...] = jnp.zeros(acc.shape, jnp.float32)
    for slot, copy in copies:
        pl.when(slot < live)(copy.wait)
    factor = math.log2(math.e) / math.sqrt(query_scalar)

    def step(distance, unused):
        keys = kv[distance, :, 0:HD]
        values = kv[distance, :, HD : 2 * HD]
        first = (block - distance) * BLOCK
        key_index = offset_ref[...] + first
        for tile in range(BLOCK // TILE):
            rows = slice(tile * TILE, (tile + 1) * TILE)
            position = position_ref[rows]
            start = start_ref[rows]
            for head in range(2):
                scores = lax.dot_general(
                    q_ref[rows, head * HD : (head + 1) * HD],
                    keys,
                    (((1,), (1,)), ((), ())),
                    preferred_element_type=jnp.float32,
                )
                pieces = []
                for k in range(BLOCK // HD):
                    index = key_index[:, k * HD : (k + 1) * HD]
                    allowed = (index >= start) & (index <= position)
                    pieces.append(
                        jnp.where(allowed, scores[:, k * HD : (k + 1) * HD] * factor, NEG)
                    )
                best = jnp.maximum(
                    jnp.maximum(pieces[0], pieces[1]), jnp.maximum(pieces[2], pieces[3])
                )
                place = slice(head * BLOCK + tile * TILE, head * BLOCK + (tile + 1) * TILE)
                old = top[place]
                new = jnp.maximum(old, jnp.max(best, axis=-1, keepdims=True))
                fade = jnp.exp2(old - new)
                exps = [jnp.exp2(piece - new) for piece in pieces]
                total[place] = total[place] * fade + (
                    (exps[0] + exps[1]) + (exps[2] + exps[3])
                )
                weights = jnp.concatenate([e.astype(jnp.bfloat16) for e in exps], axis=1)
                acc[place] = acc[place] * fade + jnp.dot(
                    weights, values, preferred_element_type=jnp.float32
                )
                top[place] = new
        return unused

    lax.fori_loop(0, live, step, 0)
    for head in range(2):
        place = slice(head * BLOCK, (head + 1) * BLOCK)
        denominator = jnp.sum(total[place], axis=-1, keepdims=True)
        out_ref[:, head * HD : (head + 1) * HD] = (acc[place] / denominator).astype(jnp.bfloat16)


def attend(where, query, position, start, offset, blocks, key_far, value_far):
    return pl.pallas_call(
        attend_kernel,
        out_shape=shape(BLOCK, 2 * HD),
        in_specs=[pl.BlockSpec(memory_space=pltpu.SMEM)]
        + whole(4)
        + [pl.BlockSpec(memory_space=pl.ANY)] * 8,
        out_specs=whole(1)[0],
        scratch_shapes=[
            pltpu.VMEM((7, BLOCK, 2 * HD), jnp.bfloat16),
            pltpu.VMEM((2 * BLOCK, HD), jnp.float32),
            pltpu.VMEM((2 * BLOCK, HD), jnp.float32),
            pltpu.VMEM((2 * BLOCK, HD), jnp.float32),
            pltpu.SemaphoreType.DMA((8,)),
        ],
        compiler_params=params(),
        name="attend",
    )(where, query, position, start, offset, *blocks, key_far, value_far)


CHUNK = 256


def output_kernel(mine_ref, theirs_ref, w_mine, w_theirs, *outs):
    def groups(weight_columns):
        return jnp.dot(mine_ref[...], w_mine[:, weight_columns], preferred_element_type=jnp.float32).astype(
            jnp.bfloat16
        ).astype(jnp.float32) + jnp.dot(
            theirs_ref[...], w_theirs[:, weight_columns], preferred_element_type=jnp.float32
        ).astype(jnp.bfloat16).astype(jnp.float32)

    for part in range(3):
        bit = BITS[ORDERS[part][0]]
        for chunk in range(THIRD // CHUNK):
            summed = groups(
                slice(part * THIRD + chunk * CHUNK, part * THIRD + (chunk + 1) * CHUNK)
            ).astype(jnp.bfloat16)
            here = slice(chunk * CHUNK, (chunk + 1) * CHUNK)
            counts = [0, 0]
            for place in range(8):
                goes = 1 if place & bit else 0
                at = counts[goes] * ROWS
                counts[goes] += 1
                outs[2 * part + goes][at : at + ROWS, here] = summed[
                    place * ROWS : (place + 1) * ROWS
                ]


def project_out(mine, theirs, w_mine, w_theirs):
    return pl.pallas_call(
        output_kernel,
        out_shape=[shape(128, THIRD)] * 6,
        in_specs=whole(4),
        out_specs=whole(6),
        compiler_params=params(),
        cost_estimate=pl.CostEstimate(
            flops=4 * 256 * 256 * D, bytes_accessed=8500000, transcendentals=0
        ),
        name="project_out",
    )(mine, theirs, w_mine, w_theirs)


def remaining(part, level):
    return sorted(BITS[link] for link in ORDERS[part][level:])


def fold_kernel(level, *refs):
    kept, came, outs = refs[0:3], refs[3:6], refs[6:]
    for part in range(3):
        bits = remaining(part, level)
        goes_bit = bits.index(BITS[ORDERS[part][level]])
        summed = (
            kept[part][...].astype(jnp.float32) + came[part][...].astype(jnp.float32)
        ).astype(jnp.bfloat16)
        counts = [0, 0]
        for k in range(1 << len(bits)):
            goes = (k >> goes_bit) & 1
            at = counts[goes] * ROWS
            counts[goes] += 1
            outs[2 * part + goes][at : at + ROWS] = summed[k * ROWS : (k + 1) * ROWS]


def fold(kept, came, level):
    rows = kept[0].shape[0] // 2
    return pl.pallas_call(
        functools.partial(fold_kernel, level),
        out_shape=[shape(rows, THIRD)] * 6,
        in_specs=whole(6),
        out_specs=whole(6),
        compiler_params=params(),
        name="fold_rows",
    )(*kept, *came)


def finish_kernel(residual_ref, gain_ref, *refs):
    kept, came, out = refs[0:3], refs[3:6], refs[6]
    sums = []
    square = jnp.zeros((ROWS, 1), jnp.float32)
    for part in range(3):
        summed = kept[part][...].astype(jnp.float32) + came[part][...].astype(jnp.float32)
        sums.append(summed)
        square = square + jnp.sum(summed * summed, axis=-1, keepdims=True)
    inverse = lax.rsqrt(square / D + epsilon)
    for part in range(3):
        here = slice(part * THIRD, (part + 1) * THIRD)
        out[:, here] = (
            residual_ref[:, here].astype(jnp.float32) + sums[part] * inverse * gain_ref[:, here]
        ).astype(jnp.bfloat16)


def finish(residual, gain, kept, came):
    return pl.pallas_call(
        finish_kernel,
        out_shape=shape(ROWS, D),
        in_specs=whole(8),
        out_specs=whole(1)[0],
        compiler_params=params(),
        name="finish",
    )(residual, gain.reshape(1, D), *kept, *came)


def reduce_tokens(halves):
    kept, goes = halves[0::2], halves[1::2]
    for level in range(3):
        came = [swap(goes[p], ORDERS[p][level]) for p in range(3)]
        if level == 2:
            return kept, came
        halves = fold(kept, came, level + 1)
        kept, goes = halves[0::2], halves[1::2]


def body(
    residual_in,
    document_start,
    input_gain,
    query_weight,
    key_weight,
    value_weight,
    query_gain,
    key_gain,
    output_weight,
    post_gain,
):
    thirds = norm_rows(residual_in, input_gain)
    pieces = gather_tokens(thirds)

    block = lax.axis_index("ctx")
    mine = lax.axis_index("mp")
    masks = jnp.array([mp_mask(k & 7) ^ (k >> 3) for k in range(16)], jnp.int32)
    owners = mine ^ masks
    inside = (owners[:, None] * ROWS + jnp.arange(ROWS, dtype=jnp.int32)[None, :]).reshape(BLOCK)
    position = block * BLOCK + inside
    start = document_start.reshape(16, ROWS)[owners].reshape(BLOCK)
    frequency = rope_base ** (-(jnp.arange(HD // 2, dtype=jnp.float32) * 2.0 / HD))
    angles = ((position - start).astype(jnp.float32) / rope_factor)[:, None] * frequency[None, :]
    cosine = jnp.cos(angles)
    sine = jnp.sin(angles)
    cosine = jnp.concatenate([cosine, cosine], axis=1)
    sine = jnp.concatenate([-sine, sine], axis=1)
    live = block - jnp.min(document_start) // BLOCK + 1
    where = jnp.stack([block, live]).astype(jnp.int32)
    position_wide = jnp.broadcast_to(position[:, None], (BLOCK, HD))
    start_wide = jnp.broadcast_to(start[:, None], (BLOCK, HD))

    w_theirs = swap(output_weight, CC)
    rows = project(pieces, [key_weight, value_weight], key_gain, cosine, sine, "project_kv")
    query = project(pieces, [query_weight], query_gain, cosine, sine, "project_q")
    blocks, key_far, value_far = share_keys(rows)
    attended = attend(
        where, query, position_wide, start_wide, inside[None, :], blocks, key_far, value_far
    )
    theirs = swap(attended[256:], CC)
    halves = project_out(attended[:256], theirs, output_weight, w_theirs)
    kept, came = reduce_tokens(halves)
    return finish(residual_in, post_gain, kept, came)


def solution(mesh):
    return jax.shard_map(
        body,
        mesh=mesh,
        in_specs=(
            P(("docs", "ctx", "mp"), None),
            P(("docs", "ctx")),
            P(),
            P(None, "mp"),
            P(None, "mp"),
            P(None, "mp"),
            P(),
            P(),
            P("mp", None),
            P(),
        ),
        out_specs=P(("docs", "ctx", "mp"), None),
        check_vma=False,
    )
```

time: 246 us -> 164 us (0.67)
  waiting for transfers between devices: 174 us -> 59 us
  Pallas kernels: 0 us -> 46.9 us
  starting transfers between devices: 0.13 us -> 38 us
  matrix products: 27.2 us -> 0 us
  other arithmetic: 23.6 us -> 3.45 us
  between operations: 14.6 us -> 2.85 us
  local copies, waits for them, and re-layouts: 3.98 us -> 12.7 us
    all_gather x3 -> x0, waiting for transfers between devices: 101 us -> none  [the longest x1 45.7 us: body(): gathered = lax.all_gather(residual_in, 'mp', axis=0, tiled=True)]
    reduce_scatter x1 -> x0, waiting for transfers between devices: 72.5 us -> none  [body(): lax.psum_scatter(jnp.dot(attended, output_weight, preferred_element_type=...]
    ppermute x0 -> x32, waiting for transfers between devices: none -> 59 us  [the longest x24 43.2 us: swap(): return lax.ppermute(value, 'mp', [(m, m ^ link) for m in range(16)])]
    pallas_call x0 -> x10, Pallas kernels: none -> 46.9 us  [the longest x2 15 us: project(): pl.pallas_call(functools.partial(project_kernel, len(weights)), out_shape...]
    ppermute x0 -> x32, starting transfers between devices: none -> 38 us  [the longest x24 20.3 us: swap(): return lax.ppermute(value, 'mp', [(m, m ^ link) for m in range(16)])]
    dot_general x6 -> x0, matrix products: 27.2 us -> none  [the longest x1 5.87 us: body(): jnp.dot(normed, query_weight, preferred_element_type=jnp.float32)]
    reduce_sum x3 -> x0, other arithmetic: 9.46 us -> none  [the longest x1 4.45 us: compute(): new_total = jnp.sum(weights, axis=-1)]
    convert_element_type x3 -> x0, other arithmetic: 3.83 us -> none  [the longest x1 1.9 us: body(): return (residual_in.astype(jnp.float32) + branch).astype(jnp.bfloat16)]
  transfers between devices with their start and end apart: 4 -> 32, of which waited for: 4 -> 19; matrix products, arithmetic and copies ran while one was open for 8% -> 5% of each run, Pallas kernels for 0% -> 17%
where the time goes in v1:
time: 164 us; the launch traced here: 163 us
  waiting for transfers between devices  59 us (36%)
  Pallas kernels  46.9 us (29%)
  starting transfers between devices  38 us (23%)
  local copies, waits for them, and re-layouts  12.7 us (8%)
  other arithmetic  3.45 us (2%)
  between operations  2.85 us (2%)
    ppermute x24, waiting for transfers between devices, swap(): return lax.ppermute(value, 'mp', [(m, m ^ link) for m in range(16)])  43.2 us
    ppermute x24, starting transfers between devices, swap(): return lax.ppermute(value, 'mp', [(m, m ^ link) for m in range(16)])  20.3 us
    ppermute x8, starting transfers between devices, move(): return lax.ppermute(value, 'ctx', pairs)  17.7 us
    ppermute x8, waiting for transfers between devices, move(): return lax.ppermute(value, 'ctx', pairs)  15.8 us
    pallas_call x2, Pallas kernels, project(): pl.pallas_call(functools.partial(project_kernel, len(weights)), out_shape...  15 us
    pallas_call x1, Pallas kernels, attend(): pl.pallas_call(attend_kernel, out_shape=shape(BLOCK, 2 * HD), in_specs=[p...  12.2 us
    unnamed x66, local copies, waits for them, and re-layouts  5.91 us
    pallas_call x1, Pallas kernels, project_out(): pl.pallas_call(output_kernel, out_shape=[shape(128, THIRD)] * 6, in_specs...  5.32 us
  transfers between devices with their start and end apart: 32, of which 19 were waited for; matrix products, arithmetic and copies ran while one was open for 5% of the time, Pallas kernels for 17%

profile of v1, /device:TPU:160, one launch (start us, length us, event | category | flops | bytes accessed | tf_op | source)
XLA Modules:
  0.0 162.9 jit_solution(18005413815781143328)
XLA Ops:
  1.4 1.9 %norm_rows.1 = (bf16[32,1792]{1,0:T(8,128)(2,1)}, bf16[32,1792]{1,0:T(8,128)(2,1)}, bf16[32,1792]{1,0:T(8,128)(2,1)}) custom-call(bf16[32,5376]{1,0:T(8,128)(2,1)} %residual_ref.1, f32[1,5376]{1,0:T(1,128)} %reshape.79.gain_ref), custom_call_target="tpu_custom_call" | custom-call | tf_op jit(solution)/shard_map/norm_rows/pallas_call | solution.py:65
  4.8 2.1 %collective-permute-start.1 = (bf16[32,1792]{1,0:T(8,128)(2,1)}, bf16[32,1792]{1,0:T(8,128)(2,1)S(1)}, u32[]{:S(2)}, u32[]{:S(2)}) collective-permute-start(bf16[32,1792]{1,0:T(8,128)(2,1)} %get-tuple-element.34.refs_1_), channel_id=1, source_target_pairs={{0,6},{1,7},{2,4},{3,5},{4,2},{5,3},{6,0},{7,1},{8,14},{9,15},{10,... | collective-permute-start | bytes 344072 | tf_op jit(solution)/shard_map/ppermute | solution.py:41
  8.5 2.5 %collective-permute-done.1.refs_4_ = bf16[32,1792]{1,0:T(8,128)(2,1)S(1)} collective-permute-done((bf16[32,1792]{1,0:T(8,128)(2,1)}, bf16[32,1792]{1,0:T(8,128)(2,1)S(1)}, u32[]{:S(2)}, u32[]{:S(2)}) %collective-permute-start.1) | collective-permute-done | bytes 114720 | tf_op jit(solution)/shard_map/ppermute | solution.py:41
  12.5 2.0 %join_rows.2 = (bf16[64,1792]{1,0:T(8,128)(2,1)}, bf16[64,1792]{1,0:T(8,128)(2,1)}, bf16[64,1792]{1,0:T(8,128)(2,1)}) custom-call(bf16[32,1792]{1,0:T(8,128)(2,1)} %get-tuple-element.33.refs_0_, bf16[32,1792]{1,0:T(8,128)(2,1)} %get-tuple-element.34.refs_1_, bf16[32,1792]{1,0:T(8,128)(2,1)} %get-tuple-element.35.refs_2_, bf16[32,1792]{1,0:T(8,128)(2,1)} %copy-done.27, ...), custom_call_target="tpu_custom_call" | custom-call | tf_op jit(solution)/shard_map/join_rows/pallas_call | solution.py:91
  18.0 4.0 %collective-permute-done.3.refs_3_ = bf16[64,1792]{1,0:T(8,128)(2,1)S(1)} collective-permute-done((bf16[64,1792]{1,0:T(8,128)(2,1)}, bf16[64,1792]{1,0:T(8,128)(2,1)S(1)}, u32[]{:S(2)}, u32[]{:S(2)}) %collective-permute-start.3) | collective-permute-done | bytes 229408 | tf_op jit(solution)/shard_map/ppermute | solution.py:41
  25.0 3.0 %join_rows.3 = (bf16[128,1792]{1,0:T(8,128)(2,1)}, bf16[128,1792]{1,0:T(8,128)(2,1)}, bf16[128,1792]{1,0:T(8,128)(2,1)}, bf16[3,128,1792]{2,1,0:T(8,128)(2,1)}) custom-call(bf16[64,1792]{1,0:T(8,128)(2,1)} %get-tuple-element.36.refs_0_, bf16[64,1792]{1,0:T(8,128)(2,1)} %get-tuple-element.37.refs_1_, bf16[64,1792]{1,0:T(8,128)(2,1)} %get-tuple-element.38.refs_2_, ...), custom_call_target="tpu_custom_call" | custom-call | tf_op jit(solution)/shard_map/join_rows/pallas_call | solution.py:91
  31.4 9.8 %collective-permute-done.6.refs_3_ = bf16[128,1792]{1,0:T(8,128)(2,1)S(1)} collective-permute-done((bf16[128,1792]{1,0:T(8,128)(2,1)}, bf16[128,1792]{1,0:T(8,128)(2,1)S(1)}, u32[]{:S(2)}, u32[]{:S(2)}) %collective-permute-start.6) | collective-permute-done | bytes 458784 | tf_op jit(solution)/shard_map/ppermute | solution.py:41
  46.5 7.2 %project_kv.1.refs_0_ = bf16[512,256]{1,0:T(8,128)(2,1)} custom-call(bf16[128,1792]{1,0:T(8,128)(2,1)} %get-tuple-element.39.refs_0_, bf16[128,1792]{1,0:T(8,128)(2,1)} %get-tuple-element.40.refs_1_, bf16[128,1792]{1,0:T(8,128)(2,1)} %get-tuple-element.41.refs_2_, bf16[128,1792]{1,0:T(8,128)(2,1)} %copy-done.1, bf16[128,1792]{1,0:T(8,128)(2,1)} %copy-done.2, ...), custom_call_target="tpu_custom_call" | custom-call | flops 1409286144 | bytes 9000000 | tf_op jit(solution)/shard_map/project_kv/pallas_call | solution.py:171
  53.7 2.9 %collective-permute-start.13 = (bf16[512,256]{1,0:T(8,128)(2,1)}, bf16[512,256]{1,0:T(8,128)(2,1)S(1)}, u32[]{:S(2)}, u32[]{:S(2)}) collective-permute-start(bf16[512,256]{1,0:T(8,128)(2,1)} %project_kv.1.refs_0_), channel_id=1, source_target_pairs={{0,16},{16,32},{32,48},{48,64},{64,80},{80,96},{1,17},{17,33},{33,... | collective-permute-start | bytes 786440 | tf_op jit(solution)/shard_map/ppermute | solution.py:193
  57.3 7.2 %collective-permute-done.13.refs_1_ = bf16[512,256]{1,0:T(8,128)(2,1)S(1)} collective-permute-done((bf16[512,256]{1,0:T(8,128)(2,1)}, bf16[512,256]{1,0:T(8,128)(2,1)S(1)}, u32[]{:S(2)}, u32[]{:S(2)}) %collective-permute-start.13) | collective-permute-done | bytes 262176 | tf_op jit(solution)/shard_map/ppermute | solution.py:193
  64.5 2.9 %collective-permute-start.14 = (bf16[512,256]{1,0:T(8,128)(2,1)S(1)}, bf16[512,256]{1,0:T(8,128)(2,1)S(1)}, u32[]{:S(2)}, u32[]{:S(2)}) collective-permute-start(bf16[512,256]{1,0:T(8,128)(2,1)S(1)} %collective-permute-done.13.refs_1_), channel_id=1, source_target_pairs={{16,32},{32,48},{48,64},{64,80},{80,96},{17,33},{33,49},{49,65},{6... | collective-permute-start | bytes 786440 | tf_op jit(solution)/shard_map/ppermute | solution.py:193
  68.1 6.7 %collective-permute-done.14.refs_2_ = bf16[512,256]{1,0:T(8,128)(2,1)S(1)} collective-permute-done((bf16[512,256]{1,0:T(8,128)(2,1)S(1)}, bf16[512,256]{1,0:T(8,128)(2,1)S(1)}, u32[]{:S(2)}, u32[]{:S(2)}) %collective-permute-start.14) | collective-permute-done | bytes 262176 | tf_op jit(solution)/shard_map/ppermute | solution.py:193
  74.8 2.4 %collective-permute-start.15 = (bf16[512,256]{1,0:T(8,128)(2,1)S(1)}, bf16[512,256]{1,0:T(8,128)(2,1)S(1)}, u32[]{:S(2)}, u32[]{:S(2)}) collective-permute-start(bf16[512,256]{1,0:T(8,128)(2,1)S(1)} %collective-permute-done.14.refs_2_), channel_id=1, source_target_pairs={{32,48},{48,64},{64,80},{80,96},{33,49},{49,65},{65,81},{81,97},{3... | collective-permute-start | bytes 786440 | tf_op jit(solution)/shard_map/ppermute | solution.py:193
  83.1 1.9 %collective-permute-done.15.refs_3_ = bf16[512,256]{1,0:T(8,128)(2,1)S(1)} collective-permute-done((bf16[512,256]{1,0:T(8,128)(2,1)S(1)}, bf16[512,256]{1,0:T(8,128)(2,1)S(1)}, u32[]{:S(2)}, u32[]{:S(2)}) %collective-permute-start.15) | collective-permute-done | bytes 262176 | tf_op jit(solution)/shard_map/ppermute | solution.py:193
  85.0 2.7 %collective-permute-start.19 = (bf16[512,128]{1,0:T(8,128)(2,1)S(1)}, bf16[512,128]{1,0:T(8,128)(2,1)S(1)}, u32[]{:S(2)}, u32[]{:S(2)}) collective-permute-start(bf16[512,128]{1,0:T(8,128)(2,1)S(1)} %slice.18), channel_id=1, source_target_pairs={{48,64},{64,80},{80,96},{49,65},{65,81},{81,97},{50,66},{66,82},{8... | collective-permute-start | bytes 393224 | tf_op jit(solution)/shard_map/ppermute | solution.py:193
  87.7 4.1 %collective-permute-start.20 = (bf16[512,128]{1,0:T(8,128)(2,1)S(1)}, bf16[512,128]{1,0:T(8,128)(2,1)S(1)}, u32[]{:S(2)}, u32[]{:S(2)}) collective-permute-start(bf16[512,128]{1,0:T(8,128)(2,1)S(1)} %slice.19), channel_id=1, source_target_pairs={{80,64},{96,80},{112,96},{81,65},{97,81},{113,97},{82,66},{98,82},... | collective-permute-start | bytes 393224 | tf_op jit(solution)/shard_map/ppermute | solution.py:193
  91.8 7.8 %project_q.1.q_ref = bf16[512,256]{1,0:T(8,128)(2,1)} custom-call(bf16[128,1792]{1,0:T(8,128)(2,1)} %get-tuple-element.39.refs_0_, bf16[128,1792]{1,0:T(8,128)(2,1)} %get-tuple-element.40.refs_1_, bf16[128,1792]{1,0:T(8,128)(2,1)} %get-tuple-element.41.refs_2_, bf16[128,1792]{1,0:T(8,128)(2,1)} %copy-done.1, bf16[128,1792]{1,0:T(8,128)(2,1)} %copy-done.2, ...), custom_call_target="tpu_custom_call" | custom-call | flops 1409286144 | bytes 9000000 | tf_op jit(solution)/shard_map/project_q/pallas_call | solution.py:171
  101.4 12.2 %attend.1 = bf16[512,256]{1,0:T(8,128)(2,1)} custom-call(s32[2]{0:T(128)} %pad_add_fusion.where_ref, bf16[512,256]{1,0:T(8,128)(2,1)} %project_q.1.q_ref, s32[512,128]{1,0:T(8,128)} %broadcast_in_dim.7.position_ref, s32[512,128]{1,0:T(8,128)} %broadcast_in_dim.8.start_ref, s32[1,512]{1,0:T(1,128)} %add.63.offset_ref, bf16[512,256]{1,0:T(8,128)(2,1)} %project_kv.1.refs_0_, ...), custom_call_target="tpu_custom_call" | custom-call | tf_op jit(solution)/shard_map/attend/pallas_call | solution.py:287
  117.3 5.3 %project_out.1 = (bf16[128,1792]{1,0:T(8,128)(2,1)}, bf16[128,1792]{1,0:T(8,128)(2,1)}, bf16[128,1792]{1,0:T(8,128)(2,1)}, bf16[128,1792]{1,0:T(8,128)(2,1)}, bf...) custom-call(bf16[256,256]{1,0:T(8,128)(2,1)} %get-tuple-element.62.mine_ref, bf16[256,256]{1,0:T(8,128)(2,1)} %copy-done.23, ...), custom_call_target="tpu_custom_call" | custom-call | flops 1409286144 | bytes 8500000 | tf_op jit(solution)/shard_map/project_out/pallas_call | solution.py:335
  125.9 9.5 %collective-permute-done.23.refs_3_ = bf16[128,1792]{1,0:T(8,128)(2,1)S(1)} collective-permute-done((bf16[128,1792]{1,0:T(8,128)(2,1)}, bf16[128,1792]{1,0:T(8,128)(2,1)S(1)}, u32[]{:S(2)}, u32[]{:S(2)}) %collective-permute-start.23) | collective-permute-done | bytes 458784 | tf_op jit(solution)/shard_map/ppermute | solution.py:41
  137.8 2.8 %fold_rows.2 = (bf16[64,1792]{1,0:T(8,128)(2,1)}, bf16[64,1792]{1,0:T(8,128)(2,1)}, bf16[64,1792]{1,0:T(8,128)(2,1)}, bf16[64,1792]{1,0:T(8,128)(2,1)}, bf16[64,...) custom-call(bf16[128,1792]{1,0:T(8,128)(2,1)} %get-tuple-element.43.refs_0_, bf16[128,1792]{1,0:T(8,128)(2,1)} %get-tuple-element.44.refs_1_, ...), custom_call_target="tpu_custom_call" | custom-call | tf_op jit(solution)/shard_map/fold_rows/pallas_call | solution.py:370
  143.9 4.7 %collective-permute-done.26.refs_3_ = bf16[64,1792]{1,0:T(8,128)(2,1)S(1)} collective-permute-done((bf16[64,1792]{1,0:T(8,128)(2,1)}, bf16[64,1792]{1,0:T(8,128)(2,1)S(1)}, u32[]{:S(2)}, u32[]{:S(2)}) %collective-permute-start.26) | collective-permute-done | bytes 229408 | tf_op jit(solution)/shard_map/ppermute | solution.py:41
  150.5 2.3 %fold_rows.3 = (bf16[32,1792]{1,0:T(8,128)(2,1)}, bf16[32,1792]{1,0:T(8,128)(2,1)}, bf16[32,1792]{1,0:T(8,128)(2,1)}, bf16[32,1792]{1,0:T(8,128)(2,1)}, bf16[32,...) custom-call(bf16[64,1792]{1,0:T(8,128)(2,1)} %get-tuple-element.49.refs_0_, bf16[64,1792]{1,0:T(8,128)(2,1)} %get-tuple-element.50.refs_1_, ...), custom_call_target="tpu_custom_call" | custom-call | tf_op jit(solution)/shard_map/fold_rows/pallas_call | solution.py:370
  160.7 2.3 %finish.1 = bf16[32,5376]{1,0:T(8,128)(2,1)} custom-call(bf16[32,5376]{1,0:T(8,128)(2,1)} %residual_ref.1, f32[1,5376]{1,0:T(1,128)} %reshape.78.gain_ref, bf16[32,1792]{1,0:T(8,128)(2,1)} %get-tuple-element.55.refs_0_, bf16[32,1792]{1,0:T(8,128)(2,1)} %get-tuple-element.56.refs_1_, bf16[32,1792]{1,0:T(8,128)(2,1)} %get-tuple-element.57.refs_2_, ...), custom_call_target="tpu_custom_call" | custom-call | tf_op jit(solution)/shard_map/finish/pallas_call | solution.py:397
  (137 shorter events, 49.7 us)
Async XLA Ops:
  4.8 6.2 %collective-permute-start.1 = (bf16[32,1792]{1,0:T(8,128)(2,1)}, bf16[32,1792]{1,0:T(8,128)(2,1)S(1)}, u32[]{:S(2)}, u32[]{:S(2)}) collective-permute-start(bf16[32,1792]{1,0:T(8,128)(2,1)} %get-tuple-element.34.refs_1_), channel_id=1, source_target_pairs={{0,6},{1,7},{2,4},{3,5},{4,2},{5,3},{6,0},{7,1},{8,14},{9,15},{10,... | collective-permute-start | bytes 344072 | tf_op jit(solution)/shard_map/ppermute | solution.py:41
  14.6 7.4 %collective-permute-start.3 = (bf16[64,1792]{1,0:T(8,128)(2,1)}, bf16[64,1792]{1,0:T(8,128)(2,1)S(1)}, u32[]{:S(2)}, u32[]{:S(2)}) collective-permute-start(bf16[64,1792]{1,0:T(8,128)(2,1)} %get-tuple-element.36.refs_0_), channel_id=1, source_target_pairs={{0,6},{1,7},{2,4},{3,5},{4,2},{5,3},{6,0},{7,1},{8,14},{9,15},{10,... | collective-permute-start | bytes 688136 | tf_op jit(solution)/shard_map/ppermute | solution.py:41
  16.4 6.2 %collective-permute-start.4 = (bf16[64,1792]{1,0:T(8,128)(2,1)}, bf16[64,1792]{1,0:T(8,128)(2,1)S(1)}, u32[]{:S(2)}, u32[]{:S(2)}) collective-permute-start(bf16[64,1792]{1,0:T(8,128)(2,1)} %get-tuple-element.37.refs_1_), channel_id=1, source_target_pairs={{0,8},{1,9},{2,10},{3,11},{4,12},{5,13},{6,14},{7,15},{8,0},{9,1},... | collective-permute-start | bytes 688136 | tf_op jit(solution)/shard_map/ppermute | solution.py:41
  18.0 6.2 %collective-permute-start.5 = (bf16[64,1792]{1,0:T(8,128)(2,1)}, bf16[64,1792]{1,0:T(8,128)(2,1)S(1)}, u32[]{:S(2)}, u32[]{:S(2)}) collective-permute-start(bf16[64,1792]{1,0:T(8,128)(2,1)} %get-tuple-element.38.refs_2_), channel_id=1, source_target_pairs={{0,2},{1,3},{2,0},{3,1},{4,6},{5,7},{6,4},{7,5},{8,10},{9,11},{10,... | collective-permute-start | bytes 688136 | tf_op jit(solution)/shard_map/ppermute | solution.py:41
  27.9 16.9 %collective-permute-start.9 = (bf16[3,128,1792]{2,1,0:T(8,128)(2,1)}, bf16[3,128,1792]{2,1,0:T(8,128)(2,1)S(1)}, u32[]{:S(2)}, u32[]{:S(2)}) collective-permute-start(bf16[3,128,1792]{2,1,0:T(8,128)(2,1)} %get-tuple-element.42), channel_id=1, source_target_pairs={{0,1},{1,0},{2,3},{3,2},{4,5},{5,4},{6,7},{7,6},{8,9},{9,8},{10,11... | collective-permute-start | bytes 4128776 | tf_op jit(solution)/shard_map/ppermute | solution.py:41
  27.9 87.4 %collective-permute-start.22 = (bf16[256,5376]{1,0:T(8,128)(2,1)}, bf16[256,5376]{1,0:T(8,128)(2,1)}, u32[]{:S(2)}, u32[]{:S(2)}) collective-permute-start(bf16[256,5376]{1,0:T(8,128)(2,1)} %w_mine.1), channel_id=1, source_target_pairs={{0,1},{1,0},{2,3},{3,2},{4,5},{5,4},{6,7},{7,6},{8,9},{9,8},{10,11... | collective-permute-start | bytes 8257544 | tf_op jit(solution)/shard_map/ppermute | solution.py:41
  28.5 12.7 %collective-permute-start.6 = (bf16[128,1792]{1,0:T(8,128)(2,1)}, bf16[128,1792]{1,0:T(8,128)(2,1)S(1)}, u32[]{:S(2)}, u32[]{:S(2)}) collective-permute-start(bf16[128,1792]{1,0:T(8,128)(2,1)} %get-tuple-element.39.refs_0_), channel_id=1, source_target_pairs={{0,8},{1,9},{2,10},{3,11},{4,12},{5,13},{6,14},{7,15},{8,0},{9,1},... | collective-permute-start | bytes 1376264 | tf_op jit(solution)/shard_map/ppermute | solution.py:41
  29.1 12.4 %collective-permute-start.7 = (bf16[128,1792]{1,0:T(8,128)(2,1)}, bf16[128,1792]{1,0:T(8,128)(2,1)S(1)}, u32[]{:S(2)}, u32[]{:S(2)}) collective-permute-start(bf16[128,1792]{1,0:T(8,128)(2,1)} %get-tuple-element.40.refs_1_), channel_id=1, source_target_pairs={{0,2},{1,3},{2,0},{3,1},{4,6},{5,7},{6,4},{7,5},{8,10},{9,11},{10,... | collective-permute-start | bytes 1376264 | tf_op jit(solution)/shard_map/ppermute | solution.py:41
  29.1 13.7 %collective-permute-start.8 = (bf16[128,1792]{1,0:T(8,128)(2,1)}, bf16[128,1792]{1,0:T(8,128)(2,1)S(1)}, u32[]{:S(2)}, u32[]{:S(2)}) collective-permute-start(bf16[128,1792]{1,0:T(8,128)(2,1)} %get-tuple-element.41.refs_2_), channel_id=1, source_target_pairs={{0,6},{1,7},{2,4},{3,5},{4,2},{5,3},{6,0},{7,1},{8,14},{9,15},{10,... | collective-permute-start | bytes 1376264 | tf_op jit(solution)/shard_map/ppermute | solution.py:41
  53.7 10.8 %collective-permute-start.13 = (bf16[512,256]{1,0:T(8,128)(2,1)}, bf16[512,256]{1,0:T(8,128)(2,1)S(1)}, u32[]{:S(2)}, u32[]{:S(2)}) collective-permute-start(bf16[512,256]{1,0:T(8,128)(2,1)} %project_kv.1.refs_0_), channel_id=1, source_target_pairs={{0,16},{16,32},{32,48},{48,64},{64,80},{80,96},{1,17},{17,33},{33,... | collective-permute-start | bytes 786440 | tf_op jit(solution)/shard_map/ppermute | solution.py:193
  56.6 10.8 %collective-permute-start.16 = (bf16[512,256]{1,0:T(8,128)(2,1)}, bf16[512,256]{1,0:T(8,128)(2,1)S(1)}, u32[]{:S(2)}, u32[]{:S(2)}) collective-permute-start(bf16[512,256]{1,0:T(8,128)(2,1)} %project_kv.1.refs_0_), channel_id=1, source_target_pairs={{0,112},{16,0},{32,16},{1,113},{17,1},{33,17},{2,114},{18,2},{34,1... | collective-permute-start | bytes 786440 | tf_op jit(solution)/shard_map/ppermute | solution.py:193
  64.5 10.3 %collective-permute-start.14 = (bf16[512,256]{1,0:T(8,128)(2,1)S(1)}, bf16[512,256]{1,0:T(8,128)(2,1)S(1)}, u32[]{:S(2)}, u32[]{:S(2)}) collective-permute-start(bf16[512,256]{1,0:T(8,128)(2,1)S(1)} %collective-permute-done.13.refs_1_), channel_id=1, source_target_pairs={{16,32},{32,48},{48,64},{64,80},{80,96},{17,33},{33,49},{49,65},{6... | collective-permute-start | bytes 786440 | tf_op jit(solution)/shard_map/ppermute | solution.py:193
  67.4 9.8 %collective-permute-start.17 = (bf16[512,256]{1,0:T(8,128)(2,1)S(1)}, bf16[512,256]{1,0:T(8,128)(2,1)S(1)}, u32[]{:S(2)}, u32[]{:S(2)}) collective-permute-start(bf16[512,256]{1,0:T(8,128)(2,1)S(1)} %collective-permute-done.16), channel_id=1, source_target_pairs={{112,96},{0,112},{16,0},{113,97},{1,113},{17,1},{114,98},{2,114},{... | collective-permute-start | bytes 786440 | tf_op jit(solution)/shard_map/ppermute | solution.py:193
  74.8 10.1 %collective-permute-start.15 = (bf16[512,256]{1,0:T(8,128)(2,1)S(1)}, bf16[512,256]{1,0:T(8,128)(2,1)S(1)}, u32[]{:S(2)}, u32[]{:S(2)}) collective-permute-start(bf16[512,256]{1,0:T(8,128)(2,1)S(1)} %collective-permute-done.14.refs_2_), channel_id=1, source_target_pairs={{32,48},{48,64},{64,80},{80,96},{33,49},{49,65},{65,81},{81,97},{3... | collective-permute-start | bytes 786440 | tf_op jit(solution)/shard_map/ppermute | solution.py:193
  77.3 10.4 %collective-permute-start.18 = (bf16[512,256]{1,0:T(8,128)(2,1)S(1)}, bf16[512,256]{1,0:T(8,128)(2,1)S(1)}, u32[]{:S(2)}, u32[]{:S(2)}) collective-permute-start(bf16[512,256]{1,0:T(8,128)(2,1)S(1)} %collective-permute-done.17.refs_5_), channel_id=1, source_target_pairs={{96,80},{112,96},{0,112},{97,81},{113,97},{1,113},{98,82},{114,98}... | collective-permute-start | bytes 786440 | tf_op jit(solution)/shard_map/ppermute | solution.py:193
  85.0 14.7 %collective-permute-start.19 = (bf16[512,128]{1,0:T(8,128)(2,1)S(1)}, bf16[512,128]{1,0:T(8,128)(2,1)S(1)}, u32[]{:S(2)}, u32[]{:S(2)}) collective-permute-start(bf16[512,128]{1,0:T(8,128)(2,1)S(1)} %slice.18), channel_id=1, source_target_pairs={{48,64},{64,80},{80,96},{49,65},{65,81},{81,97},{50,66},{66,82},{8... | collective-permute-start | bytes 393224 | tf_op jit(solution)/shard_map/ppermute | solution.py:193
  87.7 12.0 %collective-permute-start.20 = (bf16[512,128]{1,0:T(8,128)(2,1)S(1)}, bf16[512,128]{1,0:T(8,128)(2,1)S(1)}, u32[]{:S(2)}, u32[]{:S(2)}) collective-permute-start(bf16[512,128]{1,0:T(8,128)(2,1)S(1)} %slice.19), channel_id=1, source_target_pairs={{80,64},{96,80},{112,96},{81,65},{97,81},{113,97},{82,66},{98,82},... | collective-permute-start | bytes 393224 | tf_op jit(solution)/shard_map/ppermute | solution.py:193
  122.6 12.8 %collective-permute-start.23 = (bf16[128,1792]{1,0:T(8,128)(2,1)}, bf16[128,1792]{1,0:T(8,128)(2,1)S(1)}, u32[]{:S(2)}, u32[]{:S(2)}) collective-permute-start(bf16[128,1792]{1,0:T(8,128)(2,1)} %get-tuple-element.46), channel_id=1, source_target_pairs={{0,2},{1,3},{2,0},{3,1},{4,6},{5,7},{6,4},{7,5},{8,10},{9,11},{10,... | collective-permute-start | bytes 1376264 | tf_op jit(solution)/shard_map/ppermute | solution.py:41
  123.2 13.7 %collective-permute-start.24 = (bf16[128,1792]{1,0:T(8,128)(2,1)}, bf16[128,1792]{1,0:T(8,128)(2,1)S(1)}, u32[]{:S(2)}, u32[]{:S(2)}) collective-permute-start(bf16[128,1792]{1,0:T(8,128)(2,1)} %get-tuple-element.47), channel_id=1, source_target_pairs={{0,6},{1,7},{2,4},{3,5},{4,2},{5,3},{6,0},{7,1},{8,14},{9,15},{10,... | collective-permute-start | bytes 1376264 | tf_op jit(solution)/shard_map/ppermute | solution.py:41
  124.6 12.4 %collective-permute-start.25 = (bf16[128,1792]{1,0:T(8,128)(2,1)}, bf16[128,1792]{1,0:T(8,128)(2,1)S(1)}, u32[]{:S(2)}, u32[]{:S(2)}) collective-permute-start(bf16[128,1792]{1,0:T(8,128)(2,1)} %get-tuple-element.48), channel_id=1, source_target_pairs={{0,8},{1,9},{2,10},{3,11},{4,12},{5,13},{6,14},{7,15},{8,0},{9,1},... | collective-permute-start | bytes 1376264 | tf_op jit(solution)/shard_map/ppermute | solution.py:41
  140.7 7.9 %collective-permute-start.26 = (bf16[64,1792]{1,0:T(8,128)(2,1)}, bf16[64,1792]{1,0:T(8,128)(2,1)S(1)}, u32[]{:S(2)}, u32[]{:S(2)}) collective-permute-start(bf16[64,1792]{1,0:T(8,128)(2,1)} %get-tuple-element.52), channel_id=1, source_target_pairs={{0,6},{1,7},{2,4},{3,5},{4,2},{5,3},{6,0},{7,1},{8,14},{9,15},{10,... | collective-permute-start | bytes 688136 | tf_op jit(solution)/shard_map/ppermute | solution.py:41
  142.3 6.3 %collective-permute-start.27 = (bf16[64,1792]{1,0:T(8,128)(2,1)}, bf16[64,1792]{1,0:T(8,128)(2,1)S(1)}, u32[]{:S(2)}, u32[]{:S(2)}) collective-permute-start(bf16[64,1792]{1,0:T(8,128)(2,1)} %get-tuple-element.53), channel_id=1, source_target_pairs={{0,8},{1,9},{2,10},{3,11},{4,12},{5,13},{6,14},{7,15},{8,0},{9,1},... | collective-permute-start | bytes 688136 | tf_op jit(solution)/shard_map/ppermute | solution.py:41
  143.6 6.2 %collective-permute-start.28 = (bf16[64,1792]{1,0:T(8,128)(2,1)}, bf16[64,1792]{1,0:T(8,128)(2,1)S(1)}, u32[]{:S(2)}, u32[]{:S(2)}) collective-permute-start(bf16[64,1792]{1,0:T(8,128)(2,1)} %get-tuple-element.54), channel_id=1, source_target_pairs={{0,2},{1,3},{2,0},{3,1},{4,6},{5,7},{6,4},{7,5},{8,10},{9,11},{10,... | collective-permute-start | bytes 688136 | tf_op jit(solution)/shard_map/ppermute | solution.py:41
  153.8 6.2 %collective-permute-start.31 = (bf16[32,1792]{1,0:T(8,128)(2,1)}, bf16[32,1792]{1,0:T(8,128)(2,1)S(1)}, u32[]{:S(2)}, u32[]{:S(2)}) collective-permute-start(bf16[32,1792]{1,0:T(8,128)(2,1)} %get-tuple-element.60), channel_id=1, source_target_pairs={{0,6},{1,7},{2,4},{3,5},{4,2},{5,3},{6,0},{7,1},{8,14},{9,15},{10,... | collective-permute-start | bytes 344072 | tf_op jit(solution)/shard_map/ppermute | solution.py:41
  (41 other events, 251.4 us)

commit v2 on v1

v2 whole, which is shorter than its diff:
```python
import functools
import math

import jax
import jax.numpy as jnp
from jax import lax
from jax.experimental import pallas as pl
from jax.experimental.pallas import tpu as pltpu
from jax.sharding import PartitionSpec as P

query_scalar = 168.0
rope_base = 1000000.0
rope_factor = 8.0
epsilon = 1e-06

D = 5376
THIRD = D // 3
HD = 128
ROWS = 32
BLOCK = 512

XA, XB, YY, CC = 2, 6, 8, 1
ORDERS = ((XA, XB, YY), (XB, YY, XA), (YY, XA, XB))
BITS = {XA: 1, XB: 2, YY: 4}


def mp_mask(index):
    return (XA if index & 1 else 0) ^ (XB if index & 2 else 0) ^ (YY if index & 4 else 0)


def gathered_order(part):
    first, second, third = (BITS[link] for link in ORDERS[part])
    return [
        (first if k & 1 else 0) | (second if k & 2 else 0) | (third if k & 4 else 0)
        for k in range(8)
    ]


def swap(value, link):
    return lax.ppermute(value, "mp", [(m, m ^ link) for m in range(16)])


def whole(count):
    return [pl.BlockSpec(memory_space=pltpu.VMEM)] * count


def params(mebibytes):
    return pltpu.CompilerParams(vmem_limit_bytes=mebibytes * 1024 * 1024)


def shape(rows, columns, dtype=jnp.bfloat16):
    return jax.ShapeDtypeStruct((rows, columns), dtype)


def norm_kernel(x_ref, gain_ref, *outs):
    square = jnp.zeros((ROWS, HD), jnp.float32)
    for k in range(D // HD):
        x = x_ref[:, k * HD : (k + 1) * HD].astype(jnp.float32)
        square = square + x * x
    inverse = lax.rsqrt(jnp.sum(square, axis=-1, keepdims=True) / D + epsilon)
    for part, out in enumerate(outs):
        for k in range(THIRD // HD):
            at = part * (THIRD // HD) + k
            x = x_ref[:, at * HD : (at + 1) * HD].astype(jnp.float32)
            out[:, k * HD : (k + 1) * HD] = (x * inverse * gain_ref[at : at + 1]).astype(
                jnp.bfloat16
            )


def norm_rows(residual, gain):
    return pl.pallas_call(
        norm_kernel,
        out_shape=[shape(ROWS, THIRD)] * 3,
        in_specs=whole(2),
        out_specs=whole(3),
        compiler_params=params(4),
        name="norm_rows",
    )(residual, gain.reshape(D // HD, HD))


def join_kernel(extra, *refs):
    held, came, outs = refs[0:3], refs[3:6], refs[6:]
    for part in range(3):
        rows = held[part].shape[0]
        outs[part][0:rows] = held[part][...]
        outs[part][rows : 2 * rows] = came[part][...]
        if extra:
            outs[3][part, 0:rows] = held[part][...]
            outs[3][part, rows : 2 * rows] = came[part][...]


def join(held, came, extra):
    rows = held[0].shape[0]
    outs = [shape(2 * rows, THIRD)] * 3
    if extra:
        outs = outs + [jax.ShapeDtypeStruct((3, 2 * rows, THIRD), jnp.bfloat16)]
    return pl.pallas_call(
        functools.partial(join_kernel, extra),
        out_shape=outs,
        in_specs=whole(6),
        out_specs=whole(len(outs)),
        compiler_params=params(10),
        name="join_rows",
    )(*held, *came)


def gather_tokens(thirds, tables):
    came = [swap(thirds[p], ORDERS[p][0]) for p in range(3)]
    two = join(thirds, came, False)
    came = [swap(two[p], ORDERS[p][1]) for p in range(3)]
    *four, packed = join(two, came, True)
    late = [swap(four[p], ORDERS[p][2]) for p in range(3)]
    other = swap(packed, CC)
    *late, cosine, sine, where, position, start, offset = lax.optimization_barrier(
        (*late, *tables)
    )
    other_late = [swap(late[p], CC) for p in range(3)]
    return (four, late, other, other_late), cosine, sine, where, position, start, offset


def rotate(raw, gain, cosine, sine):
    inverse = lax.rsqrt(jnp.mean(raw * raw, axis=-1, keepdims=True) + epsilon)
    scaled = raw * inverse * gain
    turned = pltpu.roll(scaled, HD // 2, 1)
    return (scaled * cosine + turned * sine).astype(jnp.bfloat16)


def project_kernel(weight_count, *refs):
    x_refs = refs[0:10]
    w_refs = refs[10 : 10 + weight_count]
    gain_ref, cos_ref, sin_ref, out_ref = refs[10 + weight_count :]
    four, late, other, other_late = x_refs[0:3], x_refs[3:6], x_refs[6], x_refs[7:10]
    total = None
    for part in range(3):
        order = gathered_order(part)
        rows = []
        for core in range(2):
            for place in range(8):
                k = order.index(place)
                at = (k % 4) * ROWS
                if core == 0:
                    rows.append((four if k < 4 else late)[part][at : at + ROWS])
                elif k < 4:
                    rows.append(other[part, at : at + ROWS])
                else:
                    rows.append(other_late[part][at : at + ROWS])
        weights = [w[part * THIRD : (part + 1) * THIRD] for w in w_refs]
        product = jnp.dot(
            jnp.concatenate(rows, axis=0),
            jnp.concatenate(weights, axis=1) if weight_count == 2 else weights[0],
            preferred_element_type=jnp.float32,
        )
        total = product if part == 0 else total + product
    gain = gain_ref[...]
    out_ref[:, 0:HD] = rotate(total[:, 0:HD], gain, cos_ref[...], sin_ref[...])
    if weight_count == 1:
        out_ref[:, HD : 2 * HD] = rotate(total[:, HD : 2 * HD], gain, cos_ref[...], sin_ref[...])
    else:
        out_ref[:, HD : 2 * HD] = total[:, HD : 2 * HD].astype(jnp.bfloat16)


def project(pieces, weights, gain, cosine, sine, name):
    four, late, other, other_late = pieces
    return pl.pallas_call(
        functools.partial(project_kernel, len(weights)),
        out_shape=shape(BLOCK, 2 * HD),
        in_specs=whole(13 + len(weights)),
        out_specs=whole(1)[0],
        compiler_params=params(18),
        cost_estimate=pl.CostEstimate(
            flops=2 * BLOCK * D * 2 * HD, bytes_accessed=9000000, transcendentals=0
        ),
        name=name,
    )(*four, *late, other, *other_late, *weights, gain.reshape(1, HD), cosine, sine)


NEG = -1e30
TILE = 256


def move(value, pairs):
    return lax.ppermute(value, "ctx", pairs)


def attend_kernel(distances, joint, first, last, *refs):
    where_ref, q_ref, position_ref, start_ref, offset_ref = refs[0:5]
    refs = refs[5:]
    blocks, refs = refs[: len(joint)], refs[len(joint) :]
    if not first:
        old_state, refs = refs[0:3], refs[3:]
    if last:
        out_ref, state = refs[0], refs[1:4]
    else:
        state = refs[0:3]
    top, total, acc = state
    block = where_ref[0]
    live = where_ref[1]
    rows_here = q_ref.shape[0]
    factor = math.log2(math.e) / math.sqrt(query_scalar)

    def step(distance, keys_ref, values_ref, source):
        opening = source is None
        keys = keys_ref[...]
        values = values_ref[...]
        key_index = offset_ref[...] + (block - distance) * BLOCK
        for tile in range(rows_here // TILE):
            rows = slice(tile * TILE, (tile + 1) * TILE)
            position = position_ref[rows]
            start = start_ref[rows]
            for head in range(2):
                scores = lax.dot_general(
                    q_ref[rows, head * HD : (head + 1) * HD],
                    keys,
                    (((1,), (1,)), ((), ())),
                    preferred_element_type=jnp.float32,
                )
                pieces = []
                for k in range(BLOCK // HD):
                    index = key_index[:, k * HD : (k + 1) * HD]
                    allowed = index >= start
                    if distance == 0:
                        allowed = allowed & (index <= position)
                    pieces.append(
                        jnp.where(allowed, scores[:, k * HD : (k + 1) * HD] * factor, NEG)
                    )
                best = jnp.maximum(
                    jnp.maximum(pieces[0], pieces[1]), jnp.maximum(pieces[2], pieces[3])
                )
                best = jnp.max(best, axis=-1, keepdims=True)
                if opening:
                    new = jnp.broadcast_to(best, (TILE, HD))
                else:
                    old = source[0][head, rows]
                    new = jnp.maximum(old, best)
                exps = [jnp.exp2(piece - new) for piece in pieces]
                sums = (exps[0] + exps[1]) + (exps[2] + exps[3])
                weights = jnp.concatenate([e.astype(jnp.bfloat16) for e in exps], axis=1)
                product = jnp.dot(weights, values, preferred_element_type=jnp.float32)
                if not opening:
                    fade = jnp.exp2(old - new)
                    sums = source[1][head, rows] * fade + sums
                    product = source[2][head, rows] * fade + product
                total[head, rows] = sums
                acc[head, rows] = product
                top[head, rows] = new

    def keep():
        for new_ref, old_ref in zip(state, old_state):
            new_ref[...] = old_ref[...]

    source = None if first else old_state
    k = 0
    for distance, whole_block in zip(distances, joint):
        if whole_block == 2:
            continue
        if whole_block:
            keys_ref = blocks[k].at[:, pl.ds(0, HD)]
            values_ref = blocks[k].at[:, pl.ds(HD, HD)]
            k += 1
        else:
            keys_ref, values_ref = blocks[k], blocks[k + 1]
            k += 2
        if distance == 0:
            step(0, keys_ref, values_ref, None)
        else:
            pl.when(distance < live)(
                functools.partial(step, distance, keys_ref, values_ref, source)
            )
            if source is not state:
                pl.when(distance >= live)(keep)
        source = state
    if last:
        for head in range(2):
            denominator = jnp.sum(total[head], axis=-1, keepdims=True)
            out_ref[:, head * HD : (head + 1) * HD] = (acc[head] / denominator).astype(
                jnp.bfloat16
            )


def attend(tables, query, distances, joint, blocks, state, last, half=None):
    where, position, start, offset = tables
    first = state is None
    state = () if first else tuple(state)
    rows_here = BLOCK // 2 if last else BLOCK
    state_shape = jax.ShapeDtypeStruct((2, rows_here, HD), jnp.float32)
    if last:
        out_shape, out_specs = shape(rows_here, 2 * HD), whole(1)[0]
        scratch = [pltpu.VMEM((2, rows_here, HD), jnp.float32)] * 3
        row_specs = [
            pl.BlockSpec((rows_here, 2 * HD), lambda k: (half, 0)),
            pl.BlockSpec((rows_here, HD), lambda k: (half, 0)),
            pl.BlockSpec((rows_here, HD), lambda k: (half, 0)),
        ]
        state_specs = [pl.BlockSpec((2, rows_here, HD), lambda k: (0, half, 0))] * 3
    else:
        out_shape, out_specs = [state_shape] * 3, whole(3)
        scratch = []
        row_specs = whole(3)
        state_specs = whole(3)
    return pl.pallas_call(
        functools.partial(attend_kernel, distances, joint, first, last),
        out_shape=out_shape,
        grid=(1,) if last else (),
        in_specs=[pl.BlockSpec(memory_space=pltpu.SMEM)]
        + row_specs
        + whole(1 + len(blocks))
        + (state_specs if state else []),
        out_specs=out_specs,
        scratch_shapes=scratch,
        compiler_params=params(12),
        cost_estimate=pl.CostEstimate(
            flops=800000000 * len(distances), bytes_accessed=3000000, transcendentals=1000000
        ),
        name="attend",
    )(where, query, position, start, offset, *blocks, *state)


def share_and_attend(rows, make_query, tables):
    tie = lax.optimization_barrier
    forward, backward = rows, rows

    def onward(k, forward, backward):
        return (
            move(forward, [(c, c + 1) for c in range(k, 6)]),
            move(backward, [((c - k) % 8, (c - k - 1) % 8) for c in range(3)]),
        )

    one, back_one = onward(0, rows, rows)
    query = make_query()
    state = attend(tables, query, (0,), (1,), [rows], None, False)
    one, back_one, state = tie((one, back_one, state))
    two, back_two = onward(1, one, back_one)
    state = attend(tables, query, (1,), (1,), [one], state, False)
    two, back_two, state = tie((two, back_two, state))
    three, back_three = onward(2, two, back_two)
    state = attend(tables, query, (2, 6), (1, 1), [two, back_two], state, False)
    three, back_three, state = tie((three, back_three, state))
    key_far = move(three[:, :HD], [(3, 4), (4, 5), (5, 6)])
    value_far = move(back_three[:, HD:], [(5, 4), (6, 5), (7, 6)])
    state = attend(tables, query, (3, 5), (1, 1), [three, back_three], state, False)
    key_far, value_far, state = tie((key_far, value_far, state))
    goes = attend(tables, query, (4,), (0, 2), [key_far, value_far], state, True, 1)
    stays = attend(tables, query, (4,), (0, 2), [key_far, value_far], state, True, 0)
    return stays, swap(goes, CC)


CHUNK = 256


def output_kernel(mine_ref, theirs_ref, w_mine, w_theirs, *outs):
    def groups(weight_columns):
        return jnp.dot(mine_ref[...], w_mine[:, weight_columns], preferred_element_type=jnp.float32).astype(
            jnp.bfloat16
        ).astype(jnp.float32) + jnp.dot(
            theirs_ref[...], w_theirs[:, weight_columns], preferred_element_type=jnp.float32
        ).astype(jnp.bfloat16).astype(jnp.float32)

    for part in range(3):
        bit = BITS[ORDERS[part][0]]
        for chunk in range(THIRD // CHUNK):
            summed = groups(
                slice(part * THIRD + chunk * CHUNK, part * THIRD + (chunk + 1) * CHUNK)
            ).astype(jnp.bfloat16)
            here = slice(chunk * CHUNK, (chunk + 1) * CHUNK)
            counts = [0, 0]
            for place in range(8):
                goes = 1 if place & bit else 0
                at = counts[goes] * ROWS
                counts[goes] += 1
                outs[2 * part + goes][at : at + ROWS, here] = summed[
                    place * ROWS : (place + 1) * ROWS
                ]


def project_out(mine, theirs, w_mine, w_theirs):
    return pl.pallas_call(
        output_kernel,
        out_shape=[shape(128, THIRD)] * 6,
        in_specs=whole(4),
        out_specs=whole(6),
        compiler_params=params(24),
        cost_estimate=pl.CostEstimate(
            flops=4 * 256 * 256 * D, bytes_accessed=8500000, transcendentals=0
        ),
        name="project_out",
    )(mine, theirs, w_mine, w_theirs)


def remaining(part, level):
    return sorted(BITS[link] for link in ORDERS[part][level:])


def fold_kernel(level, *refs):
    kept, came, outs = refs[0:3], refs[3:6], refs[6:]
    for part in range(3):
        bits = remaining(part, level)
        goes_bit = bits.index(BITS[ORDERS[part][level]])
        summed = (
            kept[part][...].astype(jnp.float32) + came[part][...].astype(jnp.float32)
        ).astype(jnp.bfloat16)
        counts = [0, 0]
        for k in range(1 << len(bits)):
            goes = (k >> goes_bit) & 1
            at = counts[goes] * ROWS
            counts[goes] += 1
            outs[2 * part + goes][at : at + ROWS] = summed[k * ROWS : (k + 1) * ROWS]


def fold(kept, came, level):
    rows = kept[0].shape[0] // 2
    return pl.pallas_call(
        functools.partial(fold_kernel, level),
        out_shape=[shape(rows, THIRD)] * 6,
        in_specs=whole(6),
        out_specs=whole(6),
        compiler_params=params(12),
        name="fold_rows",
    )(*kept, *came)


def finish_kernel(residual_ref, gain_ref, *refs):
    kept, came, out, sums = refs[0:3], refs[3:6], refs[6], refs[7]
    square = jnp.zeros((ROWS, HD), jnp.float32)
    for part in range(3):
        for k in range(THIRD // HD):
            here = slice(k * HD, (k + 1) * HD)
            summed = kept[part][:, here].astype(jnp.float32) + came[part][:, here].astype(
                jnp.float32
            )
            at = part * THIRD + k * HD
            sums[:, at : at + HD] = summed
            square = square + summed * summed
    inverse = lax.rsqrt(jnp.sum(square, axis=-1, keepdims=True) / D + epsilon)
    for k in range(D // HD):
        here = slice(k * HD, (k + 1) * HD)
        out[:, here] = (
            residual_ref[:, here].astype(jnp.float32)
            + sums[:, here] * inverse * gain_ref[k : k + 1]
        ).astype(jnp.bfloat16)


def finish(residual, gain, kept, came):
    return pl.pallas_call(
        finish_kernel,
        out_shape=shape(ROWS, D),
        in_specs=whole(8),
        out_specs=whole(1)[0],
        scratch_shapes=[pltpu.VMEM((ROWS, D), jnp.float32)],
        compiler_params=params(6),
        name="finish",
    )(residual, gain.reshape(D // HD, HD), *kept, *came)


def reduce_tokens(halves):
    kept, goes = halves[0::2], halves[1::2]
    for level in range(3):
        came = [swap(goes[p], ORDERS[p][level]) for p in range(3)]
        if level == 2:
            return kept, came
        halves = fold(kept, came, level + 1)
        kept, goes = halves[0::2], halves[1::2]


def body(
    residual_in,
    document_start,
    input_gain,
    query_weight,
    key_weight,
    value_weight,
    query_gain,
    key_gain,
    output_weight,
    post_gain,
):
    thirds = norm_rows(residual_in, input_gain)

    block = lax.axis_index("ctx")
    mine = lax.axis_index("mp")
    masks = jnp.array([mp_mask(k & 7) ^ (k >> 3) for k in range(16)], jnp.int32)
    owners = mine ^ masks
    inside = (owners[:, None] * ROWS + jnp.arange(ROWS, dtype=jnp.int32)[None, :]).reshape(BLOCK)
    position = block * BLOCK + inside
    start = document_start.reshape(16, ROWS)[owners].reshape(BLOCK)
    frequency = rope_base ** (-(jnp.arange(HD // 2, dtype=jnp.float32) * 2.0 / HD))
    angles = ((position - start).astype(jnp.float32) / rope_factor)[:, None] * frequency[None, :]
    cosine = jnp.cos(angles)
    sine = jnp.sin(angles)
    cosine = jnp.concatenate([cosine, cosine], axis=1)
    sine = jnp.concatenate([-sine, sine], axis=1)
    live = block - jnp.min(document_start) // BLOCK + 1
    where = jnp.stack([block, live]).astype(jnp.int32)
    position_wide = jnp.broadcast_to(position[:, None], (BLOCK, HD))
    start_wide = jnp.broadcast_to(start[:, None], (BLOCK, HD))

    pieces, cosine, sine, where, position_wide, start_wide, offset = gather_tokens(
        thirds, (cosine, sine, where, position_wide, start_wide, inside[None, :])
    )
    w_theirs = swap(output_weight, CC)
    tables = (where, position_wide, start_wide, offset)
    rows = project(pieces, [key_weight, value_weight], key_gain, cosine, sine, "project_kv")
    mine, theirs = share_and_attend(
        rows,
        lambda: project(pieces, [query_weight], query_gain, cosine, sine, "project_q"),
        tables,
    )
    halves = project_out(mine, theirs, output_weight, w_theirs)
    kept, came = reduce_tokens(halves)
    return finish(residual_in, post_gain, kept, came)


def solution(mesh):
    return jax.shard_map(
        body,
        mesh=mesh,
        in_specs=(
            P(("docs", "ctx", "mp"), None),
            P(("docs", "ctx")),
            P(),
            P(None, "mp"),
            P(None, "mp"),
            P(None, "mp"),
            P(),
            P(),
            P("mp", None),
            P(),
        ),
        out_specs=P(("docs", "ctx", "mp"), None),
        check_vma=False,
    )
```

time: 164 us -> 127 us (0.77)
  Pallas kernels: 46.9 us -> 23.1 us
  local copies, waits for them, and re-layouts: 12.7 us -> 4.91 us
  waiting for transfers between devices: 59 us -> 51.6 us
  starting transfers between devices: 38 us -> 39.9 us
    pallas_call x2, Pallas kernels: 15 us -> 4.36 us  [project(): pl.pallas_call(functools.partial(project_kernel, len(weights)), out_shape...]
    pallas_call x2, Pallas kernels: 5.15 us -> 0.47 us  [fold(): pl.pallas_call(functools.partial(fold_kernel, level), out_shape=[shape(ro...]
    ppermute x8, waiting for transfers between devices: 15.8 us -> 11.6 us  [move(): return lax.ppermute(value, 'ctx', pairs)]
    pallas_call x2, Pallas kernels: 5.01 us -> 1.3 us  [join(): pl.pallas_call(functools.partial(join_kernel, extra), out_shape=outs, in_...]
    ppermute x24, waiting for transfers between devices: 43.2 us -> 40 us  [swap(): return lax.ppermute(value, 'mp', [(m, m ^ link) for m in range(16)])]
    unnamed x66 -> x20, local copies, waits for them, and re-layouts: 5.91 us -> 3.09 us
    reshape x2 -> x0, local copies, waits for them, and re-layouts: 2 us -> none  [the longest x1 1.39 us: norm_rows(): gain.reshape(1, D)]
    pallas_call x1, Pallas kernels: 5.32 us -> 3.38 us  [project_out(): pl.pallas_call(output_kernel, out_shape=[shape(128, THIRD)] * 6, in_specs...]
  transfers between devices with their start and end apart: 32 -> 32, of which waited for: 19 -> 23; matrix products, arithmetic and copies ran while one was open for 5% -> 4% of each run, Pallas kernels for 17% -> 14%
where the time goes in v2:
time: 127 us; the launch traced here: 126 us
  waiting for transfers between devices  51.6 us (41%)
  starting transfers between devices  39.9 us (31%)
  Pallas kernels  23.1 us (18%)
  local copies, waits for them, and re-layouts  4.91 us (4%)
  other arithmetic  3.34 us (3%)
  between operations  2.61 us (2%)
    ppermute x24, waiting for transfers between devices, swap(): return lax.ppermute(value, 'mp', [(m, m ^ link) for m in range(16)])  40 us
    ppermute x24, starting transfers between devices, swap(): return lax.ppermute(value, 'mp', [(m, m ^ link) for m in range(16)])  21.1 us
    ppermute x8, starting transfers between devices, move(): return lax.ppermute(value, 'ctx', pairs)  18.8 us
    pallas_call x6, Pallas kernels, attend(): pl.pallas_call(functools.partial(attend_kernel, distances, joint, first,...  12.4 us
    ppermute x8, waiting for transfers between devices, move(): return lax.ppermute(value, 'ctx', pairs)  11.6 us
    pallas_call x2, Pallas kernels, project(): pl.pallas_call(functools.partial(project_kernel, len(weights)), out_shape...  4.36 us
    pallas_call x1, Pallas kernels, project_out(): pl.pallas_call(output_kernel, out_shape=[shape(128, THIRD)] * 6, in_specs...  3.38 us
    unnamed x20, local copies, waits for them, and re-layouts  3.09 us
  transfers between devices with their start and end apart: 32, of which 23 were waited for; matrix products, arithmetic and copies ran while one was open for 4% of the time, Pallas kernels for 14%

profile of v2, /device:TPU:160, one launch (start us, length us, event | category | flops | bytes accessed | tf_op | source)
XLA Modules:
  0.0 125.5 jit_solution(1859613030664974599)
XLA Ops:
  3.5 2.1 %collective-permute-start.1 = (bf16[32,1792]{1,0:T(8,128)(2,1)S(1)}, bf16[32,1792]{1,0:T(8,128)(2,1)S(1)}, u32[]{:S(2)}, u32[]{:S(2)}) collective-permute-start(bf16[32,1792]{1,0:T(8,128)(2,1)S(1)} %get-tuple-element.75.refs_1_), channel_id=1, source_target_pairs={{0,6},{1,7},{2,4},{3,5},{4,2},{5,3},{6,0},{7,1},{8,14},{9,15},{10,... | collective-permute-start | bytes 344072 | tf_op jit(solution)/shard_map/ppermute | solution.py:40
  7.2 2.3 %collective-permute-done.1.refs_4_ = bf16[32,1792]{1,0:T(8,128)(2,1)S(1)} collective-permute-done((bf16[32,1792]{1,0:T(8,128)(2,1)S(1)}, bf16[32,1792]{1,0:T(8,128)(2,1)S(1)}, u32[]{:S(2)}, u32[]{:S(2)}) %collective-permute-start.1) | collective-permute-done | bytes 114720 | tf_op jit(solution)/shard_map/ppermute | solution.py:40
  23.1 2.0 %collective-permute-start.8 = (bf16[128,1792]{1,0:T(8,128)(2,1)S(1)}, bf16[128,1792]{1,0:T(8,128)(2,1)S(1)}, u32[]{:S(2)}, u32[]{:S(2)}) collective-permute-start(bf16[128,1792]{1,0:T(8,128)(2,1)S(1)} %get-tuple-element.82.refs_2_), channel_id=1, source_target_pairs={{0,6},{1,7},{2,4},{3,5},{4,2},{5,3},{6,0},{7,1},{8,14},{9,15},{10,... | collective-permute-start | bytes 1376264 | tf_op jit(solution)/shard_map/ppermute | solution.py:40
  26.4 9.1 %collective-permute-done.6.refs_3_ = bf16[128,1792]{1,0:T(8,128)(2,1)S(1)} collective-permute-done((bf16[128,1792]{1,0:T(8,128)(2,1)S(1)}, bf16[128,1792]{1,0:T(8,128)(2,1)S(1)}, u32[]{:S(2)}, u32[]{:S(2)}) %collective-permute-start.6) | collective-permute-done | bytes 458784 | tf_op jit(solution)/shard_map/ppermute | solution.py:40
  41.8 2.0 %project_kv.1.refs_5_ = bf16[512,256]{1,0:T(8,128)(2,1)S(1)} custom-call(bf16[128,1792]{1,0:T(8,128)(2,1)S(1)} %get-tuple-element.80.refs_0_, bf16[128,1792]{1,0:T(8,128)(2,1)S(1)} %get-tuple-element.81.refs_1_, bf16[128,1792]{1,0:T(8,128)(2,1)S(1)} %get-tuple-element.82.refs_2_, bf16[128,1792]{1,0:T(8,128)(2,1)S(1)} %collective-permute-done.6.refs_3_, ...), custom_call_target="tpu_custom_call" | custom-call | flops 1409286144 | bytes 9000000 | tf_op jit(solution)/shard_map/project_kv/pallas_call | solution.py:164
  43.8 2.9 %collective-permute-start.13 = (bf16[512,256]{1,0:T(8,128)(2,1)S(1)}, bf16[512,256]{1,0:T(8,128)(2,1)S(1)}, u32[]{:S(2)}, u32[]{:S(2)}) collective-permute-start(bf16[512,256]{1,0:T(8,128)(2,1)S(1)} %project_kv.1.refs_5_), channel_id=1, source_target_pairs={{0,16},{16,32},{32,48},{48,64},{64,80},{80,96},{1,17},{17,33},{33,... | collective-permute-start | bytes 786440 | tf_op jit(solution)/shard_map/ppermute | solution.py:182
  47.6 2.4 %project_q.1.refs_1_ = bf16[512,256]{1,0:T(8,128)(2,1)S(1)} custom-call(bf16[128,1792]{1,0:T(8,128)(2,1)S(1)} %get-tuple-element.80.refs_0_, bf16[128,1792]{1,0:T(8,128)(2,1)S(1)} %get-tuple-element.81.refs_1_, bf16[128,1792]{1,0:T(8,128)(2,1)S(1)} %get-tuple-element.82.refs_2_, bf16[128,1792]{1,0:T(8,128)(2,1)S(1)} %collective-permute-done.6.refs_3_, ...), custom_call_target="tpu_custom_call" | custom-call | flops 1409286144 | bytes 9000000 | tf_op jit(solution)/shard_map/project_q/pallas_call | solution.py:164
  50.0 2.0 %attend.6 = (f32[2,512,128]{2,1,0:T(8,128)S(1)}, f32[2,512,128]{2,1,0:T(8,128)S(1)}, f32[2,512,128]{2,1,0:T(8,128)S(1)}) custom-call(s32[2]{0:T(128)S(1)} %pad_add_fusion.refs_0_, bf16[512,256]{1,0:T(8,128)(2,1)S(1)} %project_q.1.refs_1_, s32[512,128]{1,0:T(8,128)S(1)} %broadcast_in_dim.7.refs_2_, s32[512,128]{1,0:T(8,128)S(1)} %broadcast_in_dim.8.refs_3_, ...), custom_call_target="tpu_custom_call" | custom-call | flops 800000000 | bytes 3000000 | tf_op jit(solution)/shard_map/attend/pallas_call | solution.py:300
  51.9 2.1 %collective-permute-done.13.refs_5_ = bf16[512,256]{1,0:T(8,128)(2,1)S(1)} collective-permute-done((bf16[512,256]{1,0:T(8,128)(2,1)S(1)}, bf16[512,256]{1,0:T(8,128)(2,1)S(1)}, u32[]{:S(2)}, u32[]{:S(2)}) %collective-permute-start.13) | collective-permute-done | bytes 262176 | tf_op jit(solution)/shard_map/ppermute | solution.py:182
  54.0 2.9 %collective-permute-start.15 = (bf16[512,256]{1,0:T(8,128)(2,1)S(1)}, bf16[512,256]{1,0:T(8,128)(2,1)S(1)}, u32[]{:S(2)}, u32[]{:S(2)}) collective-permute-start(bf16[512,256]{1,0:T(8,128)(2,1)S(1)} %collective-permute-done.13.refs_5_), channel_id=1, source_target_pairs={{16,32},{32,48},{48,64},{64,80},{80,96},{17,33},{33,49},{49,65},{6... | collective-permute-start | bytes 786440 | tf_op jit(solution)/shard_map/ppermute | solution.py:182
  57.6 1.9 %attend.7 = (f32[2,512,128]{2,1,0:T(8,128)S(1)}, f32[2,512,128]{2,1,0:T(8,128)S(1)}, f32[2,512,128]{2,1,0:T(8,128)S(1)}) custom-call(s32[2]{0:T(128)S(1)} %pad_add_fusion.refs_0_, bf16[512,256]{1,0:T(8,128)(2,1)S(1)} %project_q.1.refs_1_, s32[512,128]{1,0:T(8,128)S(1)} %broadcast_in_dim.7.refs_2_, s32[512,128]{1,0:T(8,128)S(1)} %broadcast_in_dim.8.refs_3_, ...), custom_call_target="tpu_custom_call" | custom-call | flops 800000000 | bytes 3000000 | tf_op jit(solution)/shard_map/attend/pallas_call | solution.py:300
  59.6 4.3 %collective-permute-done.15.refs_5_ = bf16[512,256]{1,0:T(8,128)(2,1)S(1)} collective-permute-done((bf16[512,256]{1,0:T(8,128)(2,1)S(1)}, bf16[512,256]{1,0:T(8,128)(2,1)S(1)}, u32[]{:S(2)}, u32[]{:S(2)}) %collective-permute-start.15) | collective-permute-done | bytes 262176 | tf_op jit(solution)/shard_map/ppermute | solution.py:182
  63.9 4.3 %collective-permute-start.17 = (bf16[512,256]{1,0:T(8,128)(2,1)S(1)}, bf16[512,256]{1,0:T(8,128)(2,1)S(1)}, u32[]{:S(2)}, u32[]{:S(2)}) collective-permute-start(bf16[512,256]{1,0:T(8,128)(2,1)S(1)} %collective-permute-done.15.refs_5_), channel_id=1, source_target_pairs={{32,48},{48,64},{64,80},{80,96},{33,49},{49,65},{65,81},{81,97},{3... | collective-permute-start | bytes 786440 | tf_op jit(solution)/shard_map/ppermute | solution.py:182
  69.5 2.0 %attend.8 = (f32[2,512,128]{2,1,0:T(8,128)S(1)}, f32[2,512,128]{2,1,0:T(8,128)S(1)}, f32[2,512,128]{2,1,0:T(8,128)S(1)}) custom-call(s32[2]{0:T(128)S(1)} %pad_add_fusion.refs_0_, bf16[512,256]{1,0:T(8,128)(2,1)S(1)} %project_q.1.refs_1_, s32[512,128]{1,0:T(8,128)S(1)} %broadcast_in_dim.7.refs_2_, s32[512,128]{1,0:T(8,128)S(1)} %broadcast_in_dim.8.refs_3_, ...), custom_call_target="tpu_custom_call" | custom-call | flops 1600000000 | bytes 3000000 | tf_op jit(solution)/shard_map/attend/pallas_call | solution.py:300
  71.5 2.1 %collective-permute-done.17.refs_5_ = bf16[512,256]{1,0:T(8,128)(2,1)S(1)} collective-permute-done((bf16[512,256]{1,0:T(8,128)(2,1)S(1)}, bf16[512,256]{1,0:T(8,128)(2,1)S(1)}, u32[]{:S(2)}, u32[]{:S(2)}) %collective-permute-start.17) | collective-permute-done | bytes 262176 | tf_op jit(solution)/shard_map/ppermute | solution.py:182
  73.6 3.1 %collective-permute-done.18.refs_6_ = bf16[512,256]{1,0:T(8,128)(2,1)S(1)} collective-permute-done((bf16[512,256]{1,0:T(8,128)(2,1)S(1)}, bf16[512,256]{1,0:T(8,128)(2,1)S(1)}, u32[]{:S(2)}, u32[]{:S(2)}) %collective-permute-start.18) | collective-permute-done | bytes 262176 | tf_op jit(solution)/shard_map/ppermute | solution.py:182
  76.7 1.9 %collective-permute-start.19 = (bf16[512,128]{1,0:T(8,128)(2,1)S(1)}, bf16[512,128]{1,0:T(8,128)(2,1)S(1)}, u32[]{:S(2)}, u32[]{:S(2)}) collective-permute-start(bf16[512,128]{1,0:T(8,128)(2,1)S(1)} %slice.6), channel_id=1, source_target_pairs={{48,64},{64,80},{80,96},{49,65},{65,81},{81,97},{50,66},{66,82},{8... | collective-permute-start | bytes 393224 | tf_op jit(solution)/shard_map/ppermute | solution.py:182
  78.7 3.9 %collective-permute-start.20 = (bf16[512,128]{1,0:T(8,128)(2,1)S(1)}, bf16[512,128]{1,0:T(8,128)(2,1)S(1)}, u32[]{:S(2)}, u32[]{:S(2)}) collective-permute-start(bf16[512,128]{1,0:T(8,128)(2,1)S(1)} %slice.7), channel_id=1, source_target_pairs={{80,64},{96,80},{112,96},{81,65},{97,81},{113,97},{82,66},{98,82},... | collective-permute-start | bytes 393224 | tf_op jit(solution)/shard_map/ppermute | solution.py:182
  82.6 3.3 %attend.9 = (f32[2,512,128]{2,1,0:T(8,128)S(1)}, f32[2,512,128]{2,1,0:T(8,128)S(1)}, f32[2,512,128]{2,1,0:T(8,128)S(1)}) custom-call(s32[2]{0:T(128)S(1)} %pad_add_fusion.refs_0_, bf16[512,256]{1,0:T(8,128)(2,1)S(1)} %project_q.1.refs_1_, s32[512,128]{1,0:T(8,128)S(1)} %broadcast_in_dim.7.refs_2_, s32[512,128]{1,0:T(8,128)S(1)} %broadcast_in_dim.8.refs_3_, ...), custom_call_target="tpu_custom_call" | custom-call | flops 1600000000 | bytes 3000000 | tf_op jit(solution)/shard_map/attend/pallas_call | solution.py:300
  89.3 3.4 %project_out.1 = (bf16[128,1792]{1,0:T(8,128)(2,1)S(1)}, bf16[128,1792]{1,0:T(8,128)(2,1)S(1)}, bf16[128,1792]{1,0:T(8,128)(2,1)S(1)}, bf16[128,1792]{1,0:T(8,12...) custom-call(bf16[256,256]{1,0:T(8,128)(2,1)S(1)} %attend.10.mine_ref, ...), custom_call_target="tpu_custom_call" | custom-call | flops 1409286144 | bytes 8500000 | tf_op jit(solution)/shard_map/project_out/pallas_call | solution.py:376
  93.3 2.0 %collective-permute-start.24 = (bf16[128,1792]{1,0:T(8,128)(2,1)S(1)}, bf16[128,1792]{1,0:T(8,128)(2,1)S(1)}, u32[]{:S(2)}, u32[]{:S(2)}) collective-permute-start(bf16[128,1792]{1,0:T(8,128)(2,1)S(1)} %get-tuple-element.129), channel_id=1, source_target_pairs={{0,6},{1,7},{2,4},{3,5},{4,2},{5,3},{6,0},{7,1},{8,14},{9,15},{10,... | collective-permute-start | bytes 1376264 | tf_op jit(solution)/shard_map/ppermute | solution.py:40
  96.9 8.8 %collective-permute-done.23.refs_3_ = bf16[128,1792]{1,0:T(8,128)(2,1)S(1)} collective-permute-done((bf16[128,1792]{1,0:T(8,128)(2,1)S(1)}, bf16[128,1792]{1,0:T(8,128)(2,1)S(1)}, u32[]{:S(2)}, u32[]{:S(2)}) %collective-permute-start.23) | collective-permute-done | bytes 458784 | tf_op jit(solution)/shard_map/ppermute | solution.py:40
  111.2 4.7 %collective-permute-done.26.refs_3_ = bf16[64,1792]{1,0:T(8,128)(2,1)S(1)} collective-permute-done((bf16[64,1792]{1,0:T(8,128)(2,1)S(1)}, bf16[64,1792]{1,0:T(8,128)(2,1)S(1)}, u32[]{:S(2)}, u32[]{:S(2)}) %collective-permute-start.26) | collective-permute-done | bytes 229408 | tf_op jit(solution)/shard_map/ppermute | solution.py:40
  119.9 2.6 %collective-permute-done.29.refs_3_ = bf16[32,1792]{1,0:T(8,128)(2,1)S(1)} collective-permute-done((bf16[32,1792]{1,0:T(8,128)(2,1)S(1)}, bf16[32,1792]{1,0:T(8,128)(2,1)S(1)}, u32[]{:S(2)}, u32[]{:S(2)}) %collective-permute-start.29) | collective-permute-done | bytes 114720 | tf_op jit(solution)/shard_map/ppermute | solution.py:40
  (93 shorter events, 44.6 us)
Async XLA Ops:
  3.5 6.0 %collective-permute-start.1 = (bf16[32,1792]{1,0:T(8,128)(2,1)S(1)}, bf16[32,1792]{1,0:T(8,128)(2,1)S(1)}, u32[]{:S(2)}, u32[]{:S(2)}) collective-permute-start(bf16[32,1792]{1,0:T(8,128)(2,1)S(1)} %get-tuple-element.75.refs_1_), channel_id=1, source_target_pairs={{0,6},{1,7},{2,4},{3,5},{4,2},{5,3},{6,0},{7,1},{8,14},{9,15},{10,... | collective-permute-start | bytes 344072 | tf_op jit(solution)/shard_map/ppermute | solution.py:40
  7.2 82.1 %collective-permute-start.22 = (bf16[256,5376]{1,0:T(8,128)(2,1)}, bf16[256,5376]{1,0:T(8,128)(2,1)}, u32[]{:S(2)}, u32[]{:S(2)}) collective-permute-start(bf16[256,5376]{1,0:T(8,128)(2,1)} %w_mine.1), channel_id=1, source_target_pairs={{0,1},{1,0},{2,3},{3,2},{4,5},{5,4},{6,7},{7,6},{8,9},{9,8},{10,11... | collective-permute-start | bytes 8257544 | tf_op jit(solution)/shard_map/ppermute | solution.py:40
  10.5 7.3 %collective-permute-start.3 = (bf16[64,1792]{1,0:T(8,128)(2,1)S(1)}, bf16[64,1792]{1,0:T(8,128)(2,1)S(1)}, u32[]{:S(2)}, u32[]{:S(2)}) collective-permute-start(bf16[64,1792]{1,0:T(8,128)(2,1)S(1)} %get-tuple-element.77.refs_0_), channel_id=1, source_target_pairs={{0,6},{1,7},{2,4},{3,5},{4,2},{5,3},{6,0},{7,1},{8,14},{9,15},{10,... | collective-permute-start | bytes 688136 | tf_op jit(solution)/shard_map/ppermute | solution.py:40
  11.8 6.0 %collective-permute-start.4 = (bf16[64,1792]{1,0:T(8,128)(2,1)S(1)}, bf16[64,1792]{1,0:T(8,128)(2,1)S(1)}, u32[]{:S(2)}, u32[]{:S(2)}) collective-permute-start(bf16[64,1792]{1,0:T(8,128)(2,1)S(1)} %get-tuple-element.78.refs_1_), channel_id=1, source_target_pairs={{0,8},{1,9},{2,10},{3,11},{4,12},{5,13},{6,14},{7,15},{8,0},{9,1},... | collective-permute-start | bytes 688136 | tf_op jit(solution)/shard_map/ppermute | solution.py:40
  13.3 6.0 %collective-permute-start.5 = (bf16[64,1792]{1,0:T(8,128)(2,1)S(1)}, bf16[64,1792]{1,0:T(8,128)(2,1)S(1)}, u32[]{:S(2)}, u32[]{:S(2)}) collective-permute-start(bf16[64,1792]{1,0:T(8,128)(2,1)S(1)} %get-tuple-element.79.refs_2_), channel_id=1, source_target_pairs={{0,2},{1,3},{2,0},{3,1},{4,6},{5,7},{6,4},{7,5},{8,10},{9,11},{10,... | collective-permute-start | bytes 688136 | tf_op jit(solution)/shard_map/ppermute | solution.py:40
  20.6 19.8 %collective-permute-start.9 = (bf16[3,128,1792]{2,1,0:T(8,128)(2,1)}, bf16[3,128,1792]{2,1,0:T(8,128)(2,1)S(1)}, u32[]{:S(2)}, u32[]{:S(2)}) collective-permute-start(bf16[3,128,1792]{2,1,0:T(8,128)(2,1)} %get-tuple-element.87), channel_id=1, source_target_pairs={{0,1},{1,0},{2,3},{3,2},{4,5},{5,4},{6,7},{7,6},{8,9},{9,8},{10,11... | collective-permute-start | bytes 4128776 | tf_op jit(solution)/shard_map/ppermute | solution.py:40
  22.5 13.0 %collective-permute-start.6 = (bf16[128,1792]{1,0:T(8,128)(2,1)S(1)}, bf16[128,1792]{1,0:T(8,128)(2,1)S(1)}, u32[]{:S(2)}, u32[]{:S(2)}) collective-permute-start(bf16[128,1792]{1,0:T(8,128)(2,1)S(1)} %get-tuple-element.80.refs_0_), channel_id=1, source_target_pairs={{0,8},{1,9},{2,10},{3,11},{4,12},{5,13},{6,14},{7,15},{8,0},{9,1},... | collective-permute-start | bytes 1376264 | tf_op jit(solution)/shard_map/ppermute | solution.py:40
  23.1 12.6 %collective-permute-start.7 = (bf16[128,1792]{1,0:T(8,128)(2,1)S(1)}, bf16[128,1792]{1,0:T(8,128)(2,1)S(1)}, u32[]{:S(2)}, u32[]{:S(2)}) collective-permute-start(bf16[128,1792]{1,0:T(8,128)(2,1)S(1)} %get-tuple-element.81.refs_1_), channel_id=1, source_target_pairs={{0,2},{1,3},{2,0},{3,1},{4,6},{5,7},{6,4},{7,5},{8,10},{9,11},{10,... | collective-permute-start | bytes 1376264 | tf_op jit(solution)/shard_map/ppermute | solution.py:40
  23.1 13.8 %collective-permute-start.8 = (bf16[128,1792]{1,0:T(8,128)(2,1)S(1)}, bf16[128,1792]{1,0:T(8,128)(2,1)S(1)}, u32[]{:S(2)}, u32[]{:S(2)}) collective-permute-start(bf16[128,1792]{1,0:T(8,128)(2,1)S(1)} %get-tuple-element.82.refs_2_), channel_id=1, source_target_pairs={{0,6},{1,7},{2,4},{3,5},{4,2},{5,3},{6,0},{7,1},{8,14},{9,15},{10,... | collective-permute-start | bytes 1376264 | tf_op jit(solution)/shard_map/ppermute | solution.py:40
  43.8 10.2 %collective-permute-start.13 = (bf16[512,256]{1,0:T(8,128)(2,1)S(1)}, bf16[512,256]{1,0:T(8,128)(2,1)S(1)}, u32[]{:S(2)}, u32[]{:S(2)}) collective-permute-start(bf16[512,256]{1,0:T(8,128)(2,1)S(1)} %project_kv.1.refs_5_), channel_id=1, source_target_pairs={{0,16},{16,32},{32,48},{48,64},{64,80},{80,96},{1,17},{17,33},{33,... | collective-permute-start | bytes 786440 | tf_op jit(solution)/shard_map/ppermute | solution.py:182
  46.7 7.3 %collective-permute-start.14 = (bf16[512,256]{1,0:T(8,128)(2,1)S(1)}, bf16[512,256]{1,0:T(8,128)(2,1)S(1)}, u32[]{:S(2)}, u32[]{:S(2)}) collective-permute-start(bf16[512,256]{1,0:T(8,128)(2,1)S(1)} %project_kv.1.refs_5_), channel_id=1, source_target_pairs={{0,112},{16,0},{32,16},{1,113},{17,1},{33,17},{2,114},{18,2},{34,1... | collective-permute-start | bytes 786440 | tf_op jit(solution)/shard_map/ppermute | solution.py:182
  54.0 9.9 %collective-permute-start.15 = (bf16[512,256]{1,0:T(8,128)(2,1)S(1)}, bf16[512,256]{1,0:T(8,128)(2,1)S(1)}, u32[]{:S(2)}, u32[]{:S(2)}) collective-permute-start(bf16[512,256]{1,0:T(8,128)(2,1)S(1)} %collective-permute-done.13.refs_5_), channel_id=1, source_target_pairs={{16,32},{32,48},{48,64},{64,80},{80,96},{17,33},{33,49},{49,65},{6... | collective-permute-start | bytes 786440 | tf_op jit(solution)/shard_map/ppermute | solution.py:182
  56.9 7.0 %collective-permute-start.16 = (bf16[512,256]{1,0:T(8,128)(2,1)S(1)}, bf16[512,256]{1,0:T(8,128)(2,1)S(1)}, u32[]{:S(2)}, u32[]{:S(2)}) collective-permute-start(bf16[512,256]{1,0:T(8,128)(2,1)S(1)} %collective-permute-done.14), channel_id=1, source_target_pairs={{112,96},{0,112},{16,0},{113,97},{1,113},{17,1},{114,98},{2,114},{... | collective-permute-start | bytes 786440 | tf_op jit(solution)/shard_map/ppermute | solution.py:182
  63.9 9.7 %collective-permute-start.17 = (bf16[512,256]{1,0:T(8,128)(2,1)S(1)}, bf16[512,256]{1,0:T(8,128)(2,1)S(1)}, u32[]{:S(2)}, u32[]{:S(2)}) collective-permute-start(bf16[512,256]{1,0:T(8,128)(2,1)S(1)} %collective-permute-done.15.refs_5_), channel_id=1, source_target_pairs={{32,48},{48,64},{64,80},{80,96},{33,49},{49,65},{65,81},{81,97},{3... | collective-permute-start | bytes 786440 | tf_op jit(solution)/shard_map/ppermute | solution.py:182
  68.2 8.5 %collective-permute-start.18 = (bf16[512,256]{1,0:T(8,128)(2,1)S(1)}, bf16[512,256]{1,0:T(8,128)(2,1)S(1)}, u32[]{:S(2)}, u32[]{:S(2)}) collective-permute-start(bf16[512,256]{1,0:T(8,128)(2,1)S(1)} %collective-permute-done.16.refs_6_), channel_id=1, source_target_pairs={{96,80},{112,96},{0,112},{97,81},{113,97},{1,113},{98,82},{114,98}... | collective-permute-start | bytes 786440 | tf_op jit(solution)/shard_map/ppermute | solution.py:182
  76.7 9.2 %collective-permute-start.19 = (bf16[512,128]{1,0:T(8,128)(2,1)S(1)}, bf16[512,128]{1,0:T(8,128)(2,1)S(1)}, u32[]{:S(2)}, u32[]{:S(2)}) collective-permute-start(bf16[512,128]{1,0:T(8,128)(2,1)S(1)} %slice.6), channel_id=1, source_target_pairs={{48,64},{64,80},{80,96},{49,65},{65,81},{81,97},{50,66},{66,82},{8... | collective-permute-start | bytes 393224 | tf_op jit(solution)/shard_map/ppermute | solution.py:182
  78.7 7.3 %collective-permute-start.20 = (bf16[512,128]{1,0:T(8,128)(2,1)S(1)}, bf16[512,128]{1,0:T(8,128)(2,1)S(1)}, u32[]{:S(2)}, u32[]{:S(2)}) collective-permute-start(bf16[512,128]{1,0:T(8,128)(2,1)S(1)} %slice.7), channel_id=1, source_target_pairs={{80,64},{96,80},{112,96},{81,65},{97,81},{113,97},{82,66},{98,82},... | collective-permute-start | bytes 393224 | tf_op jit(solution)/shard_map/ppermute | solution.py:182
  92.7 13.0 %collective-permute-start.23 = (bf16[128,1792]{1,0:T(8,128)(2,1)S(1)}, bf16[128,1792]{1,0:T(8,128)(2,1)S(1)}, u32[]{:S(2)}, u32[]{:S(2)}) collective-permute-start(bf16[128,1792]{1,0:T(8,128)(2,1)S(1)} %get-tuple-element.128), channel_id=1, source_target_pairs={{0,2},{1,3},{2,0},{3,1},{4,6},{5,7},{6,4},{7,5},{8,10},{9,11},{10,... | collective-permute-start | bytes 1376264 | tf_op jit(solution)/shard_map/ppermute | solution.py:40
  93.3 13.8 %collective-permute-start.24 = (bf16[128,1792]{1,0:T(8,128)(2,1)S(1)}, bf16[128,1792]{1,0:T(8,128)(2,1)S(1)}, u32[]{:S(2)}, u32[]{:S(2)}) collective-permute-start(bf16[128,1792]{1,0:T(8,128)(2,1)S(1)} %get-tuple-element.129), channel_id=1, source_target_pairs={{0,6},{1,7},{2,4},{3,5},{4,2},{5,3},{6,0},{7,1},{8,14},{9,15},{10,... | collective-permute-start | bytes 1376264 | tf_op jit(solution)/shard_map/ppermute | solution.py:40
  95.3 12.4 %collective-permute-start.25 = (bf16[128,1792]{1,0:T(8,128)(2,1)S(1)}, bf16[128,1792]{1,0:T(8,128)(2,1)S(1)}, u32[]{:S(2)}, u32[]{:S(2)}) collective-permute-start(bf16[128,1792]{1,0:T(8,128)(2,1)S(1)} %get-tuple-element.130), channel_id=1, source_target_pairs={{0,8},{1,9},{2,10},{3,11},{4,12},{5,13},{6,14},{7,15},{8,0},{9,1},... | collective-permute-start | bytes 1376264 | tf_op jit(solution)/shard_map/ppermute | solution.py:40
  108.0 7.9 %collective-permute-start.26 = (bf16[64,1792]{1,0:T(8,128)(2,1)S(1)}, bf16[64,1792]{1,0:T(8,128)(2,1)S(1)}, u32[]{:S(2)}, u32[]{:S(2)}) collective-permute-start(bf16[64,1792]{1,0:T(8,128)(2,1)S(1)} %get-tuple-element.134), channel_id=1, source_target_pairs={{0,6},{1,7},{2,4},{3,5},{4,2},{5,3},{6,0},{7,1},{8,14},{9,15},{10,... | collective-permute-start | bytes 688136 | tf_op jit(solution)/shard_map/ppermute | solution.py:40
  109.6 6.6 %collective-permute-start.27 = (bf16[64,1792]{1,0:T(8,128)(2,1)S(1)}, bf16[64,1792]{1,0:T(8,128)(2,1)S(1)}, u32[]{:S(2)}, u32[]{:S(2)}) collective-permute-start(bf16[64,1792]{1,0:T(8,128)(2,1)S(1)} %get-tuple-element.135), channel_id=1, source_target_pairs={{0,8},{1,9},{2,10},{3,11},{4,12},{5,13},{6,14},{7,15},{8,0},{9,1},... | collective-permute-start | bytes 688136 | tf_op jit(solution)/shard_map/ppermute | solution.py:40
  111.2 6.3 %collective-permute-start.28 = (bf16[64,1792]{1,0:T(8,128)(2,1)S(1)}, bf16[64,1792]{1,0:T(8,128)(2,1)S(1)}, u32[]{:S(2)}, u32[]{:S(2)}) collective-permute-start(bf16[64,1792]{1,0:T(8,128)(2,1)S(1)} %get-tuple-element.136), channel_id=1, source_target_pairs={{0,2},{1,3},{2,0},{3,1},{4,6},{5,7},{6,4},{7,5},{8,10},{9,11},{10,... | collective-permute-start | bytes 688136 | tf_op jit(solution)/shard_map/ppermute | solution.py:40
  118.5 6.0 %collective-permute-start.31 = (bf16[32,1792]{1,0:T(8,128)(2,1)S(1)}, bf16[32,1792]{1,0:T(8,128)(2,1)S(1)}, u32[]{:S(2)}, u32[]{:S(2)}) collective-permute-start(bf16[32,1792]{1,0:T(8,128)(2,1)S(1)} %get-tuple-element.142), channel_id=1, source_target_pairs={{0,6},{1,7},{2,4},{3,5},{4,2},{5,3},{6,0},{7,1},{8,14},{9,15},{10,... | collective-permute-start | bytes 344072 | tf_op jit(solution)/shard_map/ppermute | solution.py:40
  (18 other events, 115.8 us)

commit v3 on v2

--- a/solution.py
+++ b/solution.py
@@ -3,6 +3,7 @@
 
 import jax
 import jax.numpy as jnp
+import numpy as np
 from jax import lax
 from jax.experimental import pallas as pl
 from jax.experimental.pallas import tpu as pltpu
@@ -38,6 +39,14 @@
 
 def swap(value, link):
     return lax.ppermute(value, "mp", [(m, m ^ link) for m in range(16)])
+
+
+def swap_y_both_ways(value):
+    return lax.ppermute(
+        value,
+        ("docs", "mp"),
+        [(d * 16 + m, (d ^ (m & 1)) * 16 + (m ^ YY)) for d in range(2) for m in range(16)],
+    )
 
 
 def whole(count):
@@ -78,6 +87,71 @@
     )(residual, gain.reshape(D // HD, HD))
 
 
+def tables_kernel(
+    starts_ref, first_ref, frequency_ref, cos_ref, sin_ref, position_ref, start_ref, offset_ref, where_ref, natural
+):
+    mine = lax.axis_index("mp")
+    block = lax.axis_index("ctx")
+    row = lax.broadcasted_iota(jnp.int32, (HD, HD), 0)
+    lane = lax.broadcasted_iota(jnp.int32, (HD, HD), 1)
+    for k in range(BLOCK // HD):
+        spread = jnp.broadcast_to(starts_ref[k : k + 1].astype(jnp.float32), (HD, HD))
+        column = jnp.sum(jnp.where(row == lane, spread, 0.0), axis=-1, keepdims=True)
+        natural[k * HD : (k + 1) * HD] = jnp.broadcast_to(column, (HD, HD)).astype(jnp.int32)
+    inner = lax.broadcasted_iota(jnp.int32, (ROWS, HD), 0)
+    along = lax.broadcasted_iota(jnp.int32, (1, BLOCK), 1)
+    offset = along
+    sign = jnp.where(
+        lax.broadcasted_iota(jnp.int32, (ROWS, HD), 1) < HD // 2, -1.0, 1.0
+    )
+    for k in range(16):
+        owner = mine ^ (mp_mask(k & 7) ^ (k >> 3))
+        here = slice(k * ROWS, (k + 1) * ROWS)
+        start = natural[pl.ds(pl.multiple_of(owner * ROWS, ROWS), ROWS)]
+        position = inner + (block * BLOCK + owner * ROWS)
+        start_ref[here] = start
+        position_ref[here] = position
+        angles = ((position - start).astype(jnp.float32) / rope_factor) * frequency_ref[...]
+        cos_ref[here] = jnp.cos(angles)
+        sin_ref[here] = jnp.sin(angles) * sign
+        inside = (along >= k * ROWS) & (along < (k + 1) * ROWS)
+        offset = jnp.where(inside, along + (owner - k) * ROWS, offset)
+    offset_ref[...] = offset
+    where_ref[0] = block
+    where_ref[1] = block - (first_ref[0] >> 9) + 1
+
+
+def make_tables(document_start):
+    frequency = np.float32(rope_base) ** (
+        -(np.arange(HD // 2, dtype=np.float32) * np.float32(2.0) / np.float32(HD))
+    )
+    frequency = jnp.asarray(np.concatenate([frequency, frequency])[None, :], jnp.float32)
+    wide = lambda kind: jax.ShapeDtypeStruct((BLOCK, HD), kind)
+    return pl.pallas_call(
+        tables_kernel,
+        out_shape=[
+            wide(jnp.float32),
+            wide(jnp.float32),
+            wide(jnp.int32),
+            wide(jnp.int32),
+            jax.ShapeDtypeStruct((1, BLOCK), jnp.int32),
+            jax.ShapeDtypeStruct((2,), jnp.int32),
+        ],
+        in_specs=[
+            pl.BlockSpec(memory_space=pltpu.VMEM),
+            pl.BlockSpec(memory_space=pltpu.SMEM),
+            pl.BlockSpec(memory_space=pltpu.VMEM),
+        ],
+        out_specs=whole(5) + [pl.BlockSpec(memory_space=pltpu.SMEM)],
+        scratch_shapes=[pltpu.VMEM((BLOCK, HD), jnp.int32)],
+        compiler_params=params(4),
+        cost_estimate=pl.CostEstimate(
+            flops=4000000, bytes_accessed=1000000, transcendentals=131072
+        ),
+        name="tables",
+    )(document_start.reshape(BLOCK // HD, HD), document_start, frequency)
+
+
 def join_kernel(extra, *refs):
     held, came, outs = refs[0:3], refs[3:6], refs[6:]
     for part in range(3):
@@ -104,18 +178,21 @@
     )(*held, *came)
 
 
-def gather_tokens(thirds, tables):
+def gather_tokens(thirds, document_start, core_weight):
     came = [swap(thirds[p], ORDERS[p][0]) for p in range(3)]
     two = join(thirds, came, False)
     came = [swap(two[p], ORDERS[p][1]) for p in range(3)]
+    *came, document_start = lax.optimization_barrier((*came, document_start))
     *four, packed = join(two, came, True)
     late = [swap(four[p], ORDERS[p][2]) for p in range(3)]
     other = swap(packed, CC)
-    *late, cosine, sine, where, position, start, offset = lax.optimization_barrier(
-        (*late, *tables)
-    )
+    tables = make_tables(document_start)
+    *late, cosine, sine, position, start, offset, where, core_weight = lax.optimization_barrier(
+        (*late, *tables, core_weight)
+    )
+    both_weight = swap_y_both_ways(core_weight)
     other_late = [swap(late[p], CC) for p in range(3)]
-    return (four, late, other, other_late), cosine, sine, where, position, start, offset
+    return (four, late, other, other_late), cosine, sine, where, position, start, offset, core_weight, both_weight
 
 
 def rotate(raw, gain, cosine, sine):
@@ -166,7 +243,7 @@
         out_shape=shape(BLOCK, 2 * HD),
         in_specs=whole(13 + len(weights)),
         out_specs=whole(1)[0],
-        compiler_params=params(18),
+        compiler_params=params(14),
         cost_estimate=pl.CostEstimate(
             flops=2 * BLOCK * D * 2 * HD, bytes_accessed=9000000, transcendentals=0
         ),
@@ -178,8 +255,8 @@
 TILE = 256
 
 
-def move(value, pairs):
-    return lax.ppermute(value, "ctx", pairs)
+def move(value, step):
+    return lax.ppermute(value, "ctx", [(c, (c + step) % 8) for c in range(8)])
 
 
 def attend_kernel(distances, joint, first, last, *refs):
@@ -189,7 +266,7 @@
     if not first:
         old_state, refs = refs[0:3], refs[3:]
     if last:
-        out_ref, state = refs[0], refs[1:4]
+        out_refs, state = refs[0:2], refs[2:5]
     else:
         state = refs[0:3]
     top, total, acc = state
@@ -271,10 +348,12 @@
         source = state
     if last:
         for head in range(2):
-            denominator = jnp.sum(total[head], axis=-1, keepdims=True)
-            out_ref[:, head * HD : (head + 1) * HD] = (acc[head] / denominator).astype(
-                jnp.bfloat16
-            )
+            for quarter in range(2):
+                here = slice(quarter * 128, (quarter + 1) * 128)
+                denominator = jnp.sum(total[head, here], axis=-1, keepdims=True)
+                out_refs[quarter][:, head * HD : (head + 1) * HD] = (
+                    acc[head, here] / denominator
+                ).astype(jnp.bfloat16)
 
 
 def attend(tables, query, distances, joint, blocks, state, last, half=None):
@@ -284,7 +363,7 @@
     rows_here = BLOCK // 2 if last else BLOCK
     state_shape = jax.ShapeDtypeStruct((2, rows_here, HD), jnp.float32)
     if last:
-        out_shape, out_specs = shape(rows_here, 2 * HD), whole(1)[0]
+        out_shape, out_specs = [shape(128, 2 * HD)] * 2, whole(2)
         scratch = [pltpu.VMEM((2, rows_here, HD), jnp.float32)] * 3
         row_specs = [
             pl.BlockSpec((rows_here, 2 * HD), lambda k: (half, 0)),
@@ -307,7 +386,7 @@
         + (state_specs if state else []),
         out_specs=out_specs,
         scratch_shapes=scratch,
-        compiler_params=params(12),
+        compiler_params=params(10),
         cost_estimate=pl.CostEstimate(
             flops=800000000 * len(distances), bytes_accessed=3000000, transcendentals=1000000
         ),
@@ -315,119 +394,117 @@
     )(where, query, position, start, offset, *blocks, *state)
 
 
-def share_and_attend(rows, make_query, tables):
+def halves_kernel(keys_ref, values_ref, key_out, value_out):
+    key_out[...] = keys_ref[:, 0:HD]
+    value_out[...] = values_ref[:, HD : 2 * HD]
+
+
+def take_halves(keys, values):
+    return pl.pallas_call(
+        halves_kernel,
+        out_shape=[shape(BLOCK, HD)] * 2,
+        in_specs=whole(2),
+        out_specs=whole(2),
+        compiler_params=params(4),
+        name="take_halves",
+    )(keys, values)
+
+
+def share_and_attend(rows, make_query, tables, output_weight, core_weight, both_weight):
     tie = lax.optimization_barrier
-    forward, backward = rows, rows
-
-    def onward(k, forward, backward):
-        return (
-            move(forward, [(c, c + 1) for c in range(k, 6)]),
-            move(backward, [((c - k) % 8, (c - k - 1) % 8) for c in range(3)]),
-        )
-
-    one, back_one = onward(0, rows, rows)
+
+    def onward(forward, backward):
+        return move(forward, 1), move(backward, -1)
+
+    one, back_one = onward(rows, rows)
     query = make_query()
     state = attend(tables, query, (0,), (1,), [rows], None, False)
     one, back_one, state = tie((one, back_one, state))
-    two, back_two = onward(1, one, back_one)
+    two, back_two = onward(one, back_one)
     state = attend(tables, query, (1,), (1,), [one], state, False)
     two, back_two, state = tie((two, back_two, state))
-    three, back_three = onward(2, two, back_two)
+    three, back_three = onward(two, back_two)
     state = attend(tables, query, (2, 6), (1, 1), [two, back_two], state, False)
-    three, back_three, state = tie((three, back_three, state))
-    key_far = move(three[:, :HD], [(3, 4), (4, 5), (5, 6)])
-    value_far = move(back_three[:, HD:], [(5, 4), (6, 5), (7, 6)])
+    three, back_three, state, both_weight = tie((three, back_three, state, both_weight))
+    y_weight = swap(both_weight, CC)
+    key_half, value_half = take_halves(three, back_three)
+    key_far = move(key_half, 1)
+    value_far = move(value_half, -1)
     state = attend(tables, query, (3, 5), (1, 1), [three, back_three], state, False)
     key_far, value_far, state = tie((key_far, value_far, state))
-    goes = attend(tables, query, (4,), (0, 2), [key_far, value_far], state, True, 1)
-    stays = attend(tables, query, (4,), (0, 2), [key_far, value_far], state, True, 0)
-    return stays, swap(goes, CC)
-
-
-CHUNK = 256
-
-
-def output_kernel(mine_ref, theirs_ref, w_mine, w_theirs, *outs):
-    def groups(weight_columns):
-        return jnp.dot(mine_ref[...], w_mine[:, weight_columns], preferred_element_type=jnp.float32).astype(
-            jnp.bfloat16
-        ).astype(jnp.float32) + jnp.dot(
-            theirs_ref[...], w_theirs[:, weight_columns], preferred_element_type=jnp.float32
-        ).astype(jnp.bfloat16).astype(jnp.float32)
-
-    for part in range(3):
-        bit = BITS[ORDERS[part][0]]
-        for chunk in range(THIRD // CHUNK):
-            summed = groups(
-                slice(part * THIRD + chunk * CHUNK, part * THIRD + (chunk + 1) * CHUNK)
-            ).astype(jnp.bfloat16)
-            here = slice(chunk * CHUNK, (chunk + 1) * CHUNK)
-            counts = [0, 0]
-            for place in range(8):
-                goes = 1 if place & bit else 0
-                at = counts[goes] * ROWS
-                counts[goes] += 1
-                outs[2 * part + goes][at : at + ROWS, here] = summed[
-                    place * ROWS : (place + 1) * ROWS
-                ]
-
-
-def project_out(mine, theirs, w_mine, w_theirs):
-    return pl.pallas_call(
-        output_kernel,
-        out_shape=[shape(128, THIRD)] * 6,
-        in_specs=whole(4),
-        out_specs=whole(6),
-        compiler_params=params(24),
+    to_core, to_both = attend(tables, query, (4,), (0, 2), [key_far, value_far], state, True, 1)
+    mine, to_y = attend(tables, query, (4,), (0, 2), [key_far, value_far], state, True, 0)
+    parts = [mine, swap(to_core, CC), swap(to_y, YY), swap(to_both, CC ^ YY)]
+    return parts, [output_weight, core_weight, y_weight, both_weight]
+
+
+HALF = D // 2
+CHUNK = 384
+X_ORDERS = ((XA, XB), (XB, XA))
+
+
+def output_kernel(part, *refs):
+    rows, weights, keeps, goes = refs[0:4], refs[4:8], refs[8], refs[9]
+    for chunk in range(HALF // CHUNK):
+        here = slice(part * HALF + chunk * CHUNK, part * HALF + (chunk + 1) * CHUNK)
+        summed = jnp.zeros((128, CHUNK), jnp.float32)
+        for row, weight in zip(rows, weights):
+            group = jnp.dot(row[...], weight[:, here], preferred_element_type=jnp.float32)
+            summed = summed + group.astype(jnp.bfloat16).astype(jnp.float32)
+        summed = summed.astype(jnp.bfloat16)
+        to = slice(chunk * CHUNK, (chunk + 1) * CHUNK)
+        bit = BITS[X_ORDERS[part][0]]
+        for place in range(4):
+            out = goes if place & bit else keeps
+            at = (place >> 1 if bit == 1 else place & 1) * ROWS
+            out[at : at + ROWS, to] = summed[place * ROWS : (place + 1) * ROWS]
+
+
+def project_out(part, rows, weights):
+    return pl.pallas_call(
+        functools.partial(output_kernel, part),
+        out_shape=[shape(64, HALF)] * 2,
+        in_specs=whole(8),
+        out_specs=whole(2),
+        compiler_params=params(16),
         cost_estimate=pl.CostEstimate(
-            flops=4 * 256 * 256 * D, bytes_accessed=8500000, transcendentals=0
+            flops=2 * 128 * 1024 * HALF, bytes_accessed=6500000, transcendentals=0
         ),
         name="project_out",
-    )(mine, theirs, w_mine, w_theirs)
-
-
-def remaining(part, level):
-    return sorted(BITS[link] for link in ORDERS[part][level:])
-
-
-def fold_kernel(level, *refs):
-    kept, came, outs = refs[0:3], refs[3:6], refs[6:]
-    for part in range(3):
-        bits = remaining(part, level)
-        goes_bit = bits.index(BITS[ORDERS[part][level]])
+    )(*rows, *weights)
+
+
+def fold_kernel(*refs):
+    kept, came, outs = refs[0:2], refs[2:4], refs[4:]
+    for part in range(2):
         summed = (
             kept[part][...].astype(jnp.float32) + came[part][...].astype(jnp.float32)
         ).astype(jnp.bfloat16)
-        counts = [0, 0]
-        for k in range(1 << len(bits)):
-            goes = (k >> goes_bit) & 1
-            at = counts[goes] * ROWS
-            counts[goes] += 1
-            outs[2 * part + goes][at : at + ROWS] = summed[k * ROWS : (k + 1) * ROWS]
-
-
-def fold(kept, came, level):
-    rows = kept[0].shape[0] // 2
-    return pl.pallas_call(
-        functools.partial(fold_kernel, level),
-        out_shape=[shape(rows, THIRD)] * 6,
-        in_specs=whole(6),
-        out_specs=whole(6),
-        compiler_params=params(12),
+        outs[2 * part][...] = summed[0:ROWS]
+        outs[2 * part + 1][...] = summed[ROWS : 2 * ROWS]
+
+
+def fold(kept, came):
+    return pl.pallas_call(
+        fold_kernel,
+        out_shape=[shape(ROWS, HALF)] * 4,
+        in_specs=whole(4),
+        out_specs=whole(4),
+        compiler_params=params(8),
         name="fold_rows",
     )(*kept, *came)
 
 
 def finish_kernel(residual_ref, gain_ref, *refs):
-    kept, came, out, sums = refs[0:3], refs[3:6], refs[6], refs[7]
+    kept, came, out, sums = refs[0:2], refs[2:4], refs[4], refs[5]
     square = jnp.zeros((ROWS, HD), jnp.float32)
-    for part in range(3):
-        for k in range(THIRD // HD):
+    for part in range(2):
+        for k in range(HALF // HD):
             here = slice(k * HD, (k + 1) * HD)
             summed = kept[part][:, here].astype(jnp.float32) + came[part][:, here].astype(
                 jnp.float32
             )
-            at = part * THIRD + k * HD
+            at = part * HALF + k * HD
             sums[:, at : at + HD] = summed
             square = square + summed * summed
     inverse = lax.rsqrt(jnp.sum(square, axis=-1, keepdims=True) / D + epsilon)
@@ -443,7 +520,7 @@
     return pl.pallas_call(
         finish_kernel,
         out_shape=shape(ROWS, D),
-        in_specs=whole(8),
+        in_specs=whole(6),
         out_specs=whole(1)[0],
         scratch_shapes=[pltpu.VMEM((ROWS, D), jnp.float32)],
         compiler_params=params(6),
@@ -451,14 +528,15 @@
     )(residual, gain.reshape(D // HD, HD), *kept, *came)
 
 
-def reduce_tokens(halves):
-    kept, goes = halves[0::2], halves[1::2]
-    for level in range(3):
-        came = [swap(goes[p], ORDERS[p][level]) for p in range(3)]
-        if level == 2:
-            return kept, came
-        halves = fold(kept, came, level + 1)
-        kept, goes = halves[0::2], halves[1::2]
+def reduce_tokens(rows, weights):
+    kept, came = [], []
+    for part in range(2):
+        keeps, goes = project_out(part, rows, weights)
+        kept.append(keeps)
+        came.append(swap(goes, X_ORDERS[part][0]))
+    halves = fold(kept, came)
+    came = [swap(halves[2 * part + 1], X_ORDERS[part][1]) for part in range(2)]
+    return halves[0::2], came
 
 
 def body(
@@ -475,37 +553,22 @@
 ):
     thirds = norm_rows(residual_in, input_gain)
 
-    block = lax.axis_index("ctx")
-    mine = lax.axis_index("mp")
-    masks = jnp.array([mp_mask(k & 7) ^ (k >> 3) for k in range(16)], jnp.int32)
-    owners = mine ^ masks
-    inside = (owners[:, None] * ROWS + jnp.arange(ROWS, dtype=jnp.int32)[None, :]).reshape(BLOCK)
-    position = block * BLOCK + inside
-    start = document_start.reshape(16, ROWS)[owners].reshape(BLOCK)
-    frequency = rope_base ** (-(jnp.arange(HD // 2, dtype=jnp.float32) * 2.0 / HD))
-    angles = ((position - start).astype(jnp.float32) / rope_factor)[:, None] * frequency[None, :]
-    cosine = jnp.cos(angles)
-    sine = jnp.sin(angles)
-    cosine = jnp.concatenate([cosine, cosine], axis=1)
-    sine = jnp.concatenate([-sine, sine], axis=1)
-    live = block - jnp.min(document_start) // BLOCK + 1
-    where = jnp.stack([block, live]).astype(jnp.int32)
-    position_wide = jnp.broadcast_to(position[:, None], (BLOCK, HD))
-    start_wide = jnp.broadcast_to(start[:, None], (BLOCK, HD))
-
-    pieces, cosine, sine, where, position_wide, start_wide, offset = gather_tokens(
-        thirds, (cosine, sine, where, position_wide, start_wide, inside[None, :])
-    )
-    w_theirs = swap(output_weight, CC)
+    pieces, cosine, sine, where, position_wide, start_wide, offset, core_weight, both_weight = gather_tokens(
+        thirds,
+        document_start,
+        swap(output_weight, CC),
+    )
     tables = (where, position_wide, start_wide, offset)
     rows = project(pieces, [key_weight, value_weight], key_gain, cosine, sine, "project_kv")
-    mine, theirs = share_and_attend(
+    parts, weights = share_and_attend(
         rows,
         lambda: project(pieces, [query_weight], query_gain, cosine, sine, "project_q"),
         tables,
-    )
-    halves = project_out(mine, theirs, output_weight, w_theirs)
-    kept, came = reduce_tokens(halves)
+        output_weight,
+        core_weight,
+        both_weight,
+    )
+    kept, came = reduce_tokens(parts, weights)
     return finish(residual_in, post_gain, kept, came)
 
 

time: 127 us -> 111 us (0.87)
  the two profiles are of different devices: /device:TPU:160 before, /device:TPU:16 now
where the time goes in v3:
time: 111 us
  waiting for transfers between devices  56.3 us (51%)
  starting transfers between devices  33 us (30%)
  Pallas kernels  16 us (14%)
  local copies, waits for them, and re-layouts  5.17 us (5%)
    ppermute x22, waiting for transfers between devices, swap(): return lax.ppermute(value, 'mp', [(m, m ^ link) for m in range(16)])  38.4 us
    ppermute x8, waiting for transfers between devices, move(): return lax.ppermute(value, 'ctx', [(c, (c + step) % 8) for c in range(8)])  17.9 us
    ppermute x22, starting transfers between devices, swap(): return lax.ppermute(value, 'mp', [(m, m ^ link) for m in range(16)])  17.2 us
    ppermute x8, starting transfers between devices, move(): return lax.ppermute(value, 'ctx', [(c, (c + step) % 8) for c in range(8)])  14.6 us
    pallas_call x6, Pallas kernels, attend(): pl.pallas_call(functools.partial(attend_kernel, distances, joint, first,...  5.61 us
    unnamed x24, local copies, waits for them, and re-layouts  5.17 us
    pallas_call x2, Pallas kernels, project(): pl.pallas_call(functools.partial(project_kernel, len(weights)), out_shape...  4.36 us
    pallas_call x2, Pallas kernels, project_out(): pl.pallas_call(functools.partial(output_kernel, part), out_shape=[shape(6...  2.22 us
  transfers between devices with their start and end apart: 31, of which 25 were waited for; matrix products, arithmetic and copies ran while one was open for 0% of the time, Pallas kernels for 12%

profile of v3, /device:TPU:16, one launch (start us, length us, event | category | flops | bytes accessed | tf_op | source)
XLA Modules:
  0.0 110.7 jit_solution(14630308096217509256)
XLA Ops:
  2.1 1.6 %collective-permute-start = (bf16[32,1792]{1,0:T(8,128)(2,1)S(1)}, bf16[32,1792]{1,0:T(8,128)(2,1)S(1)}, u32[]{:S(2)}, u32[]{:S(2)}) collective-permute-start(bf16[32,1792]{1,0:T(8,128)(2,1)S(1)} %get-tuple-element.82.refs_0_), channel_id=1, source_target_pairs={{0,2},{1,3},{2,0},{3,1},{4,6},{5,7},{6,4},{7,5},{8,10},{9,11},{10,... | collective-permute-start | bytes 344072 | tf_op jit(solution)/shard_map/ppermute | solution.py:41
  3.6 2.1 %collective-permute-start.1 = (bf16[32,1792]{1,0:T(8,128)(2,1)S(1)}, bf16[32,1792]{1,0:T(8,128)(2,1)S(1)}, u32[]{:S(2)}, u32[]{:S(2)}) collective-permute-start(bf16[32,1792]{1,0:T(8,128)(2,1)S(1)} %get-tuple-element.83.refs_1_), channel_id=1, source_target_pairs={{0,6},{1,7},{2,4},{3,5},{4,2},{5,3},{6,0},{7,1},{8,14},{9,15},{10,... | collective-permute-start | bytes 344072 | tf_op jit(solution)/shard_map/ppermute | solution.py:41
  7.6 2.4 %collective-permute-done.1.refs_4_ = bf16[32,1792]{1,0:T(8,128)(2,1)S(1)} collective-permute-done((bf16[32,1792]{1,0:T(8,128)(2,1)S(1)}, bf16[32,1792]{1,0:T(8,128)(2,1)S(1)}, u32[]{:S(2)}, u32[]{:S(2)}) %collective-permute-start.1) | collective-permute-done | bytes 114720 | tf_op jit(solution)/shard_map/ppermute | solution.py:41
  10.7 1.6 %collective-permute-start.3 = (bf16[64,1792]{1,0:T(8,128)(2,1)S(1)}, bf16[64,1792]{1,0:T(8,128)(2,1)S(1)}, u32[]{:S(2)}, u32[]{:S(2)}) collective-permute-start(bf16[64,1792]{1,0:T(8,128)(2,1)S(1)} %get-tuple-element.85.refs_0_), channel_id=1, source_target_pairs={{0,6},{1,7},{2,4},{3,5},{4,2},{5,3},{6,0},{7,1},{8,14},{9,15},{10,... | collective-permute-start | bytes 688136 | tf_op jit(solution)/shard_map/ppermute | solution.py:41
  13.6 4.9 %collective-permute-done.3.refs_3_ = bf16[64,1792]{1,0:T(8,128)(2,1)S(1)} collective-permute-done((bf16[64,1792]{1,0:T(8,128)(2,1)S(1)}, bf16[64,1792]{1,0:T(8,128)(2,1)S(1)}, u32[]{:S(2)}, u32[]{:S(2)}) %collective-permute-start.3) | collective-permute-done | bytes 229408 | tf_op jit(solution)/shard_map/ppermute | solution.py:41
  23.9 2.2 %tables.1 = (f32[512,128]{1,0:T(8,128)S(1)}, f32[512,128]{1,0:T(8,128)S(1)}, s32[512,128]{1,0:T(8,128)S(1)}, s32[512,128]{1,0:T(8,128)S(1)}, s32[1,512]{1,0:T(1,128)S(1)}, /*index=5*/s32[2]{0:T(128)S(1)}) custom-call(s32[4,128]{1,0:T(4,128)S(1)} %bitcast.9, s32[512]{0:T(512)S(1)} %copy-done.10, f32[1,128]{1,0:T(1,128)S(1)} %copy-done.11), custom_call_target="tpu_custom_call" | custom-call | flops 4000000 | bytes 1000000 | tf_op jit(solution)/shard_map/tables/pallas_call | solution.py:130
  26.1 4.3 %collective-permute-done.6.refs_3_ = bf16[128,1792]{1,0:T(8,128)(2,1)S(1)} collective-permute-done((bf16[128,1792]{1,0:T(8,128)(2,1)S(1)}, bf16[128,1792]{1,0:T(8,128)(2,1)S(1)}, u32[]{:S(2)}, u32[]{:S(2)}) %collective-permute-start.6) | collective-permute-done | bytes 458784 | tf_op jit(solution)/shard_map/ppermute | solution.py:41
  34.6 2.1 %collective-permute-done.10.refs_6_ = bf16[3,128,1792]{2,1,0:T(8,128)(2,1)S(1)} collective-permute-done((bf16[3,128,1792]{2,1,0:T(8,128)(2,1)S(1)}, bf16[3,128,1792]{2,1,0:T(8,128)(2,1)S(1)}, u32[]{:S(2)}, u32[]{:S(2)}) %collective-permute-start.10) | collective-permute-done | bytes 1376288 | tf_op jit(solution)/shard_map/ppermute | solution.py:41
  40.7 2.0 %project_kv.1.refs_5_ = bf16[512,256]{1,0:T(8,128)(2,1)S(1)} custom-call(bf16[128,1792]{1,0:T(8,128)(2,1)S(1)} %get-tuple-element.91.refs_0_, bf16[128,1792]{1,0:T(8,128)(2,1)S(1)} %get-tuple-element.92.refs_1_, bf16[128,1792]{1,0:T(8,128)(2,1)S(1)} %get-tuple-element.93.refs_2_, bf16[128,1792]{1,0:T(8,128)(2,1)S(1)} %collective-permute-done.6.refs_3_, ...), custom_call_target="tpu_custom_call" | custom-call | flops 1409286144 | bytes 9000000 | tf_op jit(solution)/shard_map/project_kv/pallas_call | solution.py:241
  42.7 5.9 %collective-permute-start.15 = (bf16[512,256]{1,0:T(8,128)(2,1)S(1)}, bf16[512,256]{1,0:T(8,128)(2,1)S(1)}, u32[]{:S(2)}, u32[]{:S(2)}) collective-permute-start(bf16[512,256]{1,0:T(8,128)(2,1)S(1)} %project_kv.1.refs_5_), channel_id=1, source_target_pairs={{0,112},{16,0},{32,16},{48,32},{64,48},{80,64},{96,80},{112,96},{1... | collective-permute-start | bytes 786440 | tf_op jit(solution)/shard_map/ppermute | solution.py:259
  48.6 2.4 %project_q.1.refs_1_ = bf16[512,256]{1,0:T(8,128)(2,1)S(1)} custom-call(bf16[128,1792]{1,0:T(8,128)(2,1)S(1)} %get-tuple-element.91.refs_0_, bf16[128,1792]{1,0:T(8,128)(2,1)S(1)} %get-tuple-element.92.refs_1_, bf16[128,1792]{1,0:T(8,128)(2,1)S(1)} %get-tuple-element.93.refs_2_, bf16[128,1792]{1,0:T(8,128)(2,1)S(1)} %collective-permute-done.6.refs_3_, ...), custom_call_target="tpu_custom_call" | custom-call | flops 1409286144 | bytes 9000000 | tf_op jit(solution)/shard_map/project_q/pallas_call | solution.py:241
  51.0 2.0 %attend.6 = (f32[2,512,128]{2,1,0:T(8,128)S(1)}, f32[2,512,128]{2,1,0:T(8,128)S(1)}, f32[2,512,128]{2,1,0:T(8,128)S(1)}) custom-call(s32[2]{0:T(128)S(1)} %get-tuple-element.101.refs_0_, bf16[512,256]{1,0:T(8,128)(2,1)S(1)} %project_q.1.refs_1_, s32[512,128]{1,0:T(8,128)S(1)} %get-tuple-element.108.refs_2_, s32[512,128]{1,0:T(8,128)S(1)} %get-tuple-element.109.refs_3_, ...), custom_call_target="tpu_custom_call" | custom-call | flops 800000000 | bytes 3000000 | tf_op jit(solution)/shard_map/attend/pallas_call | solution.py:379
  54.5 3.4 %collective-permute-done.14.refs_5_ = bf16[512,256]{1,0:T(8,128)(2,1)S(1)} collective-permute-done((bf16[512,256]{1,0:T(8,128)(2,1)S(1)}, bf16[512,256]{1,0:T(8,128)(2,1)S(1)}, u32[]{:S(2)}, u32[]{:S(2)}) %collective-permute-start.14) | collective-permute-done | bytes 262176 | tf_op jit(solution)/shard_map/ppermute | solution.py:259
  58.2 1.7 %collective-permute-start.16 = (bf16[512,256]{1,0:T(8,128)(2,1)S(1)}, bf16[512,256]{1,0:T(8,128)(2,1)S(1)}, u32[]{:S(2)}, u32[]{:S(2)}) collective-permute-start(bf16[512,256]{1,0:T(8,128)(2,1)S(1)} %collective-permute-done.14.refs_5_), channel_id=1, source_target_pairs={{0,16},{16,32},{32,48},{48,64},{64,80},{80,96},{96,112},{112,0},{1... | collective-permute-start | bytes 786440 | tf_op jit(solution)/shard_map/ppermute | solution.py:259
  60.6 4.5 %collective-permute-done.17.refs_6_ = bf16[512,256]{1,0:T(8,128)(2,1)S(1)} collective-permute-done((bf16[512,256]{1,0:T(8,128)(2,1)S(1)}, bf16[512,256]{1,0:T(8,128)(2,1)S(1)}, u32[]{:S(2)}, u32[]{:S(2)}) %collective-permute-start.17) | collective-permute-done | bytes 262176 | tf_op jit(solution)/shard_map/ppermute | solution.py:259
  66.8 3.0 %collective-permute-start.19 = (bf16[512,256]{1,0:T(8,128)(2,1)S(1)}, bf16[512,256]{1,0:T(8,128)(2,1)S(1)}, u32[]{:S(2)}, u32[]{:S(2)}) collective-permute-start(bf16[512,256]{1,0:T(8,128)(2,1)S(1)} %collective-permute-done.17.refs_6_), channel_id=1, source_target_pairs={{0,112},{16,0},{32,16},{48,32},{64,48},{80,64},{96,80},{112,96},{1... | collective-permute-start | bytes 786440 | tf_op jit(solution)/shard_map/ppermute | solution.py:259
  70.5 3.7 %collective-permute-done.18.keys_ref.refs_5_ = bf16[512,256]{1,0:T(8,128)(2,1)S(1)} collective-permute-done((bf16[512,256]{1,0:T(8,128)(2,1)S(1)}, bf16[512,256]{1,0:T(8,128)(2,1)S(1)}, u32[]{:S(2)}, u32[]{:S(2)}) %collective-permute-start.18) | collective-permute-done | bytes 262176 | tf_op jit(solution)/shard_map/ppermute | solution.py:259
  74.4 3.3 %collective-permute-start.22 = (bf16[512,128]{1,0:T(8,128)(2,1)S(1)}, bf16[512,128]{1,0:T(8,128)(2,1)S(1)}, u32[]{:S(2)}, u32[]{:S(2)}) collective-permute-start(bf16[512,128]{1,0:T(8,128)(2,1)S(1)} %get-tuple-element.134), channel_id=1, source_target_pairs={{0,112},{16,0},{32,16},{48,32},{64,48},{80,64},{96,80},{112,96},{1... | collective-permute-start | bytes 393224 | tf_op jit(solution)/shard_map/ppermute | solution.py:259
  78.6 3.2 %collective-permute-done.21.refs_5_ = bf16[512,128]{1,0:T(8,128)(2,1)S(1)} collective-permute-done((bf16[512,128]{1,0:T(8,128)(2,1)S(1)}, bf16[512,128]{1,0:T(8,128)(2,1)S(1)}, u32[]{:S(2)}, u32[]{:S(2)}) %collective-permute-start.21) | collective-permute-done | bytes 131104 | tf_op jit(solution)/shard_map/ppermute | solution.py:259
  85.6 1.6 %collective-permute-done.25.refs_3_ = bf16[128,256]{1,0:T(8,128)(2,1)S(1)} collective-permute-done((bf16[128,256]{1,0:T(8,128)(2,1)S(1)}, bf16[128,256]{1,0:T(8,128)(2,1)S(1)}, u32[]{:S(2)}, u32[]{:S(2)}) %collective-permute-start.25) | collective-permute-done | bytes 65568 | tf_op jit(solution)/shard_map/ppermute | solution.py:41
  87.2 2.0 %collective-permute-done.24.refs_2_ = bf16[128,256]{1,0:T(8,128)(2,1)S(1)} collective-permute-done((bf16[128,256]{1,0:T(8,128)(2,1)S(1)}, bf16[128,256]{1,0:T(8,128)(2,1)S(1)}, u32[]{:S(2)}, u32[]{:S(2)}) %collective-permute-start.24) | collective-permute-done | bytes 65568 | tf_op jit(solution)/shard_map/ppermute | solution.py:41
  92.8 8.3 %collective-permute-done.28.refs_3_ = bf16[64,2688]{1,0:T(8,128)(2,1)S(1)} collective-permute-done((bf16[64,2688]{1,0:T(8,128)(2,1)S(1)}, bf16[64,2688]{1,0:T(8,128)(2,1)S(1)}, u32[]{:S(2)}, u32[]{:S(2)}) %collective-permute-start.28) | collective-permute-done | bytes 344096 | tf_op jit(solution)/shard_map/ppermute | solution.py:41
  102.1 2.2 %collective-permute-start.29 = (bf16[32,2688]{1,0:T(8,128)(2,1)S(1)}, bf16[32,2688]{1,0:T(8,128)(2,1)S(1)}, u32[]{:S(2)}, u32[]{:S(2)}) collective-permute-start(bf16[32,2688]{1,0:T(8,128)(2,1)S(1)} %get-tuple-element.157), channel_id=1, source_target_pairs={{0,6},{1,7},{2,4},{3,5},{4,2},{5,3},{6,0},{7,1},{8,14},{9,15},{10,... | collective-permute-start | bytes 516104 | tf_op jit(solution)/shard_map/ppermute | solution.py:41
  104.3 4.5 %collective-permute-done.29.refs_2_ = bf16[32,2688]{1,0:T(8,128)(2,1)S(1)} collective-permute-done((bf16[32,2688]{1,0:T(8,128)(2,1)S(1)}, bf16[32,2688]{1,0:T(8,128)(2,1)S(1)}, u32[]{:S(2)}, u32[]{:S(2)}) %collective-permute-start.29) | collective-permute-done | bytes 172064 | tf_op jit(solution)/shard_map/ppermute | solution.py:41
  (79 shorter events, 35.5 us)
Async XLA Ops:
  0.0 32.3 %collective-permute-start.9 = (bf16[256,5376]{1,0:T(8,128)(2,1)}, bf16[256,5376]{1,0:T(8,128)(2,1)S(1)}, u32[]{:S(2)}, u32[]{:S(2)}) collective-permute-start(bf16[256,5376]{1,0:T(8,128)(2,1)} %refs_4_.3), channel_id=1, source_target_pairs={{0,1},{1,0},{2,3},{3,2},{4,5},{5,4},{6,7},{7,6},{8,9},{9,8},{10,11... | collective-permute-start | bytes 8257544 | tf_op jit(solution)/shard_map/ppermute | solution.py:41
  2.1 5.6 %collective-permute-start = (bf16[32,1792]{1,0:T(8,128)(2,1)S(1)}, bf16[32,1792]{1,0:T(8,128)(2,1)S(1)}, u32[]{:S(2)}, u32[]{:S(2)}) collective-permute-start(bf16[32,1792]{1,0:T(8,128)(2,1)S(1)} %get-tuple-element.82.refs_0_), channel_id=1, source_target_pairs={{0,2},{1,3},{2,0},{3,1},{4,6},{5,7},{6,4},{7,5},{8,10},{9,11},{10,... | collective-permute-start | bytes 344072 | tf_op jit(solution)/shard_map/ppermute | solution.py:41
  3.6 6.4 %collective-permute-start.1 = (bf16[32,1792]{1,0:T(8,128)(2,1)S(1)}, bf16[32,1792]{1,0:T(8,128)(2,1)S(1)}, u32[]{:S(2)}, u32[]{:S(2)}) collective-permute-start(bf16[32,1792]{1,0:T(8,128)(2,1)S(1)} %get-tuple-element.83.refs_1_), channel_id=1, source_target_pairs={{0,6},{1,7},{2,4},{3,5},{4,2},{5,3},{6,0},{7,1},{8,14},{9,15},{10,... | collective-permute-start | bytes 344072 | tf_op jit(solution)/shard_map/ppermute | solution.py:41
  10.7 7.8 %collective-permute-start.3 = (bf16[64,1792]{1,0:T(8,128)(2,1)S(1)}, bf16[64,1792]{1,0:T(8,128)(2,1)S(1)}, u32[]{:S(2)}, u32[]{:S(2)}) collective-permute-start(bf16[64,1792]{1,0:T(8,128)(2,1)S(1)} %get-tuple-element.85.refs_0_), channel_id=1, source_target_pairs={{0,6},{1,7},{2,4},{3,5},{4,2},{5,3},{6,0},{7,1},{8,14},{9,15},{10,... | collective-permute-start | bytes 688136 | tf_op jit(solution)/shard_map/ppermute | solution.py:41
  12.3 6.5 %collective-permute-start.4 = (bf16[64,1792]{1,0:T(8,128)(2,1)S(1)}, bf16[64,1792]{1,0:T(8,128)(2,1)S(1)}, u32[]{:S(2)}, u32[]{:S(2)}) collective-permute-start(bf16[64,1792]{1,0:T(8,128)(2,1)S(1)} %get-tuple-element.86.refs_1_), channel_id=1, source_target_pairs={{0,8},{1,9},{2,10},{3,11},{4,12},{5,13},{6,14},{7,15},{8,0},{9,1},... | collective-permute-start | bytes 688136 | tf_op jit(solution)/shard_map/ppermute | solution.py:41
  13.6 6.3 %collective-permute-start.5 = (bf16[64,1792]{1,0:T(8,128)(2,1)S(1)}, bf16[64,1792]{1,0:T(8,128)(2,1)S(1)}, u32[]{:S(2)}, u32[]{:S(2)}) collective-permute-start(bf16[64,1792]{1,0:T(8,128)(2,1)S(1)} %get-tuple-element.87.refs_2_), channel_id=1, source_target_pairs={{0,2},{1,3},{2,0},{3,1},{4,6},{5,7},{6,4},{7,5},{8,10},{9,11},{10,... | collective-permute-start | bytes 688136 | tf_op jit(solution)/shard_map/ppermute | solution.py:41
  20.0 10.3 %collective-permute-start.6 = (bf16[128,1792]{1,0:T(8,128)(2,1)S(1)}, bf16[128,1792]{1,0:T(8,128)(2,1)S(1)}, u32[]{:S(2)}, u32[]{:S(2)}) collective-permute-start(bf16[128,1792]{1,0:T(8,128)(2,1)S(1)} %get-tuple-element.91.refs_0_), channel_id=1, source_target_pairs={{0,8},{1,9},{2,10},{3,11},{4,12},{5,13},{6,14},{7,15},{8,0},{9,1},... | collective-permute-start | bytes 1376264 | tf_op jit(solution)/shard_map/ppermute | solution.py:41
  20.8 10.0 %collective-permute-start.7 = (bf16[128,1792]{1,0:T(8,128)(2,1)S(1)}, bf16[128,1792]{1,0:T(8,128)(2,1)S(1)}, u32[]{:S(2)}, u32[]{:S(2)}) collective-permute-start(bf16[128,1792]{1,0:T(8,128)(2,1)S(1)} %get-tuple-element.92.refs_1_), channel_id=1, source_target_pairs={{0,2},{1,3},{2,0},{3,1},{4,6},{5,7},{6,4},{7,5},{8,10},{9,11},{10,... | collective-permute-start | bytes 1376264 | tf_op jit(solution)/shard_map/ppermute | solution.py:41
  21.1 11.2 %collective-permute-start.8 = (bf16[128,1792]{1,0:T(8,128)(2,1)S(1)}, bf16[128,1792]{1,0:T(8,128)(2,1)S(1)}, u32[]{:S(2)}, u32[]{:S(2)}) collective-permute-start(bf16[128,1792]{1,0:T(8,128)(2,1)S(1)} %get-tuple-element.93.refs_2_), channel_id=1, source_target_pairs={{0,6},{1,7},{2,4},{3,5},{4,2},{5,3},{6,0},{7,1},{8,14},{9,15},{10,... | collective-permute-start | bytes 1376264 | tf_op jit(solution)/shard_map/ppermute | solution.py:41
  32.3 41.9 %collective-permute-start.20 = (bf16[256,5376]{1,0:T(8,128)(2,1)S(1)}, bf16[256,5376]{1,0:T(8,128)(2,1)S(1)}, u32[]{:S(2)}, u32[]{:S(2)}) collective-permute-start(bf16[256,5376]{1,0:T(8,128)(2,1)S(1)} %collective-permute-done.9.refs_5_), channel_id=1, source_target_pairs={{0,8},{1,137},{2,10},{3,139},{4,12},{5,141},{6,14},{7,143},{8,0},{... | collective-permute-start | bytes 8257544 | tf_op jit(solution)/shard_map/ppermute | solution.py:45
  42.7 11.8 %collective-permute-start.15 = (bf16[512,256]{1,0:T(8,128)(2,1)S(1)}, bf16[512,256]{1,0:T(8,128)(2,1)S(1)}, u32[]{:S(2)}, u32[]{:S(2)}) collective-permute-start(bf16[512,256]{1,0:T(8,128)(2,1)S(1)} %project_kv.1.refs_5_), channel_id=1, source_target_pairs={{0,112},{16,0},{32,16},{48,32},{64,48},{80,64},{96,80},{112,96},{1... | collective-permute-start | bytes 786440 | tf_op jit(solution)/shard_map/ppermute | solution.py:259
  48.6 9.3 %collective-permute-start.14 = (bf16[512,256]{1,0:T(8,128)(2,1)S(1)}, bf16[512,256]{1,0:T(8,128)(2,1)S(1)}, u32[]{:S(2)}, u32[]{:S(2)}) collective-permute-start(bf16[512,256]{1,0:T(8,128)(2,1)S(1)} %project_kv.1.refs_5_), channel_id=1, source_target_pairs={{0,16},{16,32},{32,48},{48,64},{64,80},{80,96},{96,112},{112,0},{1... | collective-permute-start | bytes 786440 | tf_op jit(solution)/shard_map/ppermute | solution.py:259
  57.9 7.2 %collective-permute-start.17 = (bf16[512,256]{1,0:T(8,128)(2,1)S(1)}, bf16[512,256]{1,0:T(8,128)(2,1)S(1)}, u32[]{:S(2)}, u32[]{:S(2)}) collective-permute-start(bf16[512,256]{1,0:T(8,128)(2,1)S(1)} %collective-permute-done.15), channel_id=1, source_target_pairs={{0,112},{16,0},{32,16},{48,32},{64,48},{80,64},{96,80},{112,96},{1... | collective-permute-start | bytes 786440 | tf_op jit(solution)/shard_map/ppermute | solution.py:259
  58.2 8.5 %collective-permute-start.16 = (bf16[512,256]{1,0:T(8,128)(2,1)S(1)}, bf16[512,256]{1,0:T(8,128)(2,1)S(1)}, u32[]{:S(2)}, u32[]{:S(2)}) collective-permute-start(bf16[512,256]{1,0:T(8,128)(2,1)S(1)} %collective-permute-done.14.refs_5_), channel_id=1, source_target_pairs={{0,16},{16,32},{32,48},{48,64},{64,80},{80,96},{96,112},{112,0},{1... | collective-permute-start | bytes 786440 | tf_op jit(solution)/shard_map/ppermute | solution.py:259
  66.6 7.6 %collective-permute-start.18 = (bf16[512,256]{1,0:T(8,128)(2,1)S(1)}, bf16[512,256]{1,0:T(8,128)(2,1)S(1)}, u32[]{:S(2)}, u32[]{:S(2)}) collective-permute-start(bf16[512,256]{1,0:T(8,128)(2,1)S(1)} %collective-permute-done.16.refs_5_), channel_id=1, source_target_pairs={{0,16},{16,32},{32,48},{48,64},{64,80},{80,96},{96,112},{112,0},{1... | collective-permute-start | bytes 786440 | tf_op jit(solution)/shard_map/ppermute | solution.py:259
  66.8 7.4 %collective-permute-start.19 = (bf16[512,256]{1,0:T(8,128)(2,1)S(1)}, bf16[512,256]{1,0:T(8,128)(2,1)S(1)}, u32[]{:S(2)}, u32[]{:S(2)}) collective-permute-start(bf16[512,256]{1,0:T(8,128)(2,1)S(1)} %collective-permute-done.17.refs_6_), channel_id=1, source_target_pairs={{0,112},{16,0},{32,16},{48,32},{64,48},{80,64},{96,80},{112,96},{1... | collective-permute-start | bytes 786440 | tf_op jit(solution)/shard_map/ppermute | solution.py:259
  74.2 15.0 %collective-permute-start.26 = (bf16[256,5376]{1,0:T(8,128)(2,1)S(1)}, bf16[256,5376]{1,0:T(8,128)(2,1)S(1)}, u32[]{:S(2)}, u32[]{:S(2)}) collective-permute-start(bf16[256,5376]{1,0:T(8,128)(2,1)S(1)} %collective-permute-done.20.refs_7_), channel_id=1, source_target_pairs={{0,1},{1,0},{2,3},{3,2},{4,5},{5,4},{6,7},{7,6},{8,9},{9,8},{10,11... | collective-permute-start | bytes 8257544 | tf_op jit(solution)/shard_map/ppermute | solution.py:41
  74.3 7.5 %collective-permute-start.21 = (bf16[512,128]{1,0:T(8,128)(2,1)S(1)}, bf16[512,128]{1,0:T(8,128)(2,1)S(1)}, u32[]{:S(2)}, u32[]{:S(2)}) collective-permute-start(bf16[512,128]{1,0:T(8,128)(2,1)S(1)} %get-tuple-element.133), channel_id=1, source_target_pairs={{0,16},{16,32},{32,48},{48,64},{64,80},{80,96},{96,112},{112,0},{1... | collective-permute-start | bytes 393224 | tf_op jit(solution)/shard_map/ppermute | solution.py:259
  74.4 7.4 %collective-permute-start.22 = (bf16[512,128]{1,0:T(8,128)(2,1)S(1)}, bf16[512,128]{1,0:T(8,128)(2,1)S(1)}, u32[]{:S(2)}, u32[]{:S(2)}) collective-permute-start(bf16[512,128]{1,0:T(8,128)(2,1)S(1)} %get-tuple-element.134), channel_id=1, source_target_pairs={{0,112},{16,0},{32,16},{48,32},{64,48},{80,64},{96,80},{112,96},{1... | collective-permute-start | bytes 393224 | tf_op jit(solution)/shard_map/ppermute | solution.py:259
  84.3 5.0 %collective-permute-start.24 = (bf16[128,256]{1,0:T(8,128)(2,1)S(1)}, bf16[128,256]{1,0:T(8,128)(2,1)S(1)}, u32[]{:S(2)}, u32[]{:S(2)}) collective-permute-start(bf16[128,256]{1,0:T(8,128)(2,1)S(1)} %get-tuple-element.148), channel_id=1, source_target_pairs={{0,8},{1,9},{2,10},{3,11},{4,12},{5,13},{6,14},{7,15},{8,0},{9,1},... | collective-permute-start | bytes 196616 | tf_op jit(solution)/shard_map/ppermute | solution.py:41
  90.4 10.8 %collective-permute-start.28 = (bf16[64,2688]{1,0:T(8,128)(2,1)S(1)}, bf16[64,2688]{1,0:T(8,128)(2,1)S(1)}, u32[]{:S(2)}, u32[]{:S(2)}) collective-permute-start(bf16[64,2688]{1,0:T(8,128)(2,1)S(1)} %get-tuple-element.154), channel_id=1, source_target_pairs={{0,6},{1,7},{2,4},{3,5},{4,2},{5,3},{6,0},{7,1},{8,14},{9,15},{10,... | collective-permute-start | bytes 1032200 | tf_op jit(solution)/shard_map/ppermute | solution.py:41
  92.7 9.3 %collective-permute-start.27 = (bf16[64,2688]{1,0:T(8,128)(2,1)S(1)}, bf16[64,2688]{1,0:T(8,128)(2,1)S(1)}, u32[]{:S(2)}, u32[]{:S(2)}) collective-permute-start(bf16[64,2688]{1,0:T(8,128)(2,1)S(1)} %get-tuple-element.153), channel_id=1, source_target_pairs={{0,2},{1,3},{2,0},{3,1},{4,6},{5,7},{6,4},{7,5},{8,10},{9,11},{10,... | collective-permute-start | bytes 1032200 | tf_op jit(solution)/shard_map/ppermute | solution.py:41
  102.1 6.7 %collective-permute-start.29 = (bf16[32,2688]{1,0:T(8,128)(2,1)S(1)}, bf16[32,2688]{1,0:T(8,128)(2,1)S(1)}, u32[]{:S(2)}, u32[]{:S(2)}) collective-permute-start(bf16[32,2688]{1,0:T(8,128)(2,1)S(1)} %get-tuple-element.157), channel_id=1, source_target_pairs={{0,6},{1,7},{2,4},{3,5},{4,2},{5,3},{6,0},{7,1},{8,14},{9,15},{10,... | collective-permute-start | bytes 516104 | tf_op jit(solution)/shard_map/ppermute | solution.py:41
  104.3 5.4 %collective-permute-start.30 = (bf16[32,2688]{1,0:T(8,128)(2,1)S(1)}, bf16[32,2688]{1,0:T(8,128)(2,1)S(1)}, u32[]{:S(2)}, u32[]{:S(2)}) collective-permute-start(bf16[32,2688]{1,0:T(8,128)(2,1)S(1)} %get-tuple-element.158), channel_id=1, source_target_pairs={{0,2},{1,3},{2,0},{3,1},{4,6},{5,7},{6,4},{7,5},{8,10},{9,11},{10,... | collective-permute-start | bytes 516104 | tf_op jit(solution)/shard_map/ppermute | solution.py:41
  (19 other events, 133.2 us)

commit v4 on v3

--- a/solution.py
+++ b/solution.py
@@ -61,7 +61,16 @@
     return jax.ShapeDtypeStruct((rows, columns), dtype)
 
 
-def norm_kernel(x_ref, gain_ref, *outs):
+def norm_kernel(x_hbm, gain_hbm, *refs):
+    outs, x_ref, gain_ref, sem = refs[0:3], refs[3], refs[4], refs[5]
+    copies = [
+        pltpu.make_async_copy(x_hbm, x_ref, sem.at[0]),
+        pltpu.make_async_copy(gain_hbm, gain_ref, sem.at[1]),
+    ]
+    for copy in copies:
+        copy.start()
+    for copy in copies:
+        copy.wait()
     square = jnp.zeros((ROWS, HD), jnp.float32)
     for k in range(D // HD):
         x = x_ref[:, k * HD : (k + 1) * HD].astype(jnp.float32)
@@ -80,16 +89,46 @@
     return pl.pallas_call(
         norm_kernel,
         out_shape=[shape(ROWS, THIRD)] * 3,
-        in_specs=whole(2),
+        in_specs=[pl.BlockSpec(memory_space=pltpu.HBM)] * 2,
         out_specs=whole(3),
+        scratch_shapes=[
+            pltpu.VMEM((ROWS, D), jnp.bfloat16),
+            pltpu.VMEM((D // HD, HD), jnp.float32),
+            pltpu.SemaphoreType.DMA((2,)),
+        ],
         compiler_params=params(4),
         name="norm_rows",
     )(residual, gain.reshape(D // HD, HD))
 
 
 def tables_kernel(
-    starts_ref, first_ref, frequency_ref, cos_ref, sin_ref, position_ref, start_ref, offset_ref, where_ref, natural
+    starts_ref,
+    first_ref,
+    frequency_ref,
+    query_gain_ref,
+    key_gain_ref,
+    key_weight_ref,
+    value_weight_ref,
+    cos_ref,
+    sin_ref,
+    position_ref,
+    start_ref,
+    offset_ref,
+    query_gain_out,
+    key_gain_out,
+    weight_out,
+    where_ref,
+    natural,
+    sem,
 ):
+    copies = [
+        pltpu.make_async_copy(source, weight_out.at[:, pl.ds(k * HD, HD)], sem.at[k])
+        for k, source in enumerate((key_weight_ref, value_weight_ref))
+    ]
+    for copy in copies:
+        copy.start()
+    query_gain_out[...] = query_gain_ref[...]
+    key_gain_out[...] = key_gain_ref[...]
     mine = lax.axis_index("mp")
     block = lax.axis_index("ctx")
     row = lax.broadcasted_iota(jnp.int32, (HD, HD), 0)
@@ -119,9 +158,11 @@
     offset_ref[...] = offset
     where_ref[0] = block
     where_ref[1] = block - (first_ref[0] >> 9) + 1
-
-
-def make_tables(document_start):
+    for copy in copies:
+        copy.wait()
+
+
+def make_tables(document_start, query_gain, key_gain, key_weight, value_weight):
     frequency = np.float32(rope_base) ** (
         -(np.arange(HD // 2, dtype=np.float32) * np.float32(2.0) / np.float32(HD))
     )
@@ -135,21 +176,34 @@
             wide(jnp.int32),
             wide(jnp.int32),
             jax.ShapeDtypeStruct((1, BLOCK), jnp.int32),
+            shape(1, HD, jnp.float32),
+            shape(1, HD, jnp.float32),
+            shape(D, 2 * HD),
             jax.ShapeDtypeStruct((2,), jnp.int32),
         ],
         in_specs=[
             pl.BlockSpec(memory_space=pltpu.VMEM),
             pl.BlockSpec(memory_space=pltpu.SMEM),
-            pl.BlockSpec(memory_space=pltpu.VMEM),
+            *whole(3),
+            pl.BlockSpec(memory_space=pltpu.HBM),
+            pl.BlockSpec(memory_space=pltpu.HBM),
         ],
-        out_specs=whole(5) + [pl.BlockSpec(memory_space=pltpu.SMEM)],
-        scratch_shapes=[pltpu.VMEM((BLOCK, HD), jnp.int32)],
-        compiler_params=params(4),
+        out_specs=whole(8) + [pl.BlockSpec(memory_space=pltpu.SMEM)],
+        scratch_shapes=[pltpu.VMEM((BLOCK, HD), jnp.int32), pltpu.SemaphoreType.DMA((2,))],
+        compiler_params=params(7),
         cost_estimate=pl.CostEstimate(
             flops=4000000, bytes_accessed=1000000, transcendentals=131072
         ),
         name="tables",
-    )(document_start.reshape(BLOCK // HD, HD), document_start, frequency)
+    )(
+        document_start.reshape(BLOCK // HD, HD),
+        document_start,
+        frequency,
+        query_gain.reshape(1, HD),
+        key_gain.reshape(1, HD),
+        key_weight,
+        value_weight,
+    )
 
 
 def join_kernel(extra, *refs):
@@ -178,21 +232,22 @@
     )(*held, *came)
 
 
-def gather_tokens(thirds, document_start, core_weight):
+def gather_tokens(thirds, document_start, core_weight, *small):
     came = [swap(thirds[p], ORDERS[p][0]) for p in range(3)]
     two = join(thirds, came, False)
     came = [swap(two[p], ORDERS[p][1]) for p in range(3)]
-    *came, document_start = lax.optimization_barrier((*came, document_start))
+    *came, document_start, core_weight = lax.optimization_barrier(
+        (*came, document_start, core_weight)
+    )
     *four, packed = join(two, came, True)
     late = [swap(four[p], ORDERS[p][2]) for p in range(3)]
     other = swap(packed, CC)
-    tables = make_tables(document_start)
-    *late, cosine, sine, position, start, offset, where, core_weight = lax.optimization_barrier(
-        (*late, *tables, core_weight)
-    )
+    tables = make_tables(document_start, *small)
+    other_late = [swap(late[p], CC) for p in range(3)]
+    held = lax.optimization_barrier((*late, *tables, core_weight))
+    late, tables, core_weight = held[0:3], held[3:12], held[12]
     both_weight = swap_y_both_ways(core_weight)
-    other_late = [swap(late[p], CC) for p in range(3)]
-    return (four, late, other, other_late), cosine, sine, where, position, start, offset, core_weight, both_weight
+    return (four, late, other, other_late), tables, core_weight, both_weight
 
 
 def rotate(raw, gain, cosine, sine):
@@ -202,10 +257,9 @@
     return (scaled * cosine + turned * sine).astype(jnp.bfloat16)
 
 
-def project_kernel(weight_count, *refs):
+def project_kernel(both, *refs):
     x_refs = refs[0:10]
-    w_refs = refs[10 : 10 + weight_count]
-    gain_ref, cos_ref, sin_ref, out_ref = refs[10 + weight_count :]
+    w_ref, gain_ref, cos_ref, sin_ref, out_ref = refs[10:]
     four, late, other, other_late = x_refs[0:3], x_refs[3:6], x_refs[6], x_refs[7:10]
     total = None
     for part in range(3):
@@ -221,34 +275,33 @@
                     rows.append(other[part, at : at + ROWS])
                 else:
                     rows.append(other_late[part][at : at + ROWS])
-        weights = [w[part * THIRD : (part + 1) * THIRD] for w in w_refs]
         product = jnp.dot(
             jnp.concatenate(rows, axis=0),
-            jnp.concatenate(weights, axis=1) if weight_count == 2 else weights[0],
+            w_ref[part * THIRD : (part + 1) * THIRD],
             preferred_element_type=jnp.float32,
         )
         total = product if part == 0 else total + product
     gain = gain_ref[...]
     out_ref[:, 0:HD] = rotate(total[:, 0:HD], gain, cos_ref[...], sin_ref[...])
-    if weight_count == 1:
+    if both:
         out_ref[:, HD : 2 * HD] = rotate(total[:, HD : 2 * HD], gain, cos_ref[...], sin_ref[...])
     else:
         out_ref[:, HD : 2 * HD] = total[:, HD : 2 * HD].astype(jnp.bfloat16)
 
 
-def project(pieces, weights, gain, cosine, sine, name):
+def project(pieces, weight, gain, cosine, sine, both, name):
     four, late, other, other_late = pieces
     return pl.pallas_call(
-        functools.partial(project_kernel, len(weights)),
+        functools.partial(project_kernel, both),
         out_shape=shape(BLOCK, 2 * HD),
-        in_specs=whole(13 + len(weights)),
+        in_specs=whole(14),
         out_specs=whole(1)[0],
         compiler_params=params(14),
         cost_estimate=pl.CostEstimate(
             flops=2 * BLOCK * D * 2 * HD, bytes_accessed=9000000, transcendentals=0
         ),
         name=name,
-    )(*four, *late, other, *other_late, *weights, gain.reshape(1, HD), cosine, sine)
+    )(*four, *late, other, *other_late, weight, gain, cosine, sine)
 
 
 NEG = -1e30
@@ -266,7 +319,7 @@
     if not first:
         old_state, refs = refs[0:3], refs[3:]
     if last:
-        out_refs, state = refs[0:2], refs[2:5]
+        out_refs, state = refs[0:4], refs[4:7]
     else:
         state = refs[0:3]
     top, total, acc = state
@@ -328,8 +381,6 @@
     source = None if first else old_state
     k = 0
     for distance, whole_block in zip(distances, joint):
-        if whole_block == 2:
-            continue
         if whole_block:
             keys_ref = blocks[k].at[:, pl.ds(0, HD)]
             values_ref = blocks[k].at[:, pl.ds(HD, HD)]
@@ -348,7 +399,7 @@
         source = state
     if last:
         for head in range(2):
-            for quarter in range(2):
+            for quarter in range(4):
                 here = slice(quarter * 128, (quarter + 1) * 128)
                 denominator = jnp.sum(total[head, here], axis=-1, keepdims=True)
                 out_refs[quarter][:, head * HD : (head + 1) * HD] = (
@@ -356,34 +407,22 @@
                 ).astype(jnp.bfloat16)
 
 
-def attend(tables, query, distances, joint, blocks, state, last, half=None):
+def attend(tables, query, distances, joint, blocks, state, last):
     where, position, start, offset = tables
     first = state is None
     state = () if first else tuple(state)
-    rows_here = BLOCK // 2 if last else BLOCK
-    state_shape = jax.ShapeDtypeStruct((2, rows_here, HD), jnp.float32)
+    state_shape = jax.ShapeDtypeStruct((2, BLOCK, HD), jnp.float32)
     if last:
-        out_shape, out_specs = [shape(128, 2 * HD)] * 2, whole(2)
-        scratch = [pltpu.VMEM((2, rows_here, HD), jnp.float32)] * 3
-        row_specs = [
-            pl.BlockSpec((rows_here, 2 * HD), lambda k: (half, 0)),
-            pl.BlockSpec((rows_here, HD), lambda k: (half, 0)),
-            pl.BlockSpec((rows_here, HD), lambda k: (half, 0)),
-        ]
-        state_specs = [pl.BlockSpec((2, rows_here, HD), lambda k: (0, half, 0))] * 3
+        out_shape, out_specs = [shape(128, 2 * HD)] * 4, whole(4)
+        scratch = [pltpu.VMEM((2, BLOCK, HD), jnp.float32)] * 3
     else:
         out_shape, out_specs = [state_shape] * 3, whole(3)
         scratch = []
-        row_specs = whole(3)
-        state_specs = whole(3)
     return pl.pallas_call(
         functools.partial(attend_kernel, distances, joint, first, last),
         out_shape=out_shape,
-        grid=(1,) if last else (),
         in_specs=[pl.BlockSpec(memory_space=pltpu.SMEM)]
-        + row_specs
-        + whole(1 + len(blocks))
-        + (state_specs if state else []),
+        + whole(4 + len(blocks) + len(state)),
         out_specs=out_specs,
         scratch_shapes=scratch,
         compiler_params=params(10),
@@ -428,12 +467,11 @@
     three, back_three, state, both_weight = tie((three, back_three, state, both_weight))
     y_weight = swap(both_weight, CC)
     key_half, value_half = take_halves(three, back_three)
-    key_far = move(key_half, 1)
-    value_far = move(value_half, -1)
+    key_far = lax.ppermute(key_half, "ctx", [(3, 4), (4, 5), (5, 6)])
+    value_far = lax.ppermute(value_half, "ctx", [(5, 4), (6, 5), (7, 6)])
     state = attend(tables, query, (3, 5), (1, 1), [three, back_three], state, False)
     key_far, value_far, state = tie((key_far, value_far, state))
-    to_core, to_both = attend(tables, query, (4,), (0, 2), [key_far, value_far], state, True, 1)
-    mine, to_y = attend(tables, query, (4,), (0, 2), [key_far, value_far], state, True, 0)
+    mine, to_y, to_core, to_both = attend(tables, query, (4,), (0, 2), [key_far, value_far], state, True)
     parts = [mine, swap(to_core, CC), swap(to_y, YY), swap(to_both, CC ^ YY)]
     return parts, [output_weight, core_weight, y_weight, both_weight]
 
@@ -553,17 +591,21 @@
 ):
     thirds = norm_rows(residual_in, input_gain)
 
-    pieces, cosine, sine, where, position_wide, start_wide, offset, core_weight, both_weight = gather_tokens(
+    pieces, made, core_weight, both_weight = gather_tokens(
         thirds,
         document_start,
         swap(output_weight, CC),
-    )
-    tables = (where, position_wide, start_wide, offset)
-    rows = project(pieces, [key_weight, value_weight], key_gain, cosine, sine, "project_kv")
+        query_gain,
+        key_gain,
+        key_weight,
+        value_weight,
+    )
+    cosine, sine, position, start, offset, query_gain, key_gain, pair_weight, where = made
+    rows = project(pieces, pair_weight, key_gain, cosine, sine, False, "project_kv")
     parts, weights = share_and_attend(
         rows,
-        lambda: project(pieces, [query_weight], query_gain, cosine, sine, "project_q"),
-        tables,
+        lambda: project(pieces, query_weight, query_gain, cosine, sine, True, "project_q"),
+        (where, position, start, offset),
         output_weight,
         core_weight,
         both_weight,

time: 111 us -> 109 us (0.982)
  the two profiles are of different devices: /device:TPU:16 before, /device:TPU:160 now
where the time goes in v4:
time: 109 us
  waiting for transfers between devices  48.2 us (44%)
  starting transfers between devices  31.6 us (29%)
  Pallas kernels  22.8 us (21%)
  local copies, waits for them, and re-layouts  5.83 us (5%)
    ppermute x22, waiting for transfers between devices, swap(): return lax.ppermute(value, 'mp', [(m, m ^ link) for m in range(16)])  35.6 us
    ppermute x22, starting transfers between devices, swap(): return lax.ppermute(value, 'mp', [(m, m ^ link) for m in range(16)])  17.1 us
    pallas_call x5, Pallas kernels, attend(): pl.pallas_call(functools.partial(attend_kernel, distances, joint, first,...  11.6 us
    ppermute x6, waiting for transfers between devices, move(): return lax.ppermute(value, 'ctx', [(c, (c + step) % 8) for c in range(8)])  10.6 us
    ppermute x6, starting transfers between devices, move(): return lax.ppermute(value, 'ctx', [(c, (c + step) % 8) for c in range(8)])  6.31 us
    unnamed x24, local copies, waits for them, and re-layouts  5.83 us
    ppermute x1, starting transfers between devices, share_and_attend(): key_far = lax.ppermute(key_half, 'ctx', [(3, 4), (4, 5), (5, 6)])  4.64 us
    pallas_call x2, Pallas kernels, project(): pl.pallas_call(functools.partial(project_kernel, both), out_shape=shape(B...  4.35 us
  transfers between devices with their start and end apart: 31, of which 25 were waited for; matrix products, arithmetic and copies ran while one was open for 0% of the time, Pallas kernels for 19%

profile of v4, /device:TPU:160, one launch (start us, length us, event | category | flops | bytes accessed | tf_op | source)
XLA Modules:
  0.0 108.6 jit_solution(1397182051048684780)
XLA Ops:
  3.8 2.1 %collective-permute-start.1 = (bf16[32,1792]{1,0:T(8,128)(2,1)S(1)}, bf16[32,1792]{1,0:T(8,128)(2,1)S(1)}, u32[]{:S(2)}, u32[]{:S(2)}) collective-permute-start(bf16[32,1792]{1,0:T(8,128)(2,1)S(1)} %get-tuple-element.90.refs_1_), channel_id=1, source_target_pairs={{0,6},{1,7},{2,4},{3,5},{4,2},{5,3},{6,0},{7,1},{8,14},{9,15},{10,... | collective-permute-start | bytes 344072 | tf_op jit(solution)/shard_map/ppermute | solution.py:41
  7.8 2.4 %collective-permute-done.1.refs_4_ = bf16[32,1792]{1,0:T(8,128)(2,1)S(1)} collective-permute-done((bf16[32,1792]{1,0:T(8,128)(2,1)S(1)}, bf16[32,1792]{1,0:T(8,128)(2,1)S(1)}, u32[]{:S(2)}, u32[]{:S(2)}) %collective-permute-start.1) | collective-permute-done | bytes 114720 | tf_op jit(solution)/shard_map/ppermute | solution.py:41
  14.0 4.6 %collective-permute-done.3.refs_3_ = bf16[64,1792]{1,0:T(8,128)(2,1)S(1)} collective-permute-done((bf16[64,1792]{1,0:T(8,128)(2,1)S(1)}, bf16[64,1792]{1,0:T(8,128)(2,1)S(1)}, u32[]{:S(2)}, u32[]{:S(2)}) %collective-permute-start.3) | collective-permute-done | bytes 229408 | tf_op jit(solution)/shard_map/ppermute | solution.py:41
  26.7 2.8 %tables.1 = (f32[512,128]{1,0:T(8,128)S(1)}, f32[512,128]{1,0:T(8,128)S(1)}, s32[512,128]{1,0:T(8,128)S(1)}, s32[512,128]{1,0:T(8,128)S(1)}, s32[1,512]{1,0:T(1,...) custom-call(s32[4,128]{1,0:T(4,128)S(1)} %bitcast.7, ...), custom_call_target="tpu_custom_call" | custom-call | flops 4000000 | bytes 1000000 | tf_op jit(solution)/shard_map/tables/pallas_call | solution.py:171
  35.1 2.8 %collective-permute-done.11.refs_7_ = bf16[128,1792]{1,0:T(8,128)(2,1)S(1)} collective-permute-done((bf16[128,1792]{1,0:T(8,128)(2,1)S(1)}, bf16[128,1792]{1,0:T(8,128)(2,1)S(1)}, u32[]{:S(2)}, u32[]{:S(2)}) %collective-permute-start.11) | collective-permute-done | bytes 458784 | tf_op jit(solution)/shard_map/ppermute | solution.py:41
  39.2 2.0 %project_kv.1.refs_5_ = bf16[512,256]{1,0:T(8,128)(2,1)S(1)} custom-call(bf16[128,1792]{1,0:T(8,128)(2,1)S(1)} %get-tuple-element.98.refs_0_, bf16[128,1792]{1,0:T(8,128)(2,1)S(1)} %get-tuple-element.99.refs_1_, bf16[128,1792]{1,0:T(8,128)(2,1)S(1)} %get-tuple-element.100.refs_2_, bf16[128,1792]{1,0:T(8,128)(2,1)S(1)} %collective-permute-done.7.refs_3_, ...), custom_call_target="tpu_custom_call" | custom-call | flops 1409286144 | bytes 9000000 | tf_op jit(solution)/shard_map/project_kv/pallas_call | solution.py:294
  43.4 2.3 %project_q.1.refs_1_ = bf16[512,256]{1,0:T(8,128)(2,1)S(1)} custom-call(bf16[128,1792]{1,0:T(8,128)(2,1)S(1)} %get-tuple-element.98.refs_0_, bf16[128,1792]{1,0:T(8,128)(2,1)S(1)} %get-tuple-element.99.refs_1_, bf16[128,1792]{1,0:T(8,128)(2,1)S(1)} %get-tuple-element.100.refs_2_, bf16[128,1792]{1,0:T(8,128)(2,1)S(1)} %collective-permute-done.7.refs_3_, ...), custom_call_target="tpu_custom_call" | custom-call | flops 1409286144 | bytes 9000000 | tf_op jit(solution)/shard_map/project_q/pallas_call | solution.py:294
  45.8 2.0 %attend.5 = (f32[2,512,128]{2,1,0:T(8,128)S(1)}, f32[2,512,128]{2,1,0:T(8,128)S(1)}, f32[2,512,128]{2,1,0:T(8,128)S(1)}) custom-call(s32[2]{0:T(128)S(1)} %get-tuple-element.112.refs_0_, bf16[512,256]{1,0:T(8,128)(2,1)S(1)} %project_q.1.refs_1_, s32[512,128]{1,0:T(8,128)S(1)} %get-tuple-element.120.refs_2_, s32[512,128]{1,0:T(8,128)S(1)} %get-tuple-element.121.refs_3_, ...), custom_call_target="tpu_custom_call" | custom-call | flops 800000000 | bytes 3000000 | tf_op jit(solution)/shard_map/attend/pallas_call | solution.py:421
  47.8 2.0 %collective-permute-done.15 = bf16[512,256]{1,0:T(8,128)(2,1)S(1)} collective-permute-done((bf16[512,256]{1,0:T(8,128)(2,1)S(1)}, bf16[512,256]{1,0:T(8,128)(2,1)S(1)}, u32[]{:S(2)}, u32[]{:S(2)}) %collective-permute-start.15) | collective-permute-done | bytes 262176 | tf_op jit(solution)/shard_map/ppermute | solution.py:312
  52.5 1.9 %attend.6 = (f32[2,512,128]{2,1,0:T(8,128)S(1)}, f32[2,512,128]{2,1,0:T(8,128)S(1)}, f32[2,512,128]{2,1,0:T(8,128)S(1)}) custom-call(s32[2]{0:T(128)S(1)} %get-tuple-element.112.refs_0_, bf16[512,256]{1,0:T(8,128)(2,1)S(1)} %project_q.1.refs_1_, s32[512,128]{1,0:T(8,128)S(1)} %get-tuple-element.120.refs_2_, s32[512,128]{1,0:T(8,128)S(1)} %get-tuple-element.121.refs_3_, ...), custom_call_target="tpu_custom_call" | custom-call | flops 800000000 | bytes 3000000 | tf_op jit(solution)/shard_map/attend/pallas_call | solution.py:421
  54.5 3.2 %collective-permute-done.17.refs_6_ = bf16[512,256]{1,0:T(8,128)(2,1)S(1)} collective-permute-done((bf16[512,256]{1,0:T(8,128)(2,1)S(1)}, bf16[512,256]{1,0:T(8,128)(2,1)S(1)}, u32[]{:S(2)}, u32[]{:S(2)}) %collective-permute-start.17) | collective-permute-done | bytes 262176 | tf_op jit(solution)/shard_map/ppermute | solution.py:312
  57.7 1.6 %collective-permute-done.16.refs_5_ = bf16[512,256]{1,0:T(8,128)(2,1)S(1)} collective-permute-done((bf16[512,256]{1,0:T(8,128)(2,1)S(1)}, bf16[512,256]{1,0:T(8,128)(2,1)S(1)}, u32[]{:S(2)}, u32[]{:S(2)}) %collective-permute-start.16) | collective-permute-done | bytes 262176 | tf_op jit(solution)/shard_map/ppermute | solution.py:312
  59.6 1.7 %collective-permute-start.19 = (bf16[512,256]{1,0:T(8,128)(2,1)S(1)}, bf16[512,256]{1,0:T(8,128)(2,1)S(1)}, u32[]{:S(2)}, u32[]{:S(2)}) collective-permute-start(bf16[512,256]{1,0:T(8,128)(2,1)S(1)} %collective-permute-done.17.refs_6_), channel_id=1, source_target_pairs={{0,112},{16,0},{32,16},{48,32},{64,48},{80,64},{96,80},{112,96},{1... | collective-permute-start | bytes 786440 | tf_op jit(solution)/shard_map/ppermute | solution.py:312
  61.3 2.0 %attend.7 = (f32[2,512,128]{2,1,0:T(8,128)S(1)}, f32[2,512,128]{2,1,0:T(8,128)S(1)}, f32[2,512,128]{2,1,0:T(8,128)S(1)}) custom-call(s32[2]{0:T(128)S(1)} %get-tuple-element.112.refs_0_, bf16[512,256]{1,0:T(8,128)(2,1)S(1)} %project_q.1.refs_1_, s32[512,128]{1,0:T(8,128)S(1)} %get-tuple-element.120.refs_2_, s32[512,128]{1,0:T(8,128)S(1)} %get-tuple-element.121.refs_3_, ...), custom_call_target="tpu_custom_call" | custom-call | flops 1600000000 | bytes 3000000 | tf_op jit(solution)/shard_map/attend/pallas_call | solution.py:421
  63.3 2.4 %collective-permute-done.18.keys_ref.refs_5_ = bf16[512,256]{1,0:T(8,128)(2,1)S(1)} collective-permute-done((bf16[512,256]{1,0:T(8,128)(2,1)S(1)}, bf16[512,256]{1,0:T(8,128)(2,1)S(1)}, u32[]{:S(2)}, u32[]{:S(2)}) %collective-permute-start.18) | collective-permute-done | bytes 262176 | tf_op jit(solution)/shard_map/ppermute | solution.py:312
  66.4 4.6 %collective-permute-start.21 = (bf16[512,128]{1,0:T(8,128)(2,1)S(1)}, bf16[512,128]{1,0:T(8,128)(2,1)S(1)}, u32[]{:S(2)}, u32[]{:S(2)}) collective-permute-start(bf16[512,128]{1,0:T(8,128)(2,1)S(1)} %get-tuple-element.147), channel_id=1, source_target_pairs={{48,64},{64,80},{80,96},{49,65},{65,81},{81,97},{50,66},{66,82},{8... | collective-permute-start | bytes 393224 | tf_op jit(solution)/shard_map/ppermute | solution.py:470
  71.0 1.9 %collective-permute-start.22 = (bf16[512,128]{1,0:T(8,128)(2,1)S(1)}, bf16[512,128]{1,0:T(8,128)(2,1)S(1)}, u32[]{:S(2)}, u32[]{:S(2)}) collective-permute-start(bf16[512,128]{1,0:T(8,128)(2,1)S(1)} %get-tuple-element.148), channel_id=1, source_target_pairs={{80,64},{96,80},{112,96},{81,65},{97,81},{113,97},{82,66},{98,82},... | collective-permute-start | bytes 393224 | tf_op jit(solution)/shard_map/ppermute | solution.py:471
  72.9 3.6 %attend.8 = (f32[2,512,128]{2,1,0:T(8,128)S(1)}, f32[2,512,128]{2,1,0:T(8,128)S(1)}, f32[2,512,128]{2,1,0:T(8,128)S(1)}) custom-call(s32[2]{0:T(128)S(1)} %get-tuple-element.112.refs_0_, bf16[512,256]{1,0:T(8,128)(2,1)S(1)} %project_q.1.refs_1_, s32[512,128]{1,0:T(8,128)S(1)} %get-tuple-element.120.refs_2_, s32[512,128]{1,0:T(8,128)S(1)} %get-tuple-element.121.refs_3_, ...), custom_call_target="tpu_custom_call" | custom-call | flops 1600000000 | bytes 3000000 | tf_op jit(solution)/shard_map/attend/pallas_call | solution.py:421
  76.5 2.0 %collective-permute-done.22.refs_6_ = bf16[512,128]{1,0:T(8,128)(2,1)S(1)} collective-permute-done((bf16[512,128]{1,0:T(8,128)(2,1)S(1)}, bf16[512,128]{1,0:T(8,128)(2,1)S(1)}, u32[]{:S(2)}, u32[]{:S(2)}) %collective-permute-start.22) | collective-permute-done | bytes 131104 | tf_op jit(solution)/shard_map/ppermute | solution.py:471
  78.5 2.2 %attend.9 = (bf16[128,256]{1,0:T(8,128)(2,1)S(1)}, bf16[128,256]{1,0:T(8,128)(2,1)S(1)}, bf16[128,256]{1,0:T(8,128)(2,1)S(1)}, bf16[128,256]{1,0:T(8,128)(2,1)S(1)}) custom-call(s32[2]{0:T(128)S(1)} %get-tuple-element.112.refs_0_, bf16[512,256]{1,0:T(8,128)(2,1)S(1)} %project_q.1.refs_1_, s32[512,128]{1,0:T(8,128)S(1)} %get-tuple-element.120.refs_2_, ...), custom_call_target="tpu_custom_call" | custom-call | flops 800000000 | bytes 3000000 | tf_op jit(solution)/shard_map/attend/pallas_call | solution.py:421
  82.7 3.1 %collective-permute-done.24.refs_2_ = bf16[128,256]{1,0:T(8,128)(2,1)S(1)} collective-permute-done((bf16[128,256]{1,0:T(8,128)(2,1)S(1)}, bf16[128,256]{1,0:T(8,128)(2,1)S(1)}, u32[]{:S(2)}, u32[]{:S(2)}) %collective-permute-start.24) | collective-permute-done | bytes 65568 | tf_op jit(solution)/shard_map/ppermute | solution.py:41
  89.8 9.1 %collective-permute-done.28.refs_3_ = bf16[64,2688]{1,0:T(8,128)(2,1)S(1)} collective-permute-done((bf16[64,2688]{1,0:T(8,128)(2,1)S(1)}, bf16[64,2688]{1,0:T(8,128)(2,1)S(1)}, u32[]{:S(2)}, u32[]{:S(2)}) %collective-permute-start.28) | collective-permute-done | bytes 344096 | tf_op jit(solution)/shard_map/ppermute | solution.py:41
  99.9 2.2 %collective-permute-start.29 = (bf16[32,2688]{1,0:T(8,128)(2,1)S(1)}, bf16[32,2688]{1,0:T(8,128)(2,1)S(1)}, u32[]{:S(2)}, u32[]{:S(2)}) collective-permute-start(bf16[32,2688]{1,0:T(8,128)(2,1)S(1)} %get-tuple-element.171), channel_id=1, source_target_pairs={{0,6},{1,7},{2,4},{3,5},{4,2},{5,3},{6,0},{7,1},{8,14},{9,15},{10,... | collective-permute-start | bytes 516104 | tf_op jit(solution)/shard_map/ppermute | solution.py:41
  102.2 4.5 %collective-permute-done.29.refs_2_ = bf16[32,2688]{1,0:T(8,128)(2,1)S(1)} collective-permute-done((bf16[32,2688]{1,0:T(8,128)(2,1)S(1)}, bf16[32,2688]{1,0:T(8,128)(2,1)S(1)}, u32[]{:S(2)}, u32[]{:S(2)}) %collective-permute-start.29) | collective-permute-done | bytes 172064 | tf_op jit(solution)/shard_map/ppermute | solution.py:41
  (78 shorter events, 39.2 us)
Async XLA Ops:
  0.0 20.3 %collective-permute-start.6 = (bf16[256,5376]{1,0:T(8,128)(2,1)}, bf16[256,5376]{1,0:T(8,128)(2,1)S(1)}, u32[]{:S(2)}, u32[]{:S(2)}) collective-permute-start(bf16[256,5376]{1,0:T(8,128)(2,1)} %refs_4_.3), channel_id=1, source_target_pairs={{0,1},{1,0},{2,3},{3,2},{4,5},{5,4},{6,7},{7,6},{8,9},{9,8},{10,11... | collective-permute-start | bytes 8257544 | tf_op jit(solution)/shard_map/ppermute | solution.py:41
  2.2 5.6 %collective-permute-start = (bf16[32,1792]{1,0:T(8,128)(2,1)S(1)}, bf16[32,1792]{1,0:T(8,128)(2,1)S(1)}, u32[]{:S(2)}, u32[]{:S(2)}) collective-permute-start(bf16[32,1792]{1,0:T(8,128)(2,1)S(1)} %get-tuple-element.89.refs_0_), channel_id=1, source_target_pairs={{0,2},{1,3},{2,0},{3,1},{4,6},{5,7},{6,4},{7,5},{8,10},{9,11},{10,... | collective-permute-start | bytes 344072 | tf_op jit(solution)/shard_map/ppermute | solution.py:41
  3.8 6.4 %collective-permute-start.1 = (bf16[32,1792]{1,0:T(8,128)(2,1)S(1)}, bf16[32,1792]{1,0:T(8,128)(2,1)S(1)}, u32[]{:S(2)}, u32[]{:S(2)}) collective-permute-start(bf16[32,1792]{1,0:T(8,128)(2,1)S(1)} %get-tuple-element.90.refs_1_), channel_id=1, source_target_pairs={{0,6},{1,7},{2,4},{3,5},{4,2},{5,3},{6,0},{7,1},{8,14},{9,15},{10,... | collective-permute-start | bytes 344072 | tf_op jit(solution)/shard_map/ppermute | solution.py:41
  10.9 7.8 %collective-permute-start.3 = (bf16[64,1792]{1,0:T(8,128)(2,1)S(1)}, bf16[64,1792]{1,0:T(8,128)(2,1)S(1)}, u32[]{:S(2)}, u32[]{:S(2)}) collective-permute-start(bf16[64,1792]{1,0:T(8,128)(2,1)S(1)} %get-tuple-element.92.refs_0_), channel_id=1, source_target_pairs={{0,6},{1,7},{2,4},{3,5},{4,2},{5,3},{6,0},{7,1},{8,14},{9,15},{10,... | collective-permute-start | bytes 688136 | tf_op jit(solution)/shard_map/ppermute | solution.py:41
  12.4 6.5 %collective-permute-start.4 = (bf16[64,1792]{1,0:T(8,128)(2,1)S(1)}, bf16[64,1792]{1,0:T(8,128)(2,1)S(1)}, u32[]{:S(2)}, u32[]{:S(2)}) collective-permute-start(bf16[64,1792]{1,0:T(8,128)(2,1)S(1)} %get-tuple-element.93.refs_1_), channel_id=1, source_target_pairs={{0,8},{1,9},{2,10},{3,11},{4,12},{5,13},{6,14},{7,15},{8,0},{9,1},... | collective-permute-start | bytes 688136 | tf_op jit(solution)/shard_map/ppermute | solution.py:41
  14.0 6.3 %collective-permute-start.5 = (bf16[64,1792]{1,0:T(8,128)(2,1)S(1)}, bf16[64,1792]{1,0:T(8,128)(2,1)S(1)}, u32[]{:S(2)}, u32[]{:S(2)}) collective-permute-start(bf16[64,1792]{1,0:T(8,128)(2,1)S(1)} %get-tuple-element.94.refs_2_), channel_id=1, source_target_pairs={{0,2},{1,3},{2,0},{3,1},{4,6},{5,7},{6,4},{7,5},{8,10},{9,11},{10,... | collective-permute-start | bytes 688136 | tf_op jit(solution)/shard_map/ppermute | solution.py:41
  20.5 10.3 %collective-permute-start.7 = (bf16[128,1792]{1,0:T(8,128)(2,1)S(1)}, bf16[128,1792]{1,0:T(8,128)(2,1)S(1)}, u32[]{:S(2)}, u32[]{:S(2)}) collective-permute-start(bf16[128,1792]{1,0:T(8,128)(2,1)S(1)} %get-tuple-element.98.refs_0_), channel_id=1, source_target_pairs={{0,8},{1,9},{2,10},{3,11},{4,12},{5,13},{6,14},{7,15},{8,0},{9,1},... | collective-permute-start | bytes 1376264 | tf_op jit(solution)/shard_map/ppermute | solution.py:41
  21.0 10.1 %collective-permute-start.8 = (bf16[128,1792]{1,0:T(8,128)(2,1)S(1)}, bf16[128,1792]{1,0:T(8,128)(2,1)S(1)}, u32[]{:S(2)}, u32[]{:S(2)}) collective-permute-start(bf16[128,1792]{1,0:T(8,128)(2,1)S(1)} %get-tuple-element.99.refs_1_), channel_id=1, source_target_pairs={{0,2},{1,3},{2,0},{3,1},{4,6},{5,7},{6,4},{7,5},{8,10},{9,11},{10,... | collective-permute-start | bytes 1376264 | tf_op jit(solution)/shard_map/ppermute | solution.py:41
  21.3 11.2 %collective-permute-start.9 = (bf16[128,1792]{1,0:T(8,128)(2,1)S(1)}, bf16[128,1792]{1,0:T(8,128)(2,1)S(1)}, u32[]{:S(2)}, u32[]{:S(2)}) collective-permute-start(bf16[128,1792]{1,0:T(8,128)(2,1)S(1)} %get-tuple-element.100.refs_2_), channel_id=1, source_target_pairs={{0,6},{1,7},{2,4},{3,5},{4,2},{5,3},{6,0},{7,1},{8,14},{9,15},{10,... | collective-permute-start | bytes 1376264 | tf_op jit(solution)/shard_map/ppermute | solution.py:41
  32.5 33.8 %collective-permute-start.20 = (bf16[256,5376]{1,0:T(8,128)(2,1)S(1)}, bf16[256,5376]{1,0:T(8,128)(2,1)S(1)}, u32[]{:S(2)}, u32[]{:S(2)}) collective-permute-start(bf16[256,5376]{1,0:T(8,128)(2,1)S(1)} %collective-permute-done.6.refs_5_), channel_id=1, source_target_pairs={{0,8},{1,137},{2,10},{3,139},{4,12},{5,141},{6,14},{7,143},{8,0},{... | collective-permute-start | bytes 8257544 | tf_op jit(solution)/shard_map/ppermute | solution.py:45
  34.1 5.1 %collective-permute-start.10 = (bf16[3,128,1792]{2,1,0:T(8,128)(2,1)S(1)}, bf16[3,128,1792]{2,1,0:T(8,128)(2,1)S(1)}, u32[]{:S(2)}, u32[]{:S(2)}) collective-permute-start(bf16[3,128,1792]{2,1,0:T(8,128)(2,1)S(1)} %get-tuple-element.116), channel_id=1, source_target_pairs={{0,1},{1,0},{2,3},{3,2},{4,5},{5,4},{6,7},{7,6},{8,9},{9,8},{10,11... | collective-permute-start | bytes 4128776 | tf_op jit(solution)/shard_map/ppermute | solution.py:41
  41.2 8.6 %collective-permute-start.15 = (bf16[512,256]{1,0:T(8,128)(2,1)S(1)}, bf16[512,256]{1,0:T(8,128)(2,1)S(1)}, u32[]{:S(2)}, u32[]{:S(2)}) collective-permute-start(bf16[512,256]{1,0:T(8,128)(2,1)S(1)} %project_kv.1.refs_5_), channel_id=1, source_target_pairs={{0,112},{16,0},{32,16},{48,32},{64,48},{80,64},{96,80},{112,96},{1... | collective-permute-start | bytes 786440 | tf_op jit(solution)/shard_map/ppermute | solution.py:312
  42.4 8.1 %collective-permute-start.14 = (bf16[512,256]{1,0:T(8,128)(2,1)S(1)}, bf16[512,256]{1,0:T(8,128)(2,1)S(1)}, u32[]{:S(2)}, u32[]{:S(2)}) collective-permute-start(bf16[512,256]{1,0:T(8,128)(2,1)S(1)} %project_kv.1.refs_5_), channel_id=1, source_target_pairs={{0,16},{16,32},{32,48},{48,64},{64,80},{80,96},{96,112},{112,0},{1... | collective-permute-start | bytes 786440 | tf_op jit(solution)/shard_map/ppermute | solution.py:312
  50.5 7.2 %collective-permute-start.17 = (bf16[512,256]{1,0:T(8,128)(2,1)S(1)}, bf16[512,256]{1,0:T(8,128)(2,1)S(1)}, u32[]{:S(2)}, u32[]{:S(2)}) collective-permute-start(bf16[512,256]{1,0:T(8,128)(2,1)S(1)} %collective-permute-done.15), channel_id=1, source_target_pairs={{0,112},{16,0},{32,16},{48,32},{64,48},{80,64},{96,80},{112,96},{1... | collective-permute-start | bytes 786440 | tf_op jit(solution)/shard_map/ppermute | solution.py:312
  52.1 7.2 %collective-permute-start.16 = (bf16[512,256]{1,0:T(8,128)(2,1)S(1)}, bf16[512,256]{1,0:T(8,128)(2,1)S(1)}, u32[]{:S(2)}, u32[]{:S(2)}) collective-permute-start(bf16[512,256]{1,0:T(8,128)(2,1)S(1)} %collective-permute-done.14.refs_5_), channel_id=1, source_target_pairs={{0,16},{16,32},{32,48},{48,64},{64,80},{80,96},{96,112},{112,0},{1... | collective-permute-start | bytes 786440 | tf_op jit(solution)/shard_map/ppermute | solution.py:312
  59.3 6.4 %collective-permute-start.18 = (bf16[512,256]{1,0:T(8,128)(2,1)S(1)}, bf16[512,256]{1,0:T(8,128)(2,1)S(1)}, u32[]{:S(2)}, u32[]{:S(2)}) collective-permute-start(bf16[512,256]{1,0:T(8,128)(2,1)S(1)} %collective-permute-done.16.refs_5_), channel_id=1, source_target_pairs={{0,16},{16,32},{32,48},{48,64},{64,80},{80,96},{96,112},{112,0},{1... | collective-permute-start | bytes 786440 | tf_op jit(solution)/shard_map/ppermute | solution.py:312
  59.6 6.7 %collective-permute-start.19 = (bf16[512,256]{1,0:T(8,128)(2,1)S(1)}, bf16[512,256]{1,0:T(8,128)(2,1)S(1)}, u32[]{:S(2)}, u32[]{:S(2)}) collective-permute-start(bf16[512,256]{1,0:T(8,128)(2,1)S(1)} %collective-permute-done.17.refs_6_), channel_id=1, source_target_pairs={{0,112},{16,0},{32,16},{48,32},{64,48},{80,64},{96,80},{112,96},{1... | collective-permute-start | bytes 786440 | tf_op jit(solution)/shard_map/ppermute | solution.py:312
  66.3 19.9 %collective-permute-start.26 = (bf16[256,5376]{1,0:T(8,128)(2,1)S(1)}, bf16[256,5376]{1,0:T(8,128)(2,1)S(1)}, u32[]{:S(2)}, u32[]{:S(2)}) collective-permute-start(bf16[256,5376]{1,0:T(8,128)(2,1)S(1)} %collective-permute-done.20.refs_7_), channel_id=1, source_target_pairs={{0,1},{1,0},{2,3},{3,2},{4,5},{5,4},{6,7},{7,6},{8,9},{9,8},{10,11... | collective-permute-start | bytes 8257544 | tf_op jit(solution)/shard_map/ppermute | solution.py:41
  66.4 10.2 %collective-permute-start.21 = (bf16[512,128]{1,0:T(8,128)(2,1)S(1)}, bf16[512,128]{1,0:T(8,128)(2,1)S(1)}, u32[]{:S(2)}, u32[]{:S(2)}) collective-permute-start(bf16[512,128]{1,0:T(8,128)(2,1)S(1)} %get-tuple-element.147), channel_id=1, source_target_pairs={{48,64},{64,80},{80,96},{49,65},{65,81},{81,97},{50,66},{66,82},{8... | collective-permute-start | bytes 393224 | tf_op jit(solution)/shard_map/ppermute | solution.py:470
  71.0 7.5 %collective-permute-start.22 = (bf16[512,128]{1,0:T(8,128)(2,1)S(1)}, bf16[512,128]{1,0:T(8,128)(2,1)S(1)}, u32[]{:S(2)}, u32[]{:S(2)}) collective-permute-start(bf16[512,128]{1,0:T(8,128)(2,1)S(1)} %get-tuple-element.148), channel_id=1, source_target_pairs={{80,64},{96,80},{112,96},{81,65},{97,81},{113,97},{82,66},{98,82},... | collective-permute-start | bytes 393224 | tf_op jit(solution)/shard_map/ppermute | solution.py:471
  87.4 11.6 %collective-permute-start.28 = (bf16[64,2688]{1,0:T(8,128)(2,1)S(1)}, bf16[64,2688]{1,0:T(8,128)(2,1)S(1)}, u32[]{:S(2)}, u32[]{:S(2)}) collective-permute-start(bf16[64,2688]{1,0:T(8,128)(2,1)S(1)} %get-tuple-element.168), channel_id=1, source_target_pairs={{0,6},{1,7},{2,4},{3,5},{4,2},{5,3},{6,0},{7,1},{8,14},{9,15},{10,... | collective-permute-start | bytes 1032200 | tf_op jit(solution)/shard_map/ppermute | solution.py:41
  89.7 10.1 %collective-permute-start.27 = (bf16[64,2688]{1,0:T(8,128)(2,1)S(1)}, bf16[64,2688]{1,0:T(8,128)(2,1)S(1)}, u32[]{:S(2)}, u32[]{:S(2)}) collective-permute-start(bf16[64,2688]{1,0:T(8,128)(2,1)S(1)} %get-tuple-element.167), channel_id=1, source_target_pairs={{0,2},{1,3},{2,0},{3,1},{4,6},{5,7},{6,4},{7,5},{8,10},{9,11},{10,... | collective-permute-start | bytes 1032200 | tf_op jit(solution)/shard_map/ppermute | solution.py:41
  99.9 6.7 %collective-permute-start.29 = (bf16[32,2688]{1,0:T(8,128)(2,1)S(1)}, bf16[32,2688]{1,0:T(8,128)(2,1)S(1)}, u32[]{:S(2)}, u32[]{:S(2)}) collective-permute-start(bf16[32,2688]{1,0:T(8,128)(2,1)S(1)} %get-tuple-element.171), channel_id=1, source_target_pairs={{0,6},{1,7},{2,4},{3,5},{4,2},{5,3},{6,0},{7,1},{8,14},{9,15},{10,... | collective-permute-start | bytes 516104 | tf_op jit(solution)/shard_map/ppermute | solution.py:41
  102.2 5.4 %collective-permute-start.30 = (bf16[32,2688]{1,0:T(8,128)(2,1)S(1)}, bf16[32,2688]{1,0:T(8,128)(2,1)S(1)}, u32[]{:S(2)}, u32[]{:S(2)}) collective-permute-start(bf16[32,2688]{1,0:T(8,128)(2,1)S(1)} %get-tuple-element.172), channel_id=1, source_target_pairs={{0,2},{1,3},{2,0},{3,1},{4,6},{5,7},{6,4},{7,5},{8,10},{9,11},{10,... | collective-permute-start | bytes 516104 | tf_op jit(solution)/shard_map/ppermute | solution.py:41
  (19 other events, 117.1 us)

commit v5 on v4

--- a/solution.py
+++ b/solution.py
@@ -244,8 +244,8 @@
     other = swap(packed, CC)
     tables = make_tables(document_start, *small)
     other_late = [swap(late[p], CC) for p in range(3)]
-    held = lax.optimization_barrier((*late, *tables, core_weight))
-    late, tables, core_weight = held[0:3], held[3:12], held[12]
+    held = lax.optimization_barrier((*late, *tables, core_weight, other))
+    late, tables, core_weight, other = held[0:3], held[3:12], held[12], held[13]
     both_weight = swap_y_both_ways(core_weight)
     return (four, late, other, other_late), tables, core_weight, both_weight
 
@@ -257,15 +257,15 @@
     return (scaled * cosine + turned * sine).astype(jnp.bfloat16)
 
 
-def project_kernel(both, *refs):
-    x_refs = refs[0:10]
-    w_ref, gain_ref, cos_ref, sin_ref, out_ref = refs[10:]
-    four, late, other, other_late = x_refs[0:3], x_refs[3:6], x_refs[6], x_refs[7:10]
+def projected(x_refs, w_ref, cores):
+    four, late = x_refs[0:3], x_refs[3:6]
+    if 1 in cores:
+        other, other_late = x_refs[6], x_refs[7:10]
     total = None
     for part in range(3):
         order = gathered_order(part)
         rows = []
-        for core in range(2):
+        for core in cores:
             for place in range(8):
                 k = order.index(place)
                 at = (k % 4) * ROWS
@@ -281,27 +281,65 @@
             preferred_element_type=jnp.float32,
         )
         total = product if part == 0 else total + product
+    return total
+
+
+def query_kernel(*refs):
+    w_ref, gain_ref, cos_ref, sin_ref, out_ref = refs[10:]
+    total = projected(refs[0:10], w_ref, (0, 1))
     gain = gain_ref[...]
-    out_ref[:, 0:HD] = rotate(total[:, 0:HD], gain, cos_ref[...], sin_ref[...])
-    if both:
-        out_ref[:, HD : 2 * HD] = rotate(total[:, HD : 2 * HD], gain, cos_ref[...], sin_ref[...])
-    else:
-        out_ref[:, HD : 2 * HD] = total[:, HD : 2 * HD].astype(jnp.bfloat16)
-
-
-def project(pieces, weight, gain, cosine, sine, both, name):
-    four, late, other, other_late = pieces
-    return pl.pallas_call(
-        functools.partial(project_kernel, both),
-        out_shape=shape(BLOCK, 2 * HD),
-        in_specs=whole(14),
+    for head in range(2):
+        here = slice(head * HD, (head + 1) * HD)
+        out_ref[:, here] = rotate(total[:, here], gain, cos_ref[...], sin_ref[...])
+
+
+def key_value_kernel(core, *refs):
+    count = 10 if core else 6
+    w_ref, gain_ref, cos_ref, sin_ref = refs[count : count + 4]
+    out_ref = refs[-1]
+    total = projected(refs[0:count], w_ref, (core,))
+    table = slice(core * 256, (core + 1) * 256)
+    here = table if core else slice(0, 256)
+    if core:
+        out_ref[0:256] = refs[count + 4][...]
+    out_ref[here, 0:HD] = rotate(
+        total[:, 0:HD], gain_ref[...], cos_ref[table], sin_ref[table]
+    )
+    out_ref[here, HD : 2 * HD] = total[:, HD : 2 * HD].astype(jnp.bfloat16)
+
+
+def project_call(kernel, rows, flops, name, *operands):
+    return pl.pallas_call(
+        kernel,
+        out_shape=shape(rows, 2 * HD),
+        in_specs=whole(len(operands)),
         out_specs=whole(1)[0],
         compiler_params=params(14),
-        cost_estimate=pl.CostEstimate(
-            flops=2 * BLOCK * D * 2 * HD, bytes_accessed=9000000, transcendentals=0
-        ),
+        cost_estimate=pl.CostEstimate(flops=flops, bytes_accessed=9000000, transcendentals=0),
         name=name,
-    )(*four, *late, other, *other_late, weight, gain, cosine, sine)
+    )(*operands)
+
+
+def project_query(pieces, weight, gain, cosine, sine):
+    four, late, other, other_late = pieces
+    flops = 2 * BLOCK * D * 2 * HD
+    return project_call(
+        query_kernel, BLOCK, flops, "project_q",
+        *four, *late, other, *other_late, weight, gain, cosine, sine,
+    )
+
+
+def project_key_value(pieces, weight, gain, cosine, sine):
+    four, late, other, other_late = pieces
+    flops = BLOCK * D * 2 * HD
+    mine = project_call(
+        functools.partial(key_value_kernel, 0), 256, flops, "project_kv_mine",
+        *four, *late, weight, gain, cosine, sine,
+    )
+    return project_call(
+        functools.partial(key_value_kernel, 1), BLOCK, flops, "project_kv",
+        *four, *late, other, *other_late, weight, gain, cosine, sine, mine,
+    )
 
 
 NEG = -1e30
@@ -601,10 +639,10 @@
         value_weight,
     )
     cosine, sine, position, start, offset, query_gain, key_gain, pair_weight, where = made
-    rows = project(pieces, pair_weight, key_gain, cosine, sine, False, "project_kv")
+    rows = project_key_value(pieces, pair_weight, key_gain, cosine, sine)
     parts, weights = share_and_attend(
         rows,
-        lambda: project(pieces, query_weight, query_gain, cosine, sine, True, "project_q"),
+        lambda: project_query(pieces, query_weight, query_gain, cosine, sine),
         (where, position, start, offset),
         output_weight,
         core_weight,

time: 109 us -> 109 us (level)
  waiting for transfers between devices: 48.2 us -> 50.7 us
  Pallas kernels: 22.8 us -> 21.4 us
  starting transfers between devices: 31.6 us -> 30.5 us
    ppermute x1, waiting for transfers between devices: 0.01 us -> 2.27 us  [swap_y_both_ways(): lax.ppermute(value, ('docs', 'mp'), [(d * 16 + m, (d ^ m & 1) * 16 + (m ^...]
    ppermute x1, starting transfers between devices: 4.64 us -> 2.93 us  [share_and_attend(): key_far = lax.ppermute(key_half, 'ctx', [(3, 4), (4, 5), (5, 6)])]
    pallas_call x5, Pallas kernels: 11.6 us -> 10.2 us  [attend(): pl.pallas_call(functools.partial(attend_kernel, distances, joint, first,...]
    pallas_call x2 -> x3, Pallas kernels: 4.35 us -> 4.42 us  [project_call(): pl.pallas_call(kernel, out_shape=shape(rows, 2 * HD), in_specs=whole(len(...]
  transfers between devices with their start and end apart: 31 -> 31, of which waited for: 25 -> 26; matrix products, arithmetic and copies ran while one was open for 0% -> 0% of each run, Pallas kernels for 19% -> 17%
where the time goes in v5:
time: 109 us
  waiting for transfers between devices  50.7 us (47%)
  starting transfers between devices  30.5 us (28%)
  Pallas kernels  21.4 us (20%)
  local copies, waits for them, and re-layouts  5.83 us (5%)
    ppermute x22, waiting for transfers between devices, swap(): return lax.ppermute(value, 'mp', [(m, m ^ link) for m in range(16)])  35.4 us
    ppermute x22, starting transfers between devices, swap(): return lax.ppermute(value, 'mp', [(m, m ^ link) for m in range(16)])  16.9 us
    ppermute x6, waiting for transfers between devices, move(): return lax.ppermute(value, 'ctx', [(c, (c + step) % 8) for c in range(8)])  10.4 us
    pallas_call x5, Pallas kernels, attend(): pl.pallas_call(functools.partial(attend_kernel, distances, joint, first,...  10.2 us
    ppermute x6, starting transfers between devices, move(): return lax.ppermute(value, 'ctx', [(c, (c + step) % 8) for c in range(8)])  6.15 us
    unnamed x24, local copies, waits for them, and re-layouts  5.83 us
    pallas_call x3, Pallas kernels, project_call(): pl.pallas_call(kernel, out_shape=shape(rows, 2 * HD), in_specs=whole(len(...  4.42 us
    ppermute x1, starting transfers between devices, share_and_attend(): key_far = lax.ppermute(key_half, 'ctx', [(3, 4), (4, 5), (5, 6)])  2.93 us
  transfers between devices with their start and end apart: 31, of which 26 were waited for; matrix products, arithmetic and copies ran while one was open for 0% of the time, Pallas kernels for 17%

profile of v5, /device:TPU:160, one launch (start us, length us, event | category | flops | bytes accessed | tf_op | source)
XLA Modules:
  0.0 108.6 jit_solution(5082884069375638105)
XLA Ops:
  3.8 2.1 %collective-permute-start.1 = (bf16[32,1792]{1,0:T(8,128)(2,1)S(1)}, bf16[32,1792]{1,0:T(8,128)(2,1)S(1)}, u32[]{:S(2)}, u32[]{:S(2)}) collective-permute-start(bf16[32,1792]{1,0:T(8,128)(2,1)S(1)} %get-tuple-element.91.refs_1_), channel_id=1, source_target_pairs={{0,6},{1,7},{2,4},{3,5},{4,2},{5,3},{6,0},{7,1},{8,14},{9,15},{10,... | collective-permute-start | bytes 344072 | tf_op jit(solution)/shard_map/ppermute | solution.py:41
  7.8 2.4 %collective-permute-done.1.refs_4_ = bf16[32,1792]{1,0:T(8,128)(2,1)S(1)} collective-permute-done((bf16[32,1792]{1,0:T(8,128)(2,1)S(1)}, bf16[32,1792]{1,0:T(8,128)(2,1)S(1)}, u32[]{:S(2)}, u32[]{:S(2)}) %collective-permute-start.1) | collective-permute-done | bytes 114720 | tf_op jit(solution)/shard_map/ppermute | solution.py:41
  14.0 4.6 %collective-permute-done.3.refs_3_ = bf16[64,1792]{1,0:T(8,128)(2,1)S(1)} collective-permute-done((bf16[64,1792]{1,0:T(8,128)(2,1)S(1)}, bf16[64,1792]{1,0:T(8,128)(2,1)S(1)}, u32[]{:S(2)}, u32[]{:S(2)}) %collective-permute-start.3) | collective-permute-done | bytes 229408 | tf_op jit(solution)/shard_map/ppermute | solution.py:41
  26.8 2.8 %tables.1 = (f32[512,128]{1,0:T(8,128)S(1)}, f32[512,128]{1,0:T(8,128)S(1)}, s32[512,128]{1,0:T(8,128)S(1)}, s32[512,128]{1,0:T(8,128)S(1)}, s32[1,512]{1,0:T(1,...) custom-call(s32[4,128]{1,0:T(4,128)S(1)} %bitcast.7, ...), custom_call_target="tpu_custom_call" | custom-call | flops 4000000 | bytes 1000000 | tf_op jit(solution)/shard_map/tables/pallas_call | solution.py:171
  29.6 3.9 %collective-permute-done.7.refs_3_ = bf16[128,1792]{1,0:T(8,128)(2,1)S(1)} collective-permute-done((bf16[128,1792]{1,0:T(8,128)(2,1)S(1)}, bf16[128,1792]{1,0:T(8,128)(2,1)S(1)}, u32[]{:S(2)}, u32[]{:S(2)}) %collective-permute-start.7) | collective-permute-done | bytes 458784 | tf_op jit(solution)/shard_map/ppermute | solution.py:41
  42.8 2.3 %project_q.1.refs_1_ = bf16[512,256]{1,0:T(8,128)(2,1)S(1)} custom-call(bf16[128,1792]{1,0:T(8,128)(2,1)S(1)} %get-tuple-element.99.refs_0_, bf16[128,1792]{1,0:T(8,128)(2,1)S(1)} %get-tuple-element.100.refs_1_, bf16[128,1792]{1,0:T(8,128)(2,1)S(1)} %get-tuple-element.101.refs_2_, bf16[128,1792]{1,0:T(8,128)(2,1)S(1)} %collective-permute-done.7.refs_3_, ...), custom_call_target="tpu_custom_call" | custom-call | flops 1409286144 | bytes 9000000 | tf_op jit(solution)/shard_map/project_q/pallas_call | solution.py:312
  45.1 2.0 %attend.5 = (f32[2,512,128]{2,1,0:T(8,128)S(1)}, f32[2,512,128]{2,1,0:T(8,128)S(1)}, f32[2,512,128]{2,1,0:T(8,128)S(1)}) custom-call(s32[2]{0:T(128)S(1)} %get-tuple-element.114.refs_0_, bf16[512,256]{1,0:T(8,128)(2,1)S(1)} %project_q.1.refs_1_, s32[512,128]{1,0:T(8,128)S(1)} %get-tuple-element.122.refs_2_, s32[512,128]{1,0:T(8,128)S(1)} %get-tuple-element.123.refs_3_, ...), custom_call_target="tpu_custom_call" | custom-call | flops 800000000 | bytes 3000000 | tf_op jit(solution)/shard_map/attend/pallas_call | solution.py:459
  47.1 2.0 %collective-permute-done.15 = bf16[512,256]{1,0:T(8,128)(2,1)S(1)} collective-permute-done((bf16[512,256]{1,0:T(8,128)(2,1)S(1)}, bf16[512,256]{1,0:T(8,128)(2,1)S(1)}, u32[]{:S(2)}, u32[]{:S(2)}) %collective-permute-start.15) | collective-permute-done | bytes 262176 | tf_op jit(solution)/shard_map/ppermute | solution.py:350
  51.9 1.9 %attend.6 = (f32[2,512,128]{2,1,0:T(8,128)S(1)}, f32[2,512,128]{2,1,0:T(8,128)S(1)}, f32[2,512,128]{2,1,0:T(8,128)S(1)}) custom-call(s32[2]{0:T(128)S(1)} %get-tuple-element.114.refs_0_, bf16[512,256]{1,0:T(8,128)(2,1)S(1)} %project_q.1.refs_1_, s32[512,128]{1,0:T(8,128)S(1)} %get-tuple-element.122.refs_2_, s32[512,128]{1,0:T(8,128)S(1)} %get-tuple-element.123.refs_3_, ...), custom_call_target="tpu_custom_call" | custom-call | flops 800000000 | bytes 3000000 | tf_op jit(solution)/shard_map/attend/pallas_call | solution.py:459
  53.8 3.3 %collective-permute-done.17.refs_6_ = bf16[512,256]{1,0:T(8,128)(2,1)S(1)} collective-permute-done((bf16[512,256]{1,0:T(8,128)(2,1)S(1)}, bf16[512,256]{1,0:T(8,128)(2,1)S(1)}, u32[]{:S(2)}, u32[]{:S(2)}) %collective-permute-start.17) | collective-permute-done | bytes 262176 | tf_op jit(solution)/shard_map/ppermute | solution.py:350
  58.9 1.7 %collective-permute-start.19 = (bf16[512,256]{1,0:T(8,128)(2,1)S(1)}, bf16[512,256]{1,0:T(8,128)(2,1)S(1)}, u32[]{:S(2)}, u32[]{:S(2)}) collective-permute-start(bf16[512,256]{1,0:T(8,128)(2,1)S(1)} %collective-permute-done.17.refs_6_), channel_id=1, source_target_pairs={{0,112},{16,0},{32,16},{48,32},{64,48},{80,64},{96,80},{112,96},{1... | collective-permute-start | bytes 786440 | tf_op jit(solution)/shard_map/ppermute | solution.py:350
  60.7 2.2 %attend.7 = (f32[2,512,128]{2,1,0:T(8,128)S(1)}, f32[2,512,128]{2,1,0:T(8,128)S(1)}, f32[2,512,128]{2,1,0:T(8,128)S(1)}) custom-call(s32[2]{0:T(128)S(1)} %get-tuple-element.114.refs_0_, bf16[512,256]{1,0:T(8,128)(2,1)S(1)} %project_q.1.refs_1_, s32[512,128]{1,0:T(8,128)S(1)} %get-tuple-element.122.refs_2_, s32[512,128]{1,0:T(8,128)S(1)} %get-tuple-element.123.refs_3_, ...), custom_call_target="tpu_custom_call" | custom-call | flops 1600000000 | bytes 3000000 | tf_op jit(solution)/shard_map/attend/pallas_call | solution.py:459
  62.9 2.2 %collective-permute-done.18.keys_ref.refs_5_ = bf16[512,256]{1,0:T(8,128)(2,1)S(1)} collective-permute-done((bf16[512,256]{1,0:T(8,128)(2,1)S(1)}, bf16[512,256]{1,0:T(8,128)(2,1)S(1)}, u32[]{:S(2)}, u32[]{:S(2)}) %collective-permute-start.18) | collective-permute-done | bytes 262176 | tf_op jit(solution)/shard_map/ppermute | solution.py:350
  65.7 2.3 %collective-permute-done.20.refs_7_ = bf16[256,5376]{1,0:T(8,128)(2,1)S(1)} collective-permute-done((bf16[256,5376]{1,0:T(8,128)(2,1)S(1)}, bf16[256,5376]{1,0:T(8,128)(2,1)S(1)}, u32[]{:S(2)}, u32[]{:S(2)}) %collective-permute-start.20) | collective-permute-done | bytes 2752544 | tf_op jit(solution)/shard_map/ppermute | solution.py:45
  68.0 2.9 %collective-permute-start.21 = (bf16[512,128]{1,0:T(8,128)(2,1)S(1)}, bf16[512,128]{1,0:T(8,128)(2,1)S(1)}, u32[]{:S(2)}, u32[]{:S(2)}) collective-permute-start(bf16[512,128]{1,0:T(8,128)(2,1)S(1)} %get-tuple-element.149), channel_id=1, source_target_pairs={{48,64},{64,80},{80,96},{49,65},{65,81},{81,97},{50,66},{66,82},{8... | collective-permute-start | bytes 393224 | tf_op jit(solution)/shard_map/ppermute | solution.py:508
  70.9 2.9 %collective-permute-start.22 = (bf16[512,128]{1,0:T(8,128)(2,1)S(1)}, bf16[512,128]{1,0:T(8,128)(2,1)S(1)}, u32[]{:S(2)}, u32[]{:S(2)}) collective-permute-start(bf16[512,128]{1,0:T(8,128)(2,1)S(1)} %get-tuple-element.150), channel_id=1, source_target_pairs={{80,64},{96,80},{112,96},{81,65},{97,81},{113,97},{82,66},{98,82},... | collective-permute-start | bytes 393224 | tf_op jit(solution)/shard_map/ppermute | solution.py:509
  73.9 2.0 %attend.8 = (f32[2,512,128]{2,1,0:T(8,128)S(1)}, f32[2,512,128]{2,1,0:T(8,128)S(1)}, f32[2,512,128]{2,1,0:T(8,128)S(1)}) custom-call(s32[2]{0:T(128)S(1)} %get-tuple-element.114.refs_0_, bf16[512,256]{1,0:T(8,128)(2,1)S(1)} %project_q.1.refs_1_, s32[512,128]{1,0:T(8,128)S(1)} %get-tuple-element.122.refs_2_, s32[512,128]{1,0:T(8,128)S(1)} %get-tuple-element.123.refs_3_, ...), custom_call_target="tpu_custom_call" | custom-call | flops 1600000000 | bytes 3000000 | tf_op jit(solution)/shard_map/attend/pallas_call | solution.py:459
  75.9 2.6 %collective-permute-done.22.refs_6_ = bf16[512,128]{1,0:T(8,128)(2,1)S(1)} collective-permute-done((bf16[512,128]{1,0:T(8,128)(2,1)S(1)}, bf16[512,128]{1,0:T(8,128)(2,1)S(1)}, u32[]{:S(2)}, u32[]{:S(2)}) %collective-permute-start.22) | collective-permute-done | bytes 131104 | tf_op jit(solution)/shard_map/ppermute | solution.py:509
  78.5 2.2 %attend.9 = (bf16[128,256]{1,0:T(8,128)(2,1)S(1)}, bf16[128,256]{1,0:T(8,128)(2,1)S(1)}, bf16[128,256]{1,0:T(8,128)(2,1)S(1)}, bf16[128,256]{1,0:T(8,128)(2,1)S(1)}) custom-call(s32[2]{0:T(128)S(1)} %get-tuple-element.114.refs_0_, bf16[512,256]{1,0:T(8,128)(2,1)S(1)} %project_q.1.refs_1_, s32[512,128]{1,0:T(8,128)S(1)} %get-tuple-element.122.refs_2_, ...), custom_call_target="tpu_custom_call" | custom-call | flops 800000000 | bytes 3000000 | tf_op jit(solution)/shard_map/attend/pallas_call | solution.py:459
  80.7 1.7 %collective-permute-start.24 = (bf16[128,256]{1,0:T(8,128)(2,1)S(1)}, bf16[128,256]{1,0:T(8,128)(2,1)S(1)}, u32[]{:S(2)}, u32[]{:S(2)}) collective-permute-start(bf16[128,256]{1,0:T(8,128)(2,1)S(1)} %get-tuple-element.164), channel_id=1, source_target_pairs={{0,8},{1,9},{2,10},{3,11},{4,12},{5,13},{6,14},{7,15},{8,0},{9,1},... | collective-permute-start | bytes 196616 | tf_op jit(solution)/shard_map/ppermute | solution.py:41
  82.6 2.6 %collective-permute-done.24.refs_2_ = bf16[128,256]{1,0:T(8,128)(2,1)S(1)} collective-permute-done((bf16[128,256]{1,0:T(8,128)(2,1)S(1)}, bf16[128,256]{1,0:T(8,128)(2,1)S(1)}, u32[]{:S(2)}, u32[]{:S(2)}) %collective-permute-start.24) | collective-permute-done | bytes 65568 | tf_op jit(solution)/shard_map/ppermute | solution.py:41
  90.4 8.6 %collective-permute-done.28.refs_3_ = bf16[64,2688]{1,0:T(8,128)(2,1)S(1)} collective-permute-done((bf16[64,2688]{1,0:T(8,128)(2,1)S(1)}, bf16[64,2688]{1,0:T(8,128)(2,1)S(1)}, u32[]{:S(2)}, u32[]{:S(2)}) %collective-permute-start.28) | collective-permute-done | bytes 344096 | tf_op jit(solution)/shard_map/ppermute | solution.py:41
  100.4 1.8 %collective-permute-start.29 = (bf16[32,2688]{1,0:T(8,128)(2,1)S(1)}, bf16[32,2688]{1,0:T(8,128)(2,1)S(1)}, u32[]{:S(2)}, u32[]{:S(2)}) collective-permute-start(bf16[32,2688]{1,0:T(8,128)(2,1)S(1)} %get-tuple-element.173), channel_id=1, source_target_pairs={{0,6},{1,7},{2,4},{3,5},{4,2},{5,3},{6,0},{7,1},{8,14},{9,15},{10,... | collective-permute-start | bytes 516104 | tf_op jit(solution)/shard_map/ppermute | solution.py:41
  102.2 4.9 %collective-permute-done.29.refs_2_ = bf16[32,2688]{1,0:T(8,128)(2,1)S(1)} collective-permute-done((bf16[32,2688]{1,0:T(8,128)(2,1)S(1)}, bf16[32,2688]{1,0:T(8,128)(2,1)S(1)}, u32[]{:S(2)}, u32[]{:S(2)}) %collective-permute-start.29) | collective-permute-done | bytes 172064 | tf_op jit(solution)/shard_map/ppermute | solution.py:41
  (79 shorter events, 40.4 us)
Async XLA Ops:
  0.0 20.3 %collective-permute-start.6 = (bf16[256,5376]{1,0:T(8,128)(2,1)}, bf16[256,5376]{1,0:T(8,128)(2,1)S(1)}, u32[]{:S(2)}, u32[]{:S(2)}) collective-permute-start(bf16[256,5376]{1,0:T(8,128)(2,1)} %refs_4_.3), channel_id=1, source_target_pairs={{0,1},{1,0},{2,3},{3,2},{4,5},{5,4},{6,7},{7,6},{8,9},{9,8},{10,11... | collective-permute-start | bytes 8257544 | tf_op jit(solution)/shard_map/ppermute | solution.py:41
  2.2 5.6 %collective-permute-start = (bf16[32,1792]{1,0:T(8,128)(2,1)S(1)}, bf16[32,1792]{1,0:T(8,128)(2,1)S(1)}, u32[]{:S(2)}, u32[]{:S(2)}) collective-permute-start(bf16[32,1792]{1,0:T(8,128)(2,1)S(1)} %get-tuple-element.90.refs_0_), channel_id=1, source_target_pairs={{0,2},{1,3},{2,0},{3,1},{4,6},{5,7},{6,4},{7,5},{8,10},{9,11},{10,... | collective-permute-start | bytes 344072 | tf_op jit(solution)/shard_map/ppermute | solution.py:41
  3.8 6.4 %collective-permute-start.1 = (bf16[32,1792]{1,0:T(8,128)(2,1)S(1)}, bf16[32,1792]{1,0:T(8,128)(2,1)S(1)}, u32[]{:S(2)}, u32[]{:S(2)}) collective-permute-start(bf16[32,1792]{1,0:T(8,128)(2,1)S(1)} %get-tuple-element.91.refs_1_), channel_id=1, source_target_pairs={{0,6},{1,7},{2,4},{3,5},{4,2},{5,3},{6,0},{7,1},{8,14},{9,15},{10,... | collective-permute-start | bytes 344072 | tf_op jit(solution)/shard_map/ppermute | solution.py:41
  10.9 7.8 %collective-permute-start.3 = (bf16[64,1792]{1,0:T(8,128)(2,1)S(1)}, bf16[64,1792]{1,0:T(8,128)(2,1)S(1)}, u32[]{:S(2)}, u32[]{:S(2)}) collective-permute-start(bf16[64,1792]{1,0:T(8,128)(2,1)S(1)} %get-tuple-element.93.refs_0_), channel_id=1, source_target_pairs={{0,6},{1,7},{2,4},{3,5},{4,2},{5,3},{6,0},{7,1},{8,14},{9,15},{10,... | collective-permute-start | bytes 688136 | tf_op jit(solution)/shard_map/ppermute | solution.py:41
  12.4 6.5 %collective-permute-start.4 = (bf16[64,1792]{1,0:T(8,128)(2,1)S(1)}, bf16[64,1792]{1,0:T(8,128)(2,1)S(1)}, u32[]{:S(2)}, u32[]{:S(2)}) collective-permute-start(bf16[64,1792]{1,0:T(8,128)(2,1)S(1)} %get-tuple-element.94.refs_1_), channel_id=1, source_target_pairs={{0,8},{1,9},{2,10},{3,11},{4,12},{5,13},{6,14},{7,15},{8,0},{9,1},... | collective-permute-start | bytes 688136 | tf_op jit(solution)/shard_map/ppermute | solution.py:41
  14.0 6.3 %collective-permute-start.5 = (bf16[64,1792]{1,0:T(8,128)(2,1)S(1)}, bf16[64,1792]{1,0:T(8,128)(2,1)S(1)}, u32[]{:S(2)}, u32[]{:S(2)}) collective-permute-start(bf16[64,1792]{1,0:T(8,128)(2,1)S(1)} %get-tuple-element.95.refs_2_), channel_id=1, source_target_pairs={{0,2},{1,3},{2,0},{3,1},{4,6},{5,7},{6,4},{7,5},{8,10},{9,11},{10,... | collective-permute-start | bytes 688136 | tf_op jit(solution)/shard_map/ppermute | solution.py:41
  20.5 14.4 %collective-permute-start.10 = (bf16[3,128,1792]{2,1,0:T(8,128)(2,1)S(1)}, bf16[3,128,1792]{2,1,0:T(8,128)(2,1)S(1)}, u32[]{:S(2)}, u32[]{:S(2)}) collective-permute-start(bf16[3,128,1792]{2,1,0:T(8,128)(2,1)S(1)} %get-tuple-element.113), channel_id=1, source_target_pairs={{0,1},{1,0},{2,3},{3,2},{4,5},{5,4},{6,7},{7,6},{8,9},{9,8},{10,11... | collective-permute-start | bytes 4128776 | tf_op jit(solution)/shard_map/ppermute | solution.py:41
  20.6 12.9 %collective-permute-start.7 = (bf16[128,1792]{1,0:T(8,128)(2,1)S(1)}, bf16[128,1792]{1,0:T(8,128)(2,1)S(1)}, u32[]{:S(2)}, u32[]{:S(2)}) collective-permute-start(bf16[128,1792]{1,0:T(8,128)(2,1)S(1)} %get-tuple-element.99.refs_0_), channel_id=1, source_target_pairs={{0,8},{1,9},{2,10},{3,11},{4,12},{5,13},{6,14},{7,15},{8,0},{9,1},... | collective-permute-start | bytes 1376264 | tf_op jit(solution)/shard_map/ppermute | solution.py:41
  21.1 12.6 %collective-permute-start.8 = (bf16[128,1792]{1,0:T(8,128)(2,1)S(1)}, bf16[128,1792]{1,0:T(8,128)(2,1)S(1)}, u32[]{:S(2)}, u32[]{:S(2)}) collective-permute-start(bf16[128,1792]{1,0:T(8,128)(2,1)S(1)} %get-tuple-element.100.refs_1_), channel_id=1, source_target_pairs={{0,2},{1,3},{2,0},{3,1},{4,6},{5,7},{6,4},{7,5},{8,10},{9,11},{10,... | collective-permute-start | bytes 1376264 | tf_op jit(solution)/shard_map/ppermute | solution.py:41
  21.4 13.5 %collective-permute-start.9 = (bf16[128,1792]{1,0:T(8,128)(2,1)S(1)}, bf16[128,1792]{1,0:T(8,128)(2,1)S(1)}, u32[]{:S(2)}, u32[]{:S(2)}) collective-permute-start(bf16[128,1792]{1,0:T(8,128)(2,1)S(1)} %get-tuple-element.101.refs_2_), channel_id=1, source_target_pairs={{0,6},{1,7},{2,4},{3,5},{4,2},{5,3},{6,0},{7,1},{8,14},{9,15},{10,... | collective-permute-start | bytes 1376264 | tf_op jit(solution)/shard_map/ppermute | solution.py:41
  34.9 33.1 %collective-permute-start.20 = (bf16[256,5376]{1,0:T(8,128)(2,1)S(1)}, bf16[256,5376]{1,0:T(8,128)(2,1)S(1)}, u32[]{:S(2)}, u32[]{:S(2)}) collective-permute-start(bf16[256,5376]{1,0:T(8,128)(2,1)S(1)} %collective-permute-done.6.refs_5_), channel_id=1, source_target_pairs={{0,8},{1,137},{2,10},{3,139},{4,12},{5,141},{6,14},{7,143},{8,0},{... | collective-permute-start | bytes 8257544 | tf_op jit(solution)/shard_map/ppermute | solution.py:45
  40.6 8.4 %collective-permute-start.15 = (bf16[512,256]{1,0:T(8,128)(2,1)S(1)}, bf16[512,256]{1,0:T(8,128)(2,1)S(1)}, u32[]{:S(2)}, u32[]{:S(2)}) collective-permute-start(bf16[512,256]{1,0:T(8,128)(2,1)S(1)} %project_kv.1.refs_5_), channel_id=1, source_target_pairs={{0,112},{16,0},{32,16},{48,32},{64,48},{80,64},{96,80},{112,96},{1... | collective-permute-start | bytes 786440 | tf_op jit(solution)/shard_map/ppermute | solution.py:350
  41.7 8.1 %collective-permute-start.14 = (bf16[512,256]{1,0:T(8,128)(2,1)S(1)}, bf16[512,256]{1,0:T(8,128)(2,1)S(1)}, u32[]{:S(2)}, u32[]{:S(2)}) collective-permute-start(bf16[512,256]{1,0:T(8,128)(2,1)S(1)} %project_kv.1.refs_5_), channel_id=1, source_target_pairs={{0,16},{16,32},{32,48},{48,64},{64,80},{80,96},{96,112},{112,0},{1... | collective-permute-start | bytes 786440 | tf_op jit(solution)/shard_map/ppermute | solution.py:350
  49.8 7.2 %collective-permute-start.17 = (bf16[512,256]{1,0:T(8,128)(2,1)S(1)}, bf16[512,256]{1,0:T(8,128)(2,1)S(1)}, u32[]{:S(2)}, u32[]{:S(2)}) collective-permute-start(bf16[512,256]{1,0:T(8,128)(2,1)S(1)} %collective-permute-done.15), channel_id=1, source_target_pairs={{0,112},{16,0},{32,16},{48,32},{64,48},{80,64},{96,80},{112,96},{1... | collective-permute-start | bytes 786440 | tf_op jit(solution)/shard_map/ppermute | solution.py:350
  51.4 7.3 %collective-permute-start.16 = (bf16[512,256]{1,0:T(8,128)(2,1)S(1)}, bf16[512,256]{1,0:T(8,128)(2,1)S(1)}, u32[]{:S(2)}, u32[]{:S(2)}) collective-permute-start(bf16[512,256]{1,0:T(8,128)(2,1)S(1)} %collective-permute-done.14.refs_5_), channel_id=1, source_target_pairs={{0,16},{16,32},{32,48},{48,64},{64,80},{80,96},{96,112},{112,0},{1... | collective-permute-start | bytes 786440 | tf_op jit(solution)/shard_map/ppermute | solution.py:350
  58.7 6.4 %collective-permute-start.18 = (bf16[512,256]{1,0:T(8,128)(2,1)S(1)}, bf16[512,256]{1,0:T(8,128)(2,1)S(1)}, u32[]{:S(2)}, u32[]{:S(2)}) collective-permute-start(bf16[512,256]{1,0:T(8,128)(2,1)S(1)} %collective-permute-done.16.refs_5_), channel_id=1, source_target_pairs={{0,16},{16,32},{32,48},{48,64},{64,80},{80,96},{96,112},{112,0},{1... | collective-permute-start | bytes 786440 | tf_op jit(solution)/shard_map/ppermute | solution.py:350
  58.9 6.7 %collective-permute-start.19 = (bf16[512,256]{1,0:T(8,128)(2,1)S(1)}, bf16[512,256]{1,0:T(8,128)(2,1)S(1)}, u32[]{:S(2)}, u32[]{:S(2)}) collective-permute-start(bf16[512,256]{1,0:T(8,128)(2,1)S(1)} %collective-permute-done.17.refs_6_), channel_id=1, source_target_pairs={{0,112},{16,0},{32,16},{48,32},{64,48},{80,64},{96,80},{112,96},{1... | collective-permute-start | bytes 786440 | tf_op jit(solution)/shard_map/ppermute | solution.py:350
  68.0 18.5 %collective-permute-start.26 = (bf16[256,5376]{1,0:T(8,128)(2,1)S(1)}, bf16[256,5376]{1,0:T(8,128)(2,1)S(1)}, u32[]{:S(2)}, u32[]{:S(2)}) collective-permute-start(bf16[256,5376]{1,0:T(8,128)(2,1)S(1)} %collective-permute-done.20.refs_7_), channel_id=1, source_target_pairs={{0,1},{1,0},{2,3},{3,2},{4,5},{5,4},{6,7},{7,6},{8,9},{9,8},{10,11... | collective-permute-start | bytes 8257544 | tf_op jit(solution)/shard_map/ppermute | solution.py:41
  68.0 7.8 %collective-permute-start.21 = (bf16[512,128]{1,0:T(8,128)(2,1)S(1)}, bf16[512,128]{1,0:T(8,128)(2,1)S(1)}, u32[]{:S(2)}, u32[]{:S(2)}) collective-permute-start(bf16[512,128]{1,0:T(8,128)(2,1)S(1)} %get-tuple-element.149), channel_id=1, source_target_pairs={{48,64},{64,80},{80,96},{49,65},{65,81},{81,97},{50,66},{66,82},{8... | collective-permute-start | bytes 393224 | tf_op jit(solution)/shard_map/ppermute | solution.py:508
  70.9 7.5 %collective-permute-start.22 = (bf16[512,128]{1,0:T(8,128)(2,1)S(1)}, bf16[512,128]{1,0:T(8,128)(2,1)S(1)}, u32[]{:S(2)}, u32[]{:S(2)}) collective-permute-start(bf16[512,128]{1,0:T(8,128)(2,1)S(1)} %get-tuple-element.150), channel_id=1, source_target_pairs={{80,64},{96,80},{112,96},{81,65},{97,81},{113,97},{82,66},{98,82},... | collective-permute-start | bytes 393224 | tf_op jit(solution)/shard_map/ppermute | solution.py:509
  87.6 11.4 %collective-permute-start.28 = (bf16[64,2688]{1,0:T(8,128)(2,1)S(1)}, bf16[64,2688]{1,0:T(8,128)(2,1)S(1)}, u32[]{:S(2)}, u32[]{:S(2)}) collective-permute-start(bf16[64,2688]{1,0:T(8,128)(2,1)S(1)} %get-tuple-element.170), channel_id=1, source_target_pairs={{0,6},{1,7},{2,4},{3,5},{4,2},{5,3},{6,0},{7,1},{8,14},{9,15},{10,... | collective-permute-start | bytes 1032200 | tf_op jit(solution)/shard_map/ppermute | solution.py:41
  90.3 9.9 %collective-permute-start.27 = (bf16[64,2688]{1,0:T(8,128)(2,1)S(1)}, bf16[64,2688]{1,0:T(8,128)(2,1)S(1)}, u32[]{:S(2)}, u32[]{:S(2)}) collective-permute-start(bf16[64,2688]{1,0:T(8,128)(2,1)S(1)} %get-tuple-element.169), channel_id=1, source_target_pairs={{0,2},{1,3},{2,0},{3,1},{4,6},{5,7},{6,4},{7,5},{8,10},{9,11},{10,... | collective-permute-start | bytes 1032200 | tf_op jit(solution)/shard_map/ppermute | solution.py:41
  100.4 6.7 %collective-permute-start.29 = (bf16[32,2688]{1,0:T(8,128)(2,1)S(1)}, bf16[32,2688]{1,0:T(8,128)(2,1)S(1)}, u32[]{:S(2)}, u32[]{:S(2)}) collective-permute-start(bf16[32,2688]{1,0:T(8,128)(2,1)S(1)} %get-tuple-element.173), channel_id=1, source_target_pairs={{0,6},{1,7},{2,4},{3,5},{4,2},{5,3},{6,0},{7,1},{8,14},{9,15},{10,... | collective-permute-start | bytes 516104 | tf_op jit(solution)/shard_map/ppermute | solution.py:41
  102.2 5.4 %collective-permute-start.30 = (bf16[32,2688]{1,0:T(8,128)(2,1)S(1)}, bf16[32,2688]{1,0:T(8,128)(2,1)S(1)}, u32[]{:S(2)}, u32[]{:S(2)}) collective-permute-start(bf16[32,2688]{1,0:T(8,128)(2,1)S(1)} %get-tuple-element.174), channel_id=1, source_target_pairs={{0,2},{1,3},{2,0},{3,1},{4,6},{5,7},{6,4},{7,5},{8,10},{9,11},{10,... | collective-permute-start | bytes 516104 | tf_op jit(solution)/shard_map/ppermute | solution.py:41
  (19 other events, 106.1 us)
